TPU v7x, 32 devices: a whole 2x2x4 slice. The times are simulated.
32 devices in a mesh: grp: 2 (over y), mix: 4 (over z), ffn: 2 (over x), pair: 2 (over core).
Axes of the slice: x: 2, y: 2, z: 4, core: 2. Of those that a mesh axis runs over, the one named last changes fastest.
Arguments:
- query: bfloat16 [512, 8192], P(('grp', 'ffn', 'pair'), 'mix'), parts along dimension 0, may hold values from -100 to 100
- new_key: bfloat16 [512, 8192], P(('grp', 'ffn', 'pair'), 'mix'), parts along dimension 0, may hold values from -6 to 6
- new_value: bfloat16 [512, 8192], P(('grp', 'ffn', 'pair'), 'mix'), parts along dimension 0, may hold values from -6 to 6
- key_cache: bfloat16 [512, 32, 8192], P(('grp', 'ffn', 'pair'), None, 'mix'), parts along dimension 0, may hold values from -6 to 6
- value_cache: bfloat16 [512, 32, 8192], P(('grp', 'ffn', 'pair'), None, 'mix'), parts along dimension 0, may hold values from -6 to 6
- lengths: int32 [512], P(('grp', 'ffn', 'pair')), parts along dimension 0, may hold values from 2 to 32, as said below
- counts: int32 [8], P(('grp', 'ffn', 'pair')), parts along dimension 0, may hold values from 32 to 64, as said below
- residual: bfloat16 [512, 8192], P(('grp', 'ffn', 'pair'), 'mix'), parts along dimension 0, may hold values from -30 to 30
- norm_gain: bfloat16 [8192], P('mix'), may hold values from 0.5 to 1.5
- w_gate: bfloat16 [8192, 21888], P('mix', ('ffn', 'pair')), may hold values from -0.0625 to 0.0625
- w_up: bfloat16 [8192, 21888], P('mix', ('ffn', 'pair')), may hold values from -0.0625 to 0.0625
- w_down: bfloat16 [21888, 8192], P(('ffn', 'pair'), 'mix'), may hold values from -0.0390625 to 0.0390625
Outputs:
- block_out: bfloat16 [512, 8192], P(('grp', 'ffn', 'pair'), 'mix'), parts along dimension 0
There are 2 independent parts, one for each index of `grp`. A program takes and returns all parts, laid end to end along the dimension named above; an argument that names none is the same for every part. Nothing has to cross between parts.
Inputs may be any that keep to these rules, and one draw needn't show every extreme that they name: `counts`: candidate slots beyond a block's count are empty; some block is full. `lengths`: some candidate has 32 cached positions.
All inputs are finite; a program needn't handle non-finite values.
Results may differ from a plain program's by a relative error of at most 0.014.
Values may be sent and summed in bfloat16 or wider, within the bound.
No kernel may reach another device: no remote copies, remote signals or barrier semaphores. Data moves between devices by JAX's collectives and lax.ppermute only.
A program may use at most 192 MiB of HBM per device.

v0:
```python
import jax
import jax.numpy as jnp
from jax import lax
from jax.sharding import PartitionSpec as P

D = 8192
HD = 128


eps = 1e-05


def attend(query, new_key, new_value, key_cache, value_cache, lengths):
    rows = query.shape[0]
    heads = query.shape[1] // HD
    cache_len = key_cache.shape[1]
    scale = 1.0 / HD**0.5
    q_heads = query.reshape(rows, heads, HD)
    k_all = key_cache.reshape(rows, cache_len, heads, HD)
    v_all = value_cache.reshape(rows, cache_len, heads, HD)
    scores = jnp.einsum("chd,cphd->chp", q_heads, k_all, preferred_element_type=jnp.float32) * scale
    own = (
        jnp.einsum(
            "chd,chd->ch",
            q_heads,
            new_key.reshape(rows, heads, HD),
            preferred_element_type=jnp.float32,
        )
        * scale
    )
    valid = jnp.arange(cache_len, dtype=jnp.int32)[None, :] < lengths[:, None]
    scores = jnp.where(valid[:, None, :], scores, -jnp.inf)
    top = jnp.maximum(jnp.max(scores, axis=-1), own)
    weights = jnp.exp(scores - top[..., None])
    own_w = jnp.exp(own - top)
    total = jnp.sum(weights, axis=-1) + own_w
    probs = (weights / total[..., None]).astype(jnp.bfloat16)
    own_p = (own_w / total).astype(jnp.bfloat16)
    mixed = jnp.einsum("chp,cphd->chd", probs, v_all, preferred_element_type=jnp.float32)
    own_v = new_value.reshape(rows, heads, HD).astype(jnp.float32)
    mixed = mixed + own_p.astype(jnp.float32)[..., None] * own_v
    return mixed.reshape(rows, heads * HD)


def per_device(
    query,
    new_key,
    new_value,
    key_cache,
    value_cache,
    lengths,
    counts,
    residual,
    norm_gain,
    w_gate,
    w_up,
    w_down,
):
    mixed = attend(query, new_key, new_value, key_cache, value_cache, lengths)
    x = residual.astype(jnp.float32) + mixed
    squares = lax.psum(jnp.sum(x * x, axis=1), "mix")
    ms = squares / D
    xn = (x * lax.rsqrt(ms + eps)[:, None] * norm_gain.astype(jnp.float32)).astype(jnp.bfloat16)
    gathered = lax.all_gather(xn, ("ffn", "pair"), axis=0, tiled=True)
    hidden_width = w_gate.shape[1]
    part_gate = jnp.dot(gathered, w_gate, preferred_element_type=jnp.float32).astype(jnp.bfloat16)
    part_up = jnp.dot(gathered, w_up, preferred_element_type=jnp.float32).astype(jnp.bfloat16)
    summed = lax.psum(jnp.concatenate([part_gate, part_up], axis=1), "mix").astype(jnp.float32)
    hidden = (jax.nn.silu(summed[:, :hidden_width]) * summed[:, hidden_width:]).astype(jnp.bfloat16)
    partial_value = jnp.dot(hidden, w_down, preferred_element_type=jnp.float32)
    mlp = lax.psum_scatter(
        partial_value.astype(jnp.bfloat16), ("ffn", "pair"), scatter_dimension=0, tiled=True
    ).astype(jnp.float32)
    slots = jnp.arange(x.shape[0], dtype=jnp.int32)
    live = slots < counts[0]
    return jnp.where(live[:, None], x + mlp, jnp.zeros_like(x)).astype(jnp.bfloat16)


def solution(mesh):
    placed = (
        P(("grp", "ffn", "pair"), "mix"),
        P(("grp", "ffn", "pair"), "mix"),
        P(("grp", "ffn", "pair"), "mix"),
        P(("grp", "ffn", "pair"), None, "mix"),
        P(("grp", "ffn", "pair"), None, "mix"),
        P(("grp", "ffn", "pair")),
        P(("grp", "ffn", "pair")),
        P(("grp", "ffn", "pair"), "mix"),
        P("mix"),
        P("mix", ("ffn", "pair")),
        P("mix", ("ffn", "pair")),
        P(("ffn", "pair"), "mix"),
    )
    return jax.shard_map(
        per_device,
        mesh=mesh,
        in_specs=placed,
        out_specs=P(("grp", "ffn", "pair"), "mix"),
        check_vma=False,
    )
```

profile of v0, /device:TPU:0, one launch (start us, length us, event | category | flops | bytes accessed | tf_op | source)
XLA Modules:
  0.0 343.2 jit_solution(14524019703992737572)
XLA Ops:
  6.5 0.0 copy-start.1
  6.5 0.0 copy-start.5
  6.5 0.0 copy-start.3
  6.5 0.0 copy-start.2
  6.5 0.0 all-gather.2.cloned.1.call-start
  6.6 1.4 reshape.57
  8.0 7.8 %fusion.3 = f32[64,16,1,32]{3,2,1,0:T(1,128)S(1)} fusion(bf16[64,16,128,1]{2,3,1,0:T(2,128)(2,1)S(1)} %reshape.57, bf16[64,32,2048]{2,1,0:T(8,128)(2,1)} %param.15), kind=kOutput, calls=%fused_computation.3 | convolution fusion | flops 8388608 | bytes 8781824 | tf_op jit(solution)/shard_map/chd,cphd->chp/dot_general | solution.py:21
  15.8 0.3 copy.16
  16.1 0.0 copy-done.5
  16.1 0.0 copy-start
  16.2 0.0 copy-done.1
  16.2 0.0 copy-done.3
  16.2 0.0 copy-start.4
  16.3 0.2 fusion.14
  16.5 0.1 copy.20
  16.6 0.1 fusion.17
  16.6 0.1 fusion.16
  16.8 0.1 fusion.18
  16.8 0.5 copy.21
  17.4 0.1 copy.13
  17.4 0.0 copy-done.2
  17.5 0.1 copy.29
  17.6 5.7 %fusion = f32[64,16,1,128]{3,2,1,0:T(1,128)S(1)} fusion(bf16[64,16,32,1]{2,3,1,0:T(2,128)(2,1)S(1)} %copy.21, bf16[64,32,2048]{2,1,0:T(8,128)(2,1)} %param.16), kind=kOutput, calls=%fused_computation | convolution fusion | flops 8388608 | bytes 8978432 | tf_op jit(solution)/shard_map/chp,cphd->chd/dot_general | solution.py:39
  23.3 0.2 fusion.13
  23.5 0.0 copy-done
  23.5 0.3 multiply_reduce_fusion
  23.8 13.5 %psum.14 = f32[64]{0:T(128)S(1)} all-reduce(f32[64]{0:T(128)S(1)} %multiply_reduce_fusion), channel_id=1, replica_groups=mesh['grp'=2,'mix'=4,'ffn'=2,'pair'=2] {'mix'}, use_global_device_ids=true, to_apply=%region_3.4 | all-reduce | flops 64 | bytes 512 | tf_op jit(solution)/shard_map/psum | solution.py:61
  37.2 0.0 copy-done.4
  37.2 0.9 multiply_convert_fusion
  38.1 0.0 all-gather.2.cloned.1.call-update
  38.2 0.2 all-reduce.2.cloned.1.call-start
  38.4 14.9 %all-gather.2.cloned.1.call-done = bf16[256,2048]{1,0:T(8,128)(2,1)} async-done(((bf16[64,2048]{1,0:T(8,128)(2,1)}), bf16[256,2048]{1,0:T(8,128)(2,1)}) %all-gather.2.cloned.1.call-update) | async-done | bytes 1048592 | tf_op jit(solution)/shard_map/all_gather | solution.py:64
  53.3 0.0 copy-start.6
  53.3 13.8 %convolution_convert_fusion = bf16[256,5472]{0,1:T(8,128)(2,1)S(1)} fusion(bf16[256,2048]{1,0:T(8,128)(2,1)} %all-gather.2.cloned.1.call-done, bf16[2048,5472]{0,1:T(8,128)(2,1)} %param.22), kind=kOutput, calls=%fused_computation.6 | convolution fusion | flops 5739208704 | bytes 26263552 | tf_op jit(solution)/shard_map/dot_general | solution.py:67
  67.0 0.0 copy-done.6
  67.1 10.8 %convolution_convert_fusion.1 = bf16[256,5472]{0,1:T(8,128)(2,1)S(1)} fusion(bf16[256,2048]{1,0:T(8,128)(2,1)S(1)} %copy-done.6, bf16[2048,5472]{0,1:T(8,128)(2,1)} %param.21), kind=kOutput, calls=%fused_computation.7 | convolution fusion | flops 5739208704 | bytes 26263552 | tf_op jit(solution)/shard_map/dot_general | solution.py:66
  77.8 16.8 %pad_maximum_fusion = bf16[256,10944]{0,1:T(8,128)(2,1)} fusion(bf16[256,5472]{0,1:T(8,128)(2,1)S(1)} %convolution_convert_fusion, bf16[256,5472]{0,1:T(8,128)(2,1)S(1)} %convolution_convert_fusion.1), kind=kLoop, calls=%fused_computation.10 | loop fusion | flops 11206656 | bytes 11206656 | tf_op jit(solution)/shard_map/concatenate | solution.py:68
  94.6 0.0 all-reduce.2.cloned.1.call-update
  94.7 0.3 reduce-scatter.2.cloned.1.call-start
  94.9 200.5 %all-reduce.2.cloned.1.call-done = bf16[256,10944]{0,1:T(8,128)(2,1)} async-done(((bf16[256,10944]{0,1:T(8,128)(2,1)}), bf16[256,10944]{0,1:T(8,128)(2,1)}) %all-reduce.2.cloned.1.call-update) | async-done | bytes 5603344 | tf_op jit(solution)/shard_map/psum | solution.py:68
  295.4 3.1 convert_element_type.55
  298.5 12.2 %fusion.10 = bf16[256,2048]{1,0:T(8,128)(2,1)} fusion(bf16[5472,2048]{1,0:T(8,128)(2,1)} %param.23, f32[256,10944]{0,1:T(8,128)S(1)} %convert_element_type.55), kind=kOutput, calls=%fused_computation.13 | convolution fusion | flops 5746737152 | bytes 34668544 | tf_op jit(solution)/shard_map/dot_general | solution.py:70
  310.7 0.0 reduce-scatter.2.cloned.1.call-update
  311.4 23.4 %reduce-scatter.2.cloned.1.call-done = bf16[64,2048]{1,0:T(8,128)(2,1)} async-done(((bf16[256,2048]{1,0:T(8,128)(2,1)}), bf16[64,2048]{1,0:T(8,128)(2,1)}) %reduce-scatter.2.cloned.1.call-update) | async-done | bytes 262160 | tf_op jit(solution)/shard_map/reduce_scatter | solution.py:71
  334.8 1.9 select_convert_fusion
  (9 shorter events, 0.2 us)
Async XLA Ops:
  6.5 9.6 %copy-start.1 = (bf16[64,2048]{1,0:T(8,128)(2,1)S(1)}, bf16[64,2048]{1,0:T(8,128)(2,1)}, u32[]{:S(2)}) copy-start(bf16[64,2048]{1,0:T(8,128)(2,1)} %param.12) | copy-start | bytes 786436
  6.5 9.6 %copy-start.5 = (s32[64]{0:T(128)S(1)}, s32[64]{0:T(128)}, u32[]{:S(2)}) copy-start(s32[64]{0:T(128)} %param.17) | copy-start | bytes 772
  6.5 9.7 %copy-start.3 = (bf16[64,2048]{1,0:T(8,128)(2,1)S(1)}, bf16[64,2048]{1,0:T(8,128)(2,1)}, u32[]{:S(2)}) copy-start(bf16[64,2048]{1,0:T(8,128)(2,1)} %param.13) | copy-start | bytes 786436
  6.5 10.9 %copy-start.2 = (bf16[64,2048]{1,0:T(8,128)(2,1)S(1)}, bf16[64,2048]{1,0:T(8,128)(2,1)}, u32[]{:S(2)}) copy-start(bf16[64,2048]{1,0:T(8,128)(2,1)} %param.14) | copy-start | bytes 786436
  6.5 46.7 %all-gather.2.cloned.1.call-start = ((), (), s32[]{:S(2)}) async-start(), calls=%async_computation.1 | async-start | bytes 1310720 | tf_op jit(solution)/shard_map/all_gather | solution.py:64
  16.1 7.4 %copy-start = (bf16[64,2048]{1,0:T(8,128)(2,1)S(1)}, bf16[64,2048]{1,0:T(8,128)(2,1)}, u32[]{:S(2)}) copy-start(bf16[64,2048]{1,0:T(8,128)(2,1)} %param.19) | copy-start | bytes 786436
  16.2 21.0 %copy-start.4 = (bf16[2048]{0:T(1024)(128)(2,1)S(1)}, bf16[2048]{0:T(1024)(128)(2,1)}, u32[]{:S(2)}) copy-start(bf16[2048]{0:T(1024)(128)(2,1)} %param.20) | copy-start | bytes 12292
  38.2 257.2 %all-reduce.2.cloned.1.call-start = ((), (), s32[]{:S(2)}) async-start(), calls=%async_computation.2 | async-start | bytes 11206656 | tf_op jit(solution)/shard_map/psum | solution.py:68
  53.3 13.8 %copy-start.6 = (bf16[256,2048]{1,0:T(8,128)(2,1)S(1)}, bf16[256,2048]{1,0:T(8,128)(2,1)}, u32[]{:S(2)}) copy-start(bf16[256,2048]{1,0:T(8,128)(2,1)} %all-gather.2.cloned.1.call-done) | copy-start | bytes 3145732
  94.7 240.1 %reduce-scatter.2.cloned.1.call-start = ((), (), s32[]{:S(2)}) async-start(), calls=%async_computation.3 | async-start | bytes 1310720 | tf_op jit(solution)/shard_map/reduce_scatter | solution.py:71
Sparse Core Ops, SparseCore 0:
  38.3 14.9 all-gather.1
  94.8 200.5 all-reduce.1
  310.9 23.8 reduce-scatter.1
where the time goes:
time: 343 us
  waiting for transfers between devices  239 us (70%)
  matrix products  50.2 us (15%)
  other arithmetic  23.7 us (7%)
  between operations  14 us (4%)
  blocking collectives  13.5 us (4%)
    psum x1, waiting for transfers between devices, per_device(): lax.psum(jnp.concatenate([part_gate, part_up], axis=1), 'mix')  200 us
    reduce_scatter x1, waiting for transfers between devices, per_device(): lax.psum_scatter(partial_value.astype(jnp.bfloat16), ('ffn', 'pair'), sca...  23.4 us
    concatenate x1, other arithmetic, per_device(): jnp.concatenate([part_gate, part_up], axis=1)  16.8 us
    all_gather x1, waiting for transfers between devices, per_device(): gathered = lax.all_gather(xn, ('ffn', 'pair'), axis=0, tiled=True)  14.9 us
    dot_general x1, matrix products, per_device(): jnp.dot(gathered, w_up, preferred_element_type=jnp.float32)  13.8 us
    psum x1, blocking collectives, per_device(): squares = lax.psum(jnp.sum(x * x, axis=1), 'mix')  13.5 us
    dot_general x1, matrix products, per_device(): partial_value = jnp.dot(hidden, w_down, preferred_element_type=jnp.float32)  12.2 us
    dot_general x1, matrix products, per_device(): jnp.dot(gathered, w_gate, preferred_element_type=jnp.float32)  10.8 us
  transfers between devices with their start and end apart: 3, of which 3 were waited for; matrix products, arithmetic and copies ran while one was open for 0% of the time, Pallas kernels for 0%

commit v1 on v0

--- a/solution.py
+++ b/solution.py
@@ -1,6 +1,10 @@
+import functools
+
 import jax
 import jax.numpy as jnp
 from jax import lax
+from jax.experimental import pallas as pl
+from jax.experimental.pallas import tpu as pltpu
 from jax.sharding import PartitionSpec as P
 
 D = 8192
@@ -42,7 +46,320 @@
     return mixed.reshape(rows, heads * HD)
 
 
+WIDTH = 512
+OUTWARD = ((0, 1), (1, 0), (2, 3), (3, 2))
+ACROSS = ((0, 2), (2, 0), (1, 3), (3, 1))
+MIDDLE = ((0, 1), (1, 0), (2, 4), (4, 2), (3, 5), (5, 3), (6, 7), (7, 6))
+SWAP = ((0, 1), (1, 0))
+f32 = jnp.float32
+bf16 = jnp.bfloat16
+ANY = pl.BlockSpec(memory_space=pl.ANY)
+SMEM = pl.BlockSpec(memory_space=pltpu.SMEM)
+VMEM = pl.BlockSpec(memory_space=pltpu.VMEM)
+
+
+def outward(a):
+    return lax.ppermute(a, "mix", OUTWARD)
+
+
+def middle(a):
+    return lax.ppermute(a, ("mix", "pair"), MIDDLE)
+
+
+def swap(a, axis):
+    return lax.ppermute(a, axis, SWAP)
+
+
+def partial_products(k, rows, gate_rows, up_rows, after):
+    count, depth = rows.shape
+    units = gate_rows.shape[0]
+    half = count // 2
+    valid = min(WIDTH, units - k * WIDTH)
+    step = 256
+    steps = WIDTH // step
+
+    def kernel(rows_ref, gate_ref, up_ref, *rest):
+        out_ref, in_ref = rest[-2:]
+        i = pl.program_id(0)
+        for weight, offset in ((gate_ref, 0), (up_ref, WIDTH)):
+            part = lax.dot_general(rows_ref[...], weight[...], (((1,), (1,)), ((), ())), preferred_element_type=f32)
+            if valid < WIDTH:
+                unit = lax.broadcasted_iota(jnp.int32, part.shape, 1) + i * step
+                part = jnp.where(unit < valid, part, 0.0)
+            part = part.astype(bf16)
+            at = pl.ds(pl.multiple_of(offset + i * step, step), step)
+            out_ref[:, at] = part[:half]
+            in_ref[:, at] = part[half:]
+
+    shape = jax.ShapeDtypeStruct((half, 2 * WIDTH), bf16)
+    first = k * steps
+    return pl.pallas_call(
+        kernel,
+        grid=(steps,),
+        in_specs=[
+            pl.BlockSpec((count, depth), lambda i: (0, 0)),
+            pl.BlockSpec((step, depth), lambda i: (first + i, 0)),
+            pl.BlockSpec((step, depth), lambda i: (first + i, 0)),
+        ]
+        + [ANY] * len(after),
+        out_specs=[pl.BlockSpec((half, 2 * WIDTH), lambda i: (0, 0))] * 2,
+        out_shape=[shape, shape],
+        compiler_params=pltpu.CompilerParams(vmem_limit_bytes=24 << 20),
+        cost_estimate=pl.CostEstimate(
+            flops=4 * count * depth * WIDTH, bytes_accessed=4 * depth * WIDTH + 6 * count * WIDTH, transcendentals=0
+        ),
+        name="partial_products",
+    )(rows, gate_rows, up_rows, *after)
+
+
+def hop(outer, inv_in, t, count, got_e, got_m, part_out, part_in, after):
+    half = inv_in.shape[0]
+
+    def inside(k):
+        return 0 <= k < count
+
+    def sums_e(s):
+        return inside(s) or inside(s - 2)
+
+    def hid_e(s):
+        return inside(s - 3) or inside(s - 5)
+
+    two = 2 * WIDTH
+    names = ["outer", "inv"]
+    operands = [outer, inv_in]
+    specs = [SMEM, VMEM]
+
+    def add(name, value):
+        names.append(name)
+        operands.append(value)
+        specs.append(VMEM)
+
+    need_sum_in = inside(t - 2)
+    if need_sum_in or hid_e(t) or inside(t):
+        add("got_e", got_e)
+    if got_m is not None and (inside(t - 1) or inside(t - 4)):
+        add("got_m", got_m)
+    if inside(t + 1):
+        add("next_out", part_out[t + 1])
+    if inside(t):
+        add("out", part_out[t])
+    if inside(t - 1):
+        add("in1", part_in[t - 1])
+    if inside(t - 2):
+        add("in2", part_in[t - 2])
+    operands += after
+    specs += [ANY] * len(after)
+    nxt = t + 1
+    hid_at_e = two if sums_e(nxt) else 0
+    hid_at_got_e = two if sums_e(t) else 0
+    width_e = hid_at_e + (WIDTH if hid_e(nxt) else 0)
+    hid_at_m = two if inside(t) else 0
+    hid_at_got_m = two if inside(t - 1) else 0
+    width_m = hid_at_m + (WIDTH if inside(t - 3) else 0)
+    widths = [w for w in (width_e, width_m) if w]
+
+    def kernel(*refs):
+        r = dict(zip(names, refs))
+        outs = list(refs[len(operands) :])
+        to_e = outs.pop(0) if width_e else None
+        to_m = outs.pop(0) if width_m else None
+
+        @pl.when(r["outer"][0] != 0)
+        def _():
+            if inside(t + 1):
+                to_e[:, :two] = r["next_out"][...]
+            if inside(t - 2):
+                inv = r["inv"][...]
+                gate = (r["in2"][:, :WIDTH].astype(f32) + r["got_e"][:, :WIDTH].astype(f32)) * inv
+                up = (r["in2"][:, WIDTH:].astype(f32) + r["got_e"][:, WIDTH:two].astype(f32)) * inv
+                to_e[:, hid_at_e : hid_at_e + WIDTH] = (gate / (1.0 + jnp.exp(-gate)) * up).astype(bf16)
+
+        @pl.when(r["outer"][0] == 0)
+        def _():
+            if inside(t - 1):
+                to_e[:, :two] = (r["in1"][...].astype(f32) + r["got_m"][:, :two].astype(f32)).astype(bf16)
+            if inside(t - 4):
+                to_e[:, hid_at_e : hid_at_e + WIDTH] = r["got_m"][:, hid_at_got_m : hid_at_got_m + WIDTH]
+            if inside(t):
+                to_m[:, :two] = (r["out"][...].astype(f32) + r["got_e"][:, :two].astype(f32)).astype(bf16)
+            if inside(t - 3):
+                to_m[:, hid_at_m : hid_at_m + WIDTH] = r["got_e"][:, hid_at_got_e : hid_at_got_e + WIDTH]
+
+    outs = pl.pallas_call(
+        kernel,
+        in_specs=specs,
+        out_specs=[VMEM] * len(widths),
+        out_shape=[jax.ShapeDtypeStruct((half, w), bf16) for w in widths],
+        compiler_params=pltpu.CompilerParams(vmem_limit_bytes=24 << 20),
+        cost_estimate=pl.CostEstimate(flops=8 * half * two, bytes_accessed=10 * half * two, transcendentals=half * WIDTH),
+        name="hop",
+    )(*operands)
+    outs = list(outs)
+    to_e = (outs.pop(0), hid_at_e) if width_e else None
+    to_m = (outs.pop(0), hid_at_m) if width_m else None
+    return to_e, to_m
+
+
+def down_product(outer, total, first, chunks, w_down, final):
+    units, columns = w_down.shape
+    half = chunks[0][0][0].shape[0]
+    n = len(chunks)
+    valid = min(n * WIDTH, units - first * WIDTH)
+    step = 512
+
+    def kernel(outer_ref, *refs):
+        hids = refs[: 4 * n]
+        w_ref = refs[4 * n]
+        total_ref = refs[4 * n + 1] if total is not None else None
+        out_ref, hid = refs[-2:]
+
+        @pl.when(pl.program_id(0) == 0)
+        def _():
+            for c in range(n):
+                sent, got, from_m, late = hids[4 * c : 4 * c + 4]
+                at = pl.ds(c * WIDTH, WIDTH)
+
+                @pl.when(outer_ref[0] != 0)
+                def _():
+                    hid[:half, at] = late[...]
+                    hid[half:, at] = sent[...]
+
+                @pl.when(outer_ref[0] == 0)
+                def _():
+                    hid[:half, at] = from_m[...]
+                    hid[half:, at] = got[...]
+
+        weight = w_ref[...]
+        if valid < n * WIDTH:
+            unit = lax.broadcasted_iota(jnp.int32, weight.shape, 0)
+            weight = jnp.where(unit < valid, weight.astype(f32), 0.0).astype(bf16)
+        term = jnp.dot(hid[...], weight, preferred_element_type=f32)
+        if total_ref is not None:
+            term = term + total_ref[...]
+        out_ref[...] = term.astype(out_ref.dtype)
+
+    operands, specs = [outer], [SMEM]
+    for chunk in chunks:
+        for buffer, offset in chunk:
+            operands.append(buffer)
+            specs.append(pl.BlockSpec((half, WIDTH), functools.partial(lambda at, i: (0, at), offset // WIDTH)))
+    operands.append(w_down)
+    block = first // n
+    specs.append(pl.BlockSpec((n * WIDTH, step), lambda i: (block, i)))
+    if total is not None:
+        operands.append(total)
+        specs.append(pl.BlockSpec((2 * half, step), lambda i: (0, i)))
+    return pl.pallas_call(
+        kernel,
+        grid=(columns // step,),
+        in_specs=specs,
+        out_specs=pl.BlockSpec((2 * half, step), lambda i: (0, i)),
+        out_shape=jax.ShapeDtypeStruct((2 * half, columns), bf16 if final else f32),
+        scratch_shapes=[pltpu.VMEM((2 * half, n * WIDTH), bf16)],
+        compiler_params=pltpu.CompilerParams(vmem_limit_bytes=24 << 20),
+        cost_estimate=pl.CostEstimate(
+            flops=4 * half * n * WIDTH * columns,
+            bytes_accessed=2 * n * WIDTH * columns + 16 * half * columns,
+            transcendentals=0,
+        ),
+        name="down_product",
+    )(*operands)
+
+
+def mlp_line(scaled, rows_rms, w_gate, w_up, w_down):
+    place = lax.axis_index("mix")
+    left = place < 2
+    outer = ((place == 0) | (place == 3)).astype(jnp.int32).reshape(1)
+
+    across = swap(scaled, "ffn")
+    beside = swap(scaled, "pair")
+    diagonal = swap(across, "pair")
+    here = jnp.concatenate([scaled, across])
+    there = jnp.concatenate([beside, diagonal])
+    rows = jnp.concatenate([jnp.where(left, here, there), jnp.where(left, there, here)])
+    half = here.shape[0]
+
+    inv = jnp.concatenate([rows_rms, swap(rows_rms, "ffn")])
+    inv_in = jnp.where(left, swap(inv, "pair"), inv)
+
+    gate_rows = pltpu.with_memory_space_constraint(w_gate.T, pltpu.HBM)
+    up_rows = pltpu.with_memory_space_constraint(w_up.T, pltpu.HBM)
+    w_down = pltpu.with_memory_space_constraint(w_down, pltpu.HBM)
+    chunks = -(-gate_rows.shape[0] // WIDTH)
+    counts = (-(-chunks // 2), chunks // 2)
+    part_out, part_in = ({}, {}), ({}, {})
+    sent, got = {}, {}
+
+    def products(k, after):
+        if k < chunks:
+            a, b = partial_products(k, rows, gate_rows, up_rows, after)
+            part_out[k % 2][k // 2], part_in[k % 2][k // 2] = a, b
+            return [a]
+        return after
+
+    def send(s, t, to_e, to_m):
+        sent["e", s, t], sent["m", s, t] = to_e, to_m
+        got["e", s, t] = (outward(to_e[0]), to_e[1]) if to_e else None
+        got["m", s, t] = (middle(to_m[0]), to_m[1]) if to_m else None
+
+    def hidden_of(k):
+        s, j = k % 2, k // 2
+        return [sent["e", s, j + 3], got["e", s, j + 3], got["m", s, j + 4], got["e", s, j + 5]]
+
+    after = products(0, [])
+    send(0, 0, (part_out[0][0], 2 * WIDTH), None)
+    after = products(1, after)
+    send(1, 0, (part_out[1][0], 2 * WIDTH), None)
+    after = products(2, after)
+    total = None
+    for t in range(counts[0] + 5):
+        for s in (0, 1):
+            count = counts[s]
+            if t < count + 4:
+                got_e, got_m = got["e", s, t], got["m", s, t]
+                to_e, to_m = hop(
+                    outer,
+                    inv_in,
+                    t,
+                    count,
+                    got_e and got_e[0],
+                    got_m and got_m[0],
+                    part_out[s],
+                    part_in[s],
+                    after,
+                )
+                send(s, t + 1, to_e, to_m)
+                after = [(to_e or to_m)[0]]
+            after = products(2 * t + s + 3, after)
+            first = 2 * (t - 5)
+            if first >= 0 and ((s == 1 and first + 1 < chunks) or (s == 0 and first + 1 == chunks)):
+                pair = [hidden_of(k) for k in range(first, min(first + 2, chunks))]
+                total = down_product(outer, total, first, pair, w_down, first + 2 >= chunks)
+                after = [total]
+    far, near = total[:half], total[half:]
+    for_here = jnp.where(left, far, near)
+    for_there = jnp.where(left, near, far)
+    chip = for_here.astype(f32) + swap(for_there, "pair").astype(f32)
+    block = half // 2
+    return chip[:block] + swap(chip[block:].astype(bf16), "ffn").astype(f32)
+
+
+def mlp_sums(normed, w_gate, w_up, w_down):
+    gathered = lax.all_gather(normed, ("ffn", "pair"), axis=0, tiled=True)
+    parts = []
+    for weight in (w_gate, w_up):
+        part = jnp.dot(gathered, weight, preferred_element_type=jnp.float32).astype(jnp.bfloat16)
+        parts.append(lax.psum_scatter(part, "mix", scatter_dimension=0, tiled=True).astype(jnp.float32))
+    hidden = (jax.nn.silu(parts[0]) * parts[1]).astype(jnp.bfloat16)
+    hidden = lax.all_gather(hidden, "mix", axis=0, tiled=True)
+    partial_value = jnp.dot(hidden, w_down, preferred_element_type=jnp.float32)
+    return lax.psum_scatter(
+        partial_value.astype(jnp.bfloat16), ("ffn", "pair"), scatter_dimension=0, tiled=True
+    ).astype(jnp.float32)
+
+
 def per_device(
+    on_line,
     query,
     new_key,
     new_value,
@@ -58,25 +375,24 @@
 ):
     mixed = attend(query, new_key, new_value, key_cache, value_cache, lengths)
     x = residual.astype(jnp.float32) + mixed
-    squares = lax.psum(jnp.sum(x * x, axis=1), "mix")
-    ms = squares / D
-    xn = (x * lax.rsqrt(ms + eps)[:, None] * norm_gain.astype(jnp.float32)).astype(jnp.bfloat16)
-    gathered = lax.all_gather(xn, ("ffn", "pair"), axis=0, tiled=True)
-    hidden_width = w_gate.shape[1]
-    part_gate = jnp.dot(gathered, w_gate, preferred_element_type=jnp.float32).astype(jnp.bfloat16)
-    part_up = jnp.dot(gathered, w_up, preferred_element_type=jnp.float32).astype(jnp.bfloat16)
-    summed = lax.psum(jnp.concatenate([part_gate, part_up], axis=1), "mix").astype(jnp.float32)
-    hidden = (jax.nn.silu(summed[:, :hidden_width]) * summed[:, hidden_width:]).astype(jnp.bfloat16)
-    partial_value = jnp.dot(hidden, w_down, preferred_element_type=jnp.float32)
-    mlp = lax.psum_scatter(
-        partial_value.astype(jnp.bfloat16), ("ffn", "pair"), scatter_dimension=0, tiled=True
-    ).astype(jnp.float32)
+    gain = norm_gain.astype(jnp.float32)
+    squares = jnp.sum(x * x, axis=1, keepdims=True)
+    if on_line:
+        squares = squares + outward(squares)
+        squares = squares + lax.ppermute(squares, "mix", ACROSS)
+        inv = lax.rsqrt(squares / D + eps)
+        mlp = mlp_line((x * gain).astype(jnp.bfloat16), inv, w_gate, w_up, w_down)
+    else:
+        inv = lax.rsqrt(lax.psum(squares, "mix") / D + eps)
+        mlp = mlp_sums((x * inv * gain).astype(jnp.bfloat16), w_gate, w_up, w_down)
     slots = jnp.arange(x.shape[0], dtype=jnp.int32)
     live = slots < counts[0]
     return jnp.where(live[:, None], x + mlp, jnp.zeros_like(x)).astype(jnp.bfloat16)
 
 
 def solution(mesh):
+    sizes = mesh.shape
+    on_line = sizes["mix"] == 4 and sizes["ffn"] == 2 and sizes["pair"] == 2
     placed = (
         P(("grp", "ffn", "pair"), "mix"),
         P(("grp", "ffn", "pair"), "mix"),
@@ -92,7 +408,7 @@
         P(("ffn", "pair"), "mix"),
     )
     return jax.shard_map(
-        per_device,
+        functools.partial(per_device, on_line),
         mesh=mesh,
         in_specs=placed,
         out_specs=P(("grp", "ffn", "pair"), "mix"),

time: 343 us -> 199 us (0.58)
  waiting for transfers between devices: 239 us -> 45.7 us
  starting transfers between devices: 0.52 us -> 67.5 us
  Pallas kernels: 0 us -> 59.6 us
  matrix products: 50.2 us -> 13.4 us
  other arithmetic: 23.7 us -> 4.95 us
  blocking collectives: 13.5 us -> 0 us
  between operations: 14 us -> 1.4 us
    psum x1 -> x0, waiting for transfers between devices: 200 us -> none  [per_device(): lax.psum(jnp.concatenate([part_gate, part_up], axis=1), 'mix')]
    ppermute x0 -> x47, starting transfers between devices: none -> 67.5 us  [the longest x22 59.1 us: outward(): return lax.ppermute(a, 'mix', OUTWARD)]
    pallas_call x0 -> x36, Pallas kernels: none -> 59.6 us  [the longest x11 33.7 us: partial_products(): pl.pallas_call(kernel, grid=(steps,), in_specs=[pl.BlockSpec((count, dept...]
    ppermute x0 -> x47, waiting for transfers between devices: none -> 45.7 us  [the longest x22 30.5 us: outward(): return lax.ppermute(a, 'mix', OUTWARD)]
    dot_general x3 -> x0, matrix products: 36.8 us -> none  [the longest x1 13.8 us: per_device(): jnp.dot(gathered, w_up, preferred_element_type=jnp.float32)]
    reduce_scatter x1 -> x0, waiting for transfers between devices: 23.4 us -> none  [per_device(): lax.psum_scatter(partial_value.astype(jnp.bfloat16), ('ffn', 'pair'), sca...]
    concatenate x1 -> x2, other arithmetic: 16.8 us -> 0.18 us  [the longest x1 0.1 us: mlp_line(): jnp.concatenate([jnp.where(left, here, there), jnp.where(left, there, her...]
    all_gather x1 -> x0, waiting for transfers between devices: 14.9 us -> none  [per_device(): gathered = lax.all_gather(xn, ('ffn', 'pair'), axis=0, tiled=True)]
  transfers between devices with their start and end apart: 3 -> 47, of which waited for: 3 -> 17; matrix products, arithmetic and copies ran while one was open for 0% -> 0% of each run, Pallas kernels for 0% -> 28%
where the time goes in v1:
time: 199 us; the launch traced here: 198 us
  starting transfers between devices  67.5 us (34%)
  Pallas kernels  59.6 us (30%)
  waiting for transfers between devices  45.7 us (23%)
  matrix products  13.4 us (7%)
  local copies, waits for them, and re-layouts  5.39 us (3%)
  other arithmetic  4.95 us (2%)
    ppermute x22, starting transfers between devices, outward(): return lax.ppermute(a, 'mix', OUTWARD)  59.1 us
    pallas_call x11, Pallas kernels, partial_products(): pl.pallas_call(kernel, grid=(steps,), in_specs=[pl.BlockSpec((count, dept...  33.7 us
    ppermute x22, waiting for transfers between devices, outward(): return lax.ppermute(a, 'mix', OUTWARD)  30.5 us
    pallas_call x6, Pallas kernels, down_product(): pl.pallas_call(kernel, grid=(columns // step,), in_specs=specs, out_specs...  23.7 us
    ppermute x7, waiting for transfers between devices, swap(): return lax.ppermute(a, axis, SWAP)  12.4 us
    dot_general x1, matrix products, attend(): jnp.einsum('chd,cphd->chp', q_heads, k_all, preferred_element_type=jnp.fl...  7.78 us
    dot_general x1, matrix products, attend(): jnp.einsum('chp,cphd->chd', probs, v_all, preferred_element_type=jnp.floa...  5.66 us
    ppermute x7, starting transfers between devices, swap(): return lax.ppermute(a, axis, SWAP)  4.03 us
  transfers between devices with their start and end apart: 47, of which 17 were waited for; matrix products, arithmetic and copies ran while one was open for 0% of the time, Pallas kernels for 28%

profile of v1, /device:TPU:0, one launch (start us, length us, event | category | flops | bytes accessed | tf_op | source)
XLA Modules:
  0.0 197.9 jit_solution(15928388360208977373)
XLA Ops:
  6.1 7.8 %fusion.3 = f32[64,16,1,32]{3,2,1,0:T(1,128)S(1)} fusion(bf16[64,16,128,1]{2,3,1,0:T(2,128)(2,1)S(1)} %reshape.65, bf16[64,32,2048]{2,1,0:T(8,128)(2,1)} %param.15), kind=kOutput, calls=%fused_computation.3 | convolution fusion | flops 8388608 | bytes 8781824 | tf_op jit(solution)/shard_map/chd,cphd->chp/dot_general | solution.py:25
  15.1 5.7 %fusion = f32[64,16,1,128]{3,2,1,0:T(1,128)S(1)} fusion(bf16[64,16,32,1]{2,3,1,0:T(2,128)(2,1)S(1)} %copy.27, bf16[64,32,2048]{2,1,0:T(8,128)(2,1)} %param.16), kind=kOutput, calls=%fused_computation | convolution fusion | flops 8388608 | bytes 8978432 | tf_op jit(solution)/shard_map/chp,cphd->chd/dot_general | solution.py:43
  22.5 2.6 %collective-permute-start.4 = (bf16[64,2048]{1,0:T(8,128)(2,1)S(1)}, bf16[64,2048]{1,0:T(8,128)(2,1)S(1)}, u32[]{:S(2)}, u32[]{:S(2)}) collective-permute-start(bf16[64,2048]{1,0:T(8,128)(2,1)S(1)} %get-tuple-element.119), channel_id=1, source_target_pairs={{0,2},{2,0},{1,3},{3,1},{4,6},{6,4},{5,7},{7,5},{8,10},{10,8},{9,1... | collective-permute-start | bytes 786440 | tf_op jit(solution)/shard_map/ppermute | solution.py:70
  25.1 1.6 collective-permute-start
  26.7 2.0 collective-permute-done
  28.7 2.6 %collective-permute-start.1 = (f32[64,1]{0,1:T(1,128)S(1)}, f32[64,1]{0,1:T(1,128)S(1)}, u32[]{:S(2)}, u32[]{:S(2)}) collective-permute-start(f32[64,1]{0,1:T(1,128)S(1)} %bitcast_add_fusion.1), channel_id=1, source_target_pairs={{0,8},{8,0},{4,12},{12,4},{1,9},{9,1},{5,13},{13,5},{2,10},{10,2},... | collective-permute-start | bytes 776 | tf_op jit(solution)/shard_map/ppermute | solution.py:382
  31.2 1.9 collective-permute-done.1
  33.3 3.3 %collective-permute-done.2 = f32[64,1]{0,1:T(1,128)S(1)} collective-permute-done((f32[64,1]{0,1:T(1,128)S(1)}, f32[64,1]{0,1:T(1,128)S(1)}, u32[]{:S(2)}, u32[]{:S(2)}) %collective-permute-start.2) | collective-permute-done | bytes 288 | tf_op jit(solution)/shard_map/ppermute | solution.py:70
  37.3 3.1 %partial_products.11 = (bf16[128,1024]{1,0:T(8,128)(2,1)S(1)}, bf16[128,1024]{1,0:T(8,128)(2,1)S(1)}) custom-call(bf16[256,2048]{1,0:T(8,128)(2,1)S(1)} %pad_maximum_fusion.rows_ref, bf16[5472,2048]{1,0:T(8,128)(2,1)} %bitcast.58, bf16[5472,2048]{1,0:T(8,128)(2,1)} %bitcast.69), custom_call_target="tpu_custom_call" | custom-call | flops 1073741824 | bytes 4980736 | tf_op jit(solution)/shard_map/partial_products/pallas_call | solution.py:96
  40.4 1.6 collective-permute-start.7
  42.1 3.1 %partial_products.12 = (bf16[128,1024]{1,0:T(8,128)(2,1)S(1)}, bf16[128,1024]{1,0:T(8,128)(2,1)S(1)}) custom-call(bf16[256,2048]{1,0:T(8,128)(2,1)S(1)} %pad_maximum_fusion.rows_ref, bf16[5472,2048]{1,0:T(8,128)(2,1)} %bitcast.59, bf16[5472,2048]{1,0:T(8,128)(2,1)} %bitcast.70, bf16[128,1024]{1,0:T(8,128)(2,1)S(1)} %get-tuple-element.61.rest_0_.refs_4_), custom_call_target="tpu_custom_call" | custom-call | flops 1073741824 | bytes 4980736 | tf_op jit(solution)/shard_map/partial_products/pallas_call | solution.py:96
  45.7 3.1 %partial_products.13 = (bf16[128,1024]{1,0:T(8,128)(2,1)S(1)}, bf16[128,1024]{1,0:T(8,128)(2,1)S(1)}) custom-call(bf16[256,2048]{1,0:T(8,128)(2,1)S(1)} %pad_maximum_fusion.rows_ref, bf16[5472,2048]{1,0:T(8,128)(2,1)} %bitcast.60, bf16[5472,2048]{1,0:T(8,128)(2,1)} %bitcast.71, bf16[128,1024]{1,0:T(8,128)(2,1)S(1)} %get-tuple-element.62.rest_0_.refs_4_), custom_call_target="tpu_custom_call" | custom-call | flops 1073741824 | bytes 4980736 | tf_op jit(solution)/shard_map/partial_products/pallas_call | solution.py:96
  49.7 3.2 %collective-permute-start.8 = (bf16[128,1024]{1,0:T(8,128)(2,1)S(1)}, bf16[128,1024]{1,0:T(8,128)(2,1)S(1)}, u32[]{:S(2)}, u32[]{:S(2)}) collective-permute-start(bf16[128,1024]{1,0:T(8,128)(2,1)S(1)} %get-tuple-element.64.rest_0_), channel_id=1, source_target_pairs={{0,4},{4,0},{8,12},{12,8},{1,5},{5,1},{9,13},{13,9},{2,6},{6,2},{1... | collective-permute-start | bytes 786440 | tf_op jit(solution)/shard_map/ppermute | solution.py:62
  52.9 3.1 %partial_products.14 = (bf16[128,1024]{1,0:T(8,128)(2,1)S(1)}, bf16[128,1024]{1,0:T(8,128)(2,1)S(1)}) custom-call(bf16[256,2048]{1,0:T(8,128)(2,1)S(1)} %pad_maximum_fusion.rows_ref, bf16[5472,2048]{1,0:T(8,128)(2,1)} %bitcast.61, bf16[5472,2048]{1,0:T(8,128)(2,1)} %bitcast.72, bf16[128,1024]{1,0:T(8,128)(2,1)S(1)} %get-tuple-element.64.rest_0_), custom_call_target="tpu_custom_call" | custom-call | flops 1073741824 | bytes 4980736 | tf_op jit(solution)/shard_map/partial_products/pallas_call | solution.py:96
  56.1 2.4 %collective-permute-start.13 = (bf16[128,1024]{1,0:T(8,128)(2,1)S(1)}, bf16[128,1024]{1,0:T(8,128)(2,1)S(1)}, u32[]{:S(2)}, u32[]{:S(2)}) collective-permute-start(bf16[128,1024]{1,0:T(8,128)(2,1)S(1)} %get-tuple-element.67.rest_0_), channel_id=1, source_target_pairs={{0,4},{4,0},{8,12},{12,8},{1,5},{5,1},{9,13},{13,9},{2,6},{6,2},{1... | collective-permute-start | bytes 786440 | tf_op jit(solution)/shard_map/ppermute | solution.py:62
  58.5 3.1 %partial_products.15 = (bf16[128,1024]{1,0:T(8,128)(2,1)S(1)}, bf16[128,1024]{1,0:T(8,128)(2,1)S(1)}) custom-call(bf16[256,2048]{1,0:T(8,128)(2,1)S(1)} %pad_maximum_fusion.rows_ref, bf16[5472,2048]{1,0:T(8,128)(2,1)} %bitcast.62, bf16[5472,2048]{1,0:T(8,128)(2,1)} %bitcast.73, bf16[128,1024]{1,0:T(8,128)(2,1)S(1)} %get-tuple-element.67.rest_0_), custom_call_target="tpu_custom_call" | custom-call | flops 1073741824 | bytes 4980736 | tf_op jit(solution)/shard_map/partial_products/pallas_call | solution.py:96
  61.9 2.5 %collective-permute-start.11 = (bf16[128,1024]{1,0:T(8,128)(2,1)S(1)}, bf16[128,1024]{1,0:T(8,128)(2,1)S(1)}, u32[]{:S(2)}, u32[]{:S(2)}) collective-permute-start(bf16[128,1024]{1,0:T(8,128)(2,1)S(1)} %get-tuple-element.70.rest_0_), channel_id=1, source_target_pairs={{0,4},{4,0},{8,12},{12,8},{1,5},{5,1},{9,13},{13,9},{2,6},{6,2},{1... | collective-permute-start | bytes 786440 | tf_op jit(solution)/shard_map/ppermute | solution.py:62
  64.4 3.1 %partial_products.16 = (bf16[128,1024]{1,0:T(8,128)(2,1)S(1)}, bf16[128,1024]{1,0:T(8,128)(2,1)S(1)}) custom-call(bf16[256,2048]{1,0:T(8,128)(2,1)S(1)} %pad_maximum_fusion.rows_ref, bf16[5472,2048]{1,0:T(8,128)(2,1)} %bitcast.63, bf16[5472,2048]{1,0:T(8,128)(2,1)} %bitcast.74, bf16[128,1024]{1,0:T(8,128)(2,1)S(1)} %get-tuple-element.70.rest_0_), custom_call_target="tpu_custom_call" | custom-call | flops 1073741824 | bytes 4980736 | tf_op jit(solution)/shard_map/partial_products/pallas_call | solution.py:96
  67.5 3.1 %partial_products.17 = (bf16[128,1024]{1,0:T(8,128)(2,1)S(1)}, bf16[128,1024]{1,0:T(8,128)(2,1)S(1)}) custom-call(bf16[256,2048]{1,0:T(8,128)(2,1)S(1)} %pad_maximum_fusion.rows_ref, bf16[5472,2048]{1,0:T(8,128)(2,1)} %bitcast.64, bf16[5472,2048]{1,0:T(8,128)(2,1)} %bitcast.75, bf16[128,1024]{1,0:T(8,128)(2,1)S(1)} %get-tuple-element.75.rest_0_), custom_call_target="tpu_custom_call" | custom-call | flops 1073741824 | bytes 4980736 | tf_op jit(solution)/shard_map/partial_products/pallas_call | solution.py:96
  71.8 1.6 collective-permute-start.15
  73.4 3.2 %collective-permute-start.17 = (bf16[128,1024]{1,0:T(8,128)(2,1)S(1)}, bf16[128,1024]{1,0:T(8,128)(2,1)S(1)}, u32[]{:S(2)}, u32[]{:S(2)}) collective-permute-start(bf16[128,1024]{1,0:T(8,128)(2,1)S(1)} %get-tuple-element.75.rest_0_), channel_id=1, source_target_pairs={{0,4},{4,0},{8,12},{12,8},{1,5},{5,1},{9,13},{13,9},{2,6},{6,2},{1... | collective-permute-start | bytes 786440 | tf_op jit(solution)/shard_map/ppermute | solution.py:62
  76.6 3.1 %partial_products.18 = (bf16[128,1024]{1,0:T(8,128)(2,1)S(1)}, bf16[128,1024]{1,0:T(8,128)(2,1)S(1)}) custom-call(bf16[256,2048]{1,0:T(8,128)(2,1)S(1)} %pad_maximum_fusion.rows_ref, bf16[5472,2048]{1,0:T(8,128)(2,1)} %bitcast.65, bf16[5472,2048]{1,0:T(8,128)(2,1)} %bitcast.76, bf16[128,1536]{1,0:T(8,128)(2,1)S(1)} %get-tuple-element.78.rest_0_.refs_0_), custom_call_target="tpu_custom_call" | custom-call | flops 1073741824 | bytes 4980736 | tf_op jit(solution)/shard_map/partial_products/pallas_call | solution.py:96
  79.7 8.5 %collective-permute-done.17.refs_2_ = bf16[128,1024]{1,0:T(8,128)(2,1)S(1)} collective-permute-done((bf16[128,1024]{1,0:T(8,128)(2,1)S(1)}, bf16[128,1024]{1,0:T(8,128)(2,1)S(1)}, u32[]{:S(2)}, u32[]{:S(2)}) %collective-permute-start.17) | collective-permute-done | bytes 262176 | tf_op jit(solution)/shard_map/ppermute | solution.py:62
  90.0 3.1 %partial_products.19 = (bf16[128,1024]{1,0:T(8,128)(2,1)S(1)}, bf16[128,1024]{1,0:T(8,128)(2,1)S(1)}) custom-call(bf16[256,2048]{1,0:T(8,128)(2,1)S(1)} %pad_maximum_fusion.rows_ref, bf16[5472,2048]{1,0:T(8,128)(2,1)} %bitcast.66, bf16[5472,2048]{1,0:T(8,128)(2,1)} %bitcast.77, bf16[128,1536]{1,0:T(8,128)(2,1)S(1)} %get-tuple-element.83.rest_0_.refs_4_), custom_call_target="tpu_custom_call" | custom-call | flops 1073741824 | bytes 4980736 | tf_op jit(solution)/shard_map/partial_products/pallas_call | solution.py:96
  93.3 3.2 %collective-permute-start.19 = (bf16[128,1536]{1,0:T(8,128)(2,1)S(1)}, bf16[128,1536]{1,0:T(8,128)(2,1)S(1)}, u32[]{:S(2)}, u32[]{:S(2)}) collective-permute-start(bf16[128,1536]{1,0:T(8,128)(2,1)S(1)} %get-tuple-element.86.rest_0_.refs_0_), channel_id=1, source_target_pairs={{0,4},{4,0},{8,12},{12,8},{1,5},{5,1},{9,13},{13,9},{2,6},{6,2},{1... | collective-permute-start | bytes 1179656 | tf_op jit(solution)/shard_map/ppermute | solution.py:62
  96.5 3.1 %partial_products.20 = (bf16[128,1024]{1,0:T(8,128)(2,1)S(1)}, bf16[128,1024]{1,0:T(8,128)(2,1)S(1)}) custom-call(bf16[256,2048]{1,0:T(8,128)(2,1)S(1)} %pad_maximum_fusion.rows_ref, bf16[5472,2048]{1,0:T(8,128)(2,1)} %bitcast.67, bf16[5472,2048]{1,0:T(8,128)(2,1)} %bitcast.78, bf16[128,1536]{1,0:T(8,128)(2,1)S(1)} %get-tuple-element.86.rest_0_.refs_0_), custom_call_target="tpu_custom_call" | custom-call | flops 1073741824 | bytes 4980736 | tf_op jit(solution)/shard_map/partial_products/pallas_call | solution.py:96
  100.4 11.5 %collective-permute-start.25 = (bf16[128,1536]{1,0:T(8,128)(2,1)S(1)}, bf16[128,1536]{1,0:T(8,128)(2,1)S(1)}, u32[]{:S(2)}, u32[]{:S(2)}) collective-permute-start(bf16[128,1536]{1,0:T(8,128)(2,1)S(1)} %get-tuple-element.91.rest_0_.refs_4_), channel_id=1, source_target_pairs={{0,4},{4,0},{8,12},{12,8},{1,5},{5,1},{9,13},{13,9},{2,6},{6,2},{1... | collective-permute-start | bytes 1179656 | tf_op jit(solution)/shard_map/ppermute | solution.py:62
  111.9 3.1 %partial_products.21 = (bf16[128,1024]{1,0:T(8,128)(2,1)S(1)}, bf16[128,1024]{1,0:T(8,128)(2,1)S(1)}) custom-call(bf16[256,2048]{1,0:T(8,128)(2,1)S(1)} %pad_maximum_fusion.rows_ref, bf16[5472,2048]{1,0:T(8,128)(2,1)} %bitcast.68, bf16[5472,2048]{1,0:T(8,128)(2,1)} %bitcast.79, bf16[128,1536]{1,0:T(8,128)(2,1)S(1)} %get-tuple-element.91.rest_0_.refs_4_), custom_call_target="tpu_custom_call" | custom-call | flops 1073741824 | bytes 4980736 | tf_op jit(solution)/shard_map/partial_products/pallas_call | solution.py:96
  115.5 3.8 %collective-permute-done.25.refs_2_.refs_5_ = bf16[128,1536]{1,0:T(8,128)(2,1)S(1)} collective-permute-done((bf16[128,1536]{1,0:T(8,128)(2,1)S(1)}, bf16[128,1536]{1,0:T(8,128)(2,1)S(1)}, u32[]{:S(2)}, u32[]{:S(2)}) %collective-permute-start.25) | collective-permute-done | bytes 393248 | tf_op jit(solution)/shard_map/ppermute | solution.py:62
  119.5 4.6 %collective-permute-start.29 = (bf16[128,1536]{1,0:T(8,128)(2,1)S(1)}, bf16[128,1536]{1,0:T(8,128)(2,1)S(1)}, u32[]{:S(2)}, u32[]{:S(2)}) collective-permute-start(bf16[128,1536]{1,0:T(8,128)(2,1)S(1)} %get-tuple-element.99.refs_7_.refs_4_), channel_id=1, source_target_pairs={{0,4},{4,0},{8,12},{12,8},{1,5},{5,1},{9,13},{13,9},{2,6},{6,2},{1... | collective-permute-start | bytes 1179656 | tf_op jit(solution)/shard_map/ppermute | solution.py:62
  124.1 3.6 %collective-permute-done.23.refs_2_.refs_3_.refs_1_ = bf16[128,1536]{1,0:T(8,128)(2,1)S(1)} collective-permute-done((bf16[128,1536]{1,0:T(8,128)(2,1)S(1)}, bf16[128,1536]{1,0:T(8,128)(2,1)S(1)}, u32[]{:S(2)}, u32[]{:S(2)}) %collective-permute-start.23) | collective-permute-done | bytes 393248 | tf_op jit(solution)/shard_map/ppermute | solution.py:62
  128.0 4.6 %collective-permute-start.27 = (bf16[128,1536]{1,0:T(8,128)(2,1)S(1)}, bf16[128,1536]{1,0:T(8,128)(2,1)S(1)}, u32[]{:S(2)}, u32[]{:S(2)}) collective-permute-start(bf16[128,1536]{1,0:T(8,128)(2,1)S(1)} %get-tuple-element.100.refs_6_.refs_0_), channel_id=1, source_target_pairs={{0,4},{4,0},{8,12},{12,8},{1,5},{5,1},{9,13},{13,9},{2,6},{6,2},{1... | collective-permute-start | bytes 1179656 | tf_op jit(solution)/shard_map/ppermute | solution.py:62
  132.6 3.6 %collective-permute-done.29.refs_7_.refs_2_.refs_5_ = bf16[128,1536]{1,0:T(8,128)(2,1)S(1)} collective-permute-done((bf16[128,1536]{1,0:T(8,128)(2,1)S(1)}, bf16[128,1536]{1,0:T(8,128)(2,1)S(1)}, u32[]{:S(2)}, u32[]{:S(2)}) %collective-permute-start.29) | collective-permute-done | bytes 393248 | tf_op jit(solution)/shard_map/ppermute | solution.py:62
  136.3 2.9 %collective-permute-start.33 = (bf16[128,1536]{1,0:T(8,128)(2,1)S(1)}, bf16[128,1536]{1,0:T(8,128)(2,1)S(1)}, u32[]{:S(2)}, u32[]{:S(2)}) collective-permute-start(bf16[128,1536]{1,0:T(8,128)(2,1)S(1)} %get-tuple-element.107.refs_4_), channel_id=1, source_target_pairs={{0,4},{4,0},{8,12},{12,8},{1,5},{5,1},{9,13},{13,9},{2,6},{6,2},{1... | collective-permute-start | bytes 1179656 | tf_op jit(solution)/shard_map/ppermute | solution.py:62
  139.2 4.1 %down_product.6.refs_6_.refs_9_ = f32[256,2048]{1,0:T(8,128)S(1)} custom-call(s32[1]{0:T(128)} %bitcast.5.refs_0_.outer_ref, bf16[128,1536]{1,0:T(8,128)(2,1)S(1)} %get-tuple-element.78.rest_0_.refs_0_, bf16[128,1536]{1,0:T(8,128)(2,1)S(1)} %collective-permute-done.15.refs_2_.refs_1_, bf16[128,1536]{1,0:T(8,128)(2,1)S(1)} %collective-permute-done.20.refs_3_.refs_2_, ...), custom_call_target="tpu_custom_call" | custom-call | flops 1073741824 | bytes 8388608 | tf_op jit(solution)/shard_map/down_product/pallas_call | solution.py:252
  144.7 2.4 %collective-permute-start.30 = (bf16[128,1536]{1,0:T(8,128)(2,1)S(1)}, bf16[128,1536]{1,0:T(8,128)(2,1)S(1)}, u32[]{:S(2)}, u32[]{:S(2)}) collective-permute-start(bf16[128,1536]{1,0:T(8,128)(2,1)S(1)} %get-tuple-element.103.refs_5_.refs_0_), channel_id=1, source_target_pairs={{0,4},{4,0},{8,12},{12,8},{1,5},{5,1},{9,13},{13,9},{2,6},{6,2},{1... | collective-permute-start | bytes 1179656 | tf_op jit(solution)/shard_map/ppermute | solution.py:62
  148.5 4.5 %collective-permute-done.33.refs_7_.refs_2_.refs_5_ = bf16[128,1536]{1,0:T(8,128)(2,1)S(1)} collective-permute-done((bf16[128,1536]{1,0:T(8,128)(2,1)S(1)}, bf16[128,1536]{1,0:T(8,128)(2,1)S(1)}, u32[]{:S(2)}, u32[]{:S(2)}) %collective-permute-start.33) | collective-permute-done | bytes 393248 | tf_op jit(solution)/shard_map/ppermute | solution.py:62
  153.3 3.2 %collective-permute-start.37 = (bf16[128,512]{1,0:T(8,128)(2,1)S(1)}, bf16[128,512]{1,0:T(8,128)(2,1)S(1)}, u32[]{:S(2)}, u32[]{:S(2)}) collective-permute-start(bf16[128,512]{1,0:T(8,128)(2,1)S(1)} %get-tuple-element.111.refs_4_), channel_id=1, source_target_pairs={{0,4},{4,0},{8,12},{12,8},{1,5},{5,1},{9,13},{13,9},{2,6},{6,2},{1... | collective-permute-start | bytes 393224 | tf_op jit(solution)/shard_map/ppermute | solution.py:62
  156.4 4.1 %down_product.7.refs_5_.refs_9_ = f32[256,2048]{1,0:T(8,128)S(1)} custom-call(s32[1]{0:T(128)} %bitcast.5.refs_0_.outer_ref, bf16[128,1536]{1,0:T(8,128)(2,1)S(1)} %get-tuple-element.86.rest_0_.refs_0_, bf16[128,1536]{1,0:T(8,128)(2,1)S(1)} %collective-permute-done.19.refs_2_.refs_1_, bf16[128,1536]{1,0:T(8,128)(2,1)S(1)} %collective-permute-done.24.refs_3_.refs_2_, ...), custom_call_target="tpu_custom_call" | custom-call | flops 1073741824 | bytes 8388608 | tf_op jit(solution)/shard_map/down_product/pallas_call | solution.py:252
  161.5 2.9 %collective-permute-start.34 = (bf16[128,512]{1,0:T(8,128)(2,1)S(1)}, bf16[128,512]{1,0:T(8,128)(2,1)S(1)}, u32[]{:S(2)}, u32[]{:S(2)}) collective-permute-start(bf16[128,512]{1,0:T(8,128)(2,1)S(1)} %get-tuple-element.108.refs_4_.refs_0_), channel_id=1, source_target_pairs={{0,4},{4,0},{8,12},{12,8},{1,5},{5,1},{9,13},{13,9},{2,6},{6,2},{1... | collective-permute-start | bytes 393224 | tf_op jit(solution)/shard_map/ppermute | solution.py:62
  165.5 4.1 %down_product.8.refs_4_.refs_9_ = f32[256,2048]{1,0:T(8,128)S(1)} custom-call(s32[1]{0:T(128)} %bitcast.5.refs_0_.outer_ref, bf16[128,1536]{1,0:T(8,128)(2,1)S(1)} %get-tuple-element.94.refs_7_.refs_0_, bf16[128,1536]{1,0:T(8,128)(2,1)S(1)} %collective-permute-done.23.refs_2_.refs_3_.refs_1_, bf16[128,1536]{1,0:T(8,128)(2,1)S(1)} %collective-permute-done.28.refs_3_.refs_2_, ...), custom_call_target="tpu_custom_call" | custom-call | flops 1073741824 | bytes 8388608 | tf_op jit(solution)/shard_map/down_product/pallas_call | solution.py:252
  170.2 2.5 %collective-permute-start.39 = (bf16[128,512]{1,0:T(8,128)(2,1)S(1)}, bf16[128,512]{1,0:T(8,128)(2,1)S(1)}, u32[]{:S(2)}, u32[]{:S(2)}) collective-permute-start(bf16[128,512]{1,0:T(8,128)(2,1)S(1)} %get-tuple-element.113.refs_4_), channel_id=1, source_target_pairs={{0,4},{4,0},{8,12},{12,8},{1,5},{5,1},{9,13},{13,9},{2,6},{6,2},{1... | collective-permute-start | bytes 393224 | tf_op jit(solution)/shard_map/ppermute | solution.py:62
  172.8 4.1 %down_product.9.refs_4_.refs_9_ = f32[256,2048]{1,0:T(8,128)S(1)} custom-call(s32[1]{0:T(128)} %bitcast.5.refs_0_.outer_ref, bf16[128,1536]{1,0:T(8,128)(2,1)S(1)} %get-tuple-element.100.refs_6_.refs_0_, bf16[128,1536]{1,0:T(8,128)(2,1)S(1)} %collective-permute-done.27.refs_2_.refs_3_.refs_1_, bf16[128,512]{1,0:T(8,128)(2,1)S(1)} %collective-permute-done.31.refs_3_.refs_2_, ...), custom_call_target="tpu_custom_call" | custom-call | flops 1073741824 | bytes 8388608 | tf_op jit(solution)/shard_map/down_product/pallas_call | solution.py:252
  177.1 1.9 collective-permute-start.42
  179.0 4.1 %down_product.10.refs_5_ = f32[256,2048]{1,0:T(8,128)S(1)} custom-call(s32[1]{0:T(128)} %bitcast.5.refs_0_.outer_ref, bf16[128,1536]{1,0:T(8,128)(2,1)S(1)} %get-tuple-element.103.refs_5_.refs_0_, bf16[128,1536]{1,0:T(8,128)(2,1)S(1)} %collective-permute-done.30.refs_2_.refs_3_.refs_1_, bf16[128,512]{1,0:T(8,128)(2,1)S(1)} %collective-permute-done.35.refs_3_.refs_2_, ...), custom_call_target="tpu_custom_call" | custom-call | flops 1073741824 | bytes 8388608 | tf_op jit(solution)/shard_map/down_product/pallas_call | solution.py:252
  183.1 3.1 %down_product.11 = bf16[256,2048]{1,0:T(8,128)(2,1)S(1)} custom-call(s32[1]{0:T(128)} %bitcast.5.refs_0_.outer_ref, bf16[128,512]{1,0:T(8,128)(2,1)S(1)} %get-tuple-element.108.refs_4_.refs_0_, bf16[128,512]{1,0:T(8,128)(2,1)S(1)} %collective-permute-done.34.refs_2_.refs_3_.refs_1_, bf16[128,512]{1,0:T(8,128)(2,1)S(1)} %collective-permute-done.38.refs_3_.refs_2_, ...), custom_call_target="tpu_custom_call" | custom-call | flops 536870912 | bytes 6291456 | tf_op jit(solution)/shard_map/down_product/pallas_call | solution.py:252
  186.4 1.9 collective-permute-done.45
  189.8 7.1 %collective-permute-done.46 = bf16[64,2048]{1,0:T(8,128)(2,1)S(1)} collective-permute-done((bf16[64,2048]{1,0:T(8,128)(2,1)S(1)}, bf16[64,2048]{1,0:T(8,128)(2,1)S(1)}, u32[]{:S(2)}, u32[]{:S(2)}) %collective-permute-start.46) | collective-permute-done | bytes 262176 | tf_op jit(solution)/shard_map/ppermute | solution.py:70
  (125 shorter events, 24.7 us)
Async XLA Ops:
  22.0 14.9 %collective-permute-start.5 = (bf16[64,2048]{1,0:T(8,128)(2,1)S(1)}, bf16[64,2048]{1,0:T(8,128)(2,1)S(1)}, u32[]{:S(2)}, u32[]{:S(2)}) collective-permute-start(bf16[64,2048]{1,0:T(8,128)(2,1)S(1)} %get-tuple-element.119), channel_id=1, source_target_pairs={{0,1},{1,0},{2,3},{3,2},{4,5},{5,4},{6,7},{7,6},{8,9},{9,8},{10,11... | collective-permute-start | bytes 786440 | tf_op jit(solution)/shard_map/ppermute | solution.py:70
  22.5 10.8 %collective-permute-start.4 = (bf16[64,2048]{1,0:T(8,128)(2,1)S(1)}, bf16[64,2048]{1,0:T(8,128)(2,1)S(1)}, u32[]{:S(2)}, u32[]{:S(2)}) collective-permute-start(bf16[64,2048]{1,0:T(8,128)(2,1)S(1)} %get-tuple-element.119), channel_id=1, source_target_pairs={{0,2},{2,0},{1,3},{3,1},{4,6},{6,4},{5,7},{7,5},{8,10},{10,8},{9,1... | collective-permute-start | bytes 786440 | tf_op jit(solution)/shard_map/ppermute | solution.py:70
  25.1 3.5 %collective-permute-start = (f32[64,1]{0,1:T(1,128)S(1)}, f32[64,1]{0,1:T(1,128)S(1)}, u32[]{:S(2)}, u32[]{:S(2)}) collective-permute-start(f32[64,1]{0,1:T(1,128)S(1)} %bitcast.87), channel_id=1, source_target_pairs={{0,4},{4,0},{8,12},{12,8},{1,5},{5,1},{9,13},{13,9},{2,6},{6,2},{1... | collective-permute-start | bytes 776 | tf_op jit(solution)/shard_map/ppermute | solution.py:62
  28.7 4.4 %collective-permute-start.1 = (f32[64,1]{0,1:T(1,128)S(1)}, f32[64,1]{0,1:T(1,128)S(1)}, u32[]{:S(2)}, u32[]{:S(2)}) collective-permute-start(f32[64,1]{0,1:T(1,128)S(1)} %bitcast_add_fusion.1), channel_id=1, source_target_pairs={{0,8},{8,0},{4,12},{12,4},{1,9},{9,1},{5,13},{13,5},{2,10},{10,2},... | collective-permute-start | bytes 776 | tf_op jit(solution)/shard_map/ppermute | solution.py:382
  33.1 3.5 %collective-permute-start.2 = (f32[64,1]{0,1:T(1,128)S(1)}, f32[64,1]{0,1:T(1,128)S(1)}, u32[]{:S(2)}, u32[]{:S(2)}) collective-permute-start(f32[64,1]{0,1:T(1,128)S(1)} %add_rsqrt_fusion), channel_id=1, source_target_pairs={{0,2},{2,0},{1,3},{3,1},{4,6},{6,4},{5,7},{7,5},{8,10},{10,8},{9,1... | collective-permute-start | bytes 776 | tf_op jit(solution)/shard_map/ppermute | solution.py:70
  33.3 3.6 %collective-permute-start.6 = (bf16[64,2048]{1,0:T(8,128)(2,1)S(1)}, bf16[64,2048]{1,0:T(8,128)(2,1)S(1)}, u32[]{:S(2)}, u32[]{:S(2)}) collective-permute-start(bf16[64,2048]{1,0:T(8,128)(2,1)S(1)} %collective-permute-done.4), channel_id=1, source_target_pairs={{0,1},{1,0},{2,3},{3,2},{4,5},{5,4},{6,7},{7,6},{8,9},{9,8},{10,11... | collective-permute-start | bytes 786440 | tf_op jit(solution)/shard_map/ppermute | solution.py:70
  36.8 5.2 %collective-permute-start.3 = (f32[128,1]{1,0:T(8,128)S(1)}, f32[128,1]{1,0:T(8,128)S(1)}, u32[]{:S(2)}, u32[]{:S(2)}) collective-permute-start(f32[128,1]{1,0:T(8,128)S(1)} %copy.18), channel_id=1, source_target_pairs={{0,1},{1,0},{2,3},{3,2},{4,5},{5,4},{6,7},{7,6},{8,9},{9,8},{10,11... | collective-permute-start | bytes 1544 | tf_op jit(solution)/shard_map/ppermute | solution.py:70
  40.4 9.2 %collective-permute-start.7 = (bf16[128,1024]{1,0:T(8,128)(2,1)S(1)}, bf16[128,1024]{1,0:T(8,128)(2,1)S(1)}, u32[]{:S(2)}, u32[]{:S(2)}) collective-permute-start(bf16[128,1024]{1,0:T(8,128)(2,1)S(1)} %get-tuple-element.61.rest_0_.refs_4_), channel_id=1, source_target_pairs={{0,4},{4,0},{8,12},{12,8},{1,5},{5,1},{9,13},{13,9},{2,6},{6,2},{1... | collective-permute-start | bytes 786440 | tf_op jit(solution)/shard_map/ppermute | solution.py:62
  45.2 10.8 %collective-permute-start.10 = (bf16[128,1024]{1,0:T(8,128)(2,1)S(1)}, bf16[128,1024]{1,0:T(8,128)(2,1)S(1)}, u32[]{:S(2)}, u32[]{:S(2)}) collective-permute-start(bf16[128,1024]{1,0:T(8,128)(2,1)S(1)} %get-tuple-element.62.rest_0_.refs_4_), channel_id=1, source_target_pairs={{0,4},{4,0},{8,12},{12,8},{1,5},{5,1},{9,13},{13,9},{2,6},{6,2},{1... | collective-permute-start | bytes 786440 | tf_op jit(solution)/shard_map/ppermute | solution.py:62
  49.6 11.9 %collective-permute-start.9 = (bf16[128,1024]{1,0:T(8,128)(2,1)S(1)}, bf16[128,1024]{1,0:T(8,128)(2,1)S(1)}, u32[]{:S(2)}, u32[]{:S(2)}) collective-permute-start(bf16[128,1024]{1,0:T(8,128)(2,1)S(1)} %get-tuple-element.65), channel_id=1, source_target_pairs={{0,1},{1,0},{4,8},{8,4},{5,9},{9,5},{12,13},{13,12},{2,3},{3,2},{6... | collective-permute-start | bytes 786440 | tf_op jit(solution)/shard_map/ppermute | solution.py:66
  49.7 11.9 %collective-permute-start.8 = (bf16[128,1024]{1,0:T(8,128)(2,1)S(1)}, bf16[128,1024]{1,0:T(8,128)(2,1)S(1)}, u32[]{:S(2)}, u32[]{:S(2)}) collective-permute-start(bf16[128,1024]{1,0:T(8,128)(2,1)S(1)} %get-tuple-element.64.rest_0_), channel_id=1, source_target_pairs={{0,4},{4,0},{8,12},{12,8},{1,5},{5,1},{9,13},{13,9},{2,6},{6,2},{1... | collective-permute-start | bytes 786440 | tf_op jit(solution)/shard_map/ppermute | solution.py:62
  56.0 11.4 %collective-permute-start.14 = (bf16[128,1024]{1,0:T(8,128)(2,1)S(1)}, bf16[128,1024]{1,0:T(8,128)(2,1)S(1)}, u32[]{:S(2)}, u32[]{:S(2)}) collective-permute-start(bf16[128,1024]{1,0:T(8,128)(2,1)S(1)} %get-tuple-element.72), channel_id=1, source_target_pairs={{0,1},{1,0},{4,8},{8,4},{5,9},{9,5},{12,13},{13,12},{2,3},{3,2},{6... | collective-permute-start | bytes 786440 | tf_op jit(solution)/shard_map/ppermute | solution.py:66
  56.1 11.4 %collective-permute-start.13 = (bf16[128,1024]{1,0:T(8,128)(2,1)S(1)}, bf16[128,1024]{1,0:T(8,128)(2,1)S(1)}, u32[]{:S(2)}, u32[]{:S(2)}) collective-permute-start(bf16[128,1024]{1,0:T(8,128)(2,1)S(1)} %get-tuple-element.67.rest_0_), channel_id=1, source_target_pairs={{0,4},{4,0},{8,12},{12,8},{1,5},{5,1},{9,13},{13,9},{2,6},{6,2},{1... | collective-permute-start | bytes 786440 | tf_op jit(solution)/shard_map/ppermute | solution.py:62
  61.8 8.8 %collective-permute-start.12 = (bf16[128,1024]{1,0:T(8,128)(2,1)S(1)}, bf16[128,1024]{1,0:T(8,128)(2,1)S(1)}, u32[]{:S(2)}, u32[]{:S(2)}) collective-permute-start(bf16[128,1024]{1,0:T(8,128)(2,1)S(1)} %get-tuple-element.71), channel_id=1, source_target_pairs={{0,1},{1,0},{4,8},{8,4},{5,9},{9,5},{12,13},{13,12},{2,3},{3,2},{6... | collective-permute-start | bytes 786440 | tf_op jit(solution)/shard_map/ppermute | solution.py:66
  61.9 9.8 %collective-permute-start.11 = (bf16[128,1024]{1,0:T(8,128)(2,1)S(1)}, bf16[128,1024]{1,0:T(8,128)(2,1)S(1)}, u32[]{:S(2)}, u32[]{:S(2)}) collective-permute-start(bf16[128,1024]{1,0:T(8,128)(2,1)S(1)} %get-tuple-element.70.rest_0_), channel_id=1, source_target_pairs={{0,4},{4,0},{8,12},{12,8},{1,5},{5,1},{9,13},{13,9},{2,6},{6,2},{1... | collective-permute-start | bytes 786440 | tf_op jit(solution)/shard_map/ppermute | solution.py:62
  71.8 21.2 %collective-permute-start.15 = (bf16[128,1536]{1,0:T(8,128)(2,1)S(1)}, bf16[128,1536]{1,0:T(8,128)(2,1)S(1)}, u32[]{:S(2)}, u32[]{:S(2)}) collective-permute-start(bf16[128,1536]{1,0:T(8,128)(2,1)S(1)} %get-tuple-element.78.rest_0_.refs_0_), channel_id=1, source_target_pairs={{0,4},{4,0},{8,12},{12,8},{1,5},{5,1},{9,13},{13,9},{2,6},{6,2},{1... | collective-permute-start | bytes 1179656 | tf_op jit(solution)/shard_map/ppermute | solution.py:62
  73.4 6.3 %collective-permute-start.18 = (bf16[128,1024]{1,0:T(8,128)(2,1)S(1)}, bf16[128,1024]{1,0:T(8,128)(2,1)S(1)}, u32[]{:S(2)}, u32[]{:S(2)}) collective-permute-start(bf16[128,1024]{1,0:T(8,128)(2,1)S(1)} %get-tuple-element.80), channel_id=1, source_target_pairs={{0,1},{1,0},{4,8},{8,4},{5,9},{9,5},{12,13},{13,12},{2,3},{3,2},{6... | collective-permute-start | bytes 786440 | tf_op jit(solution)/shard_map/ppermute | solution.py:66
  73.4 14.8 %collective-permute-start.17 = (bf16[128,1024]{1,0:T(8,128)(2,1)S(1)}, bf16[128,1024]{1,0:T(8,128)(2,1)S(1)}, u32[]{:S(2)}, u32[]{:S(2)}) collective-permute-start(bf16[128,1024]{1,0:T(8,128)(2,1)S(1)} %get-tuple-element.75.rest_0_), channel_id=1, source_target_pairs={{0,4},{4,0},{8,12},{12,8},{1,5},{5,1},{9,13},{13,9},{2,6},{6,2},{1... | collective-permute-start | bytes 786440 | tf_op jit(solution)/shard_map/ppermute | solution.py:62
  76.6 16.4 %collective-permute-start.16 = (bf16[128,1024]{1,0:T(8,128)(2,1)S(1)}, bf16[128,1024]{1,0:T(8,128)(2,1)S(1)}, u32[]{:S(2)}, u32[]{:S(2)}) collective-permute-start(bf16[128,1024]{1,0:T(8,128)(2,1)S(1)} %get-tuple-element.79), channel_id=1, source_target_pairs={{0,1},{1,0},{4,8},{8,4},{5,9},{9,5},{12,13},{13,12},{2,3},{3,2},{6... | collective-permute-start | bytes 786440 | tf_op jit(solution)/shard_map/ppermute | solution.py:66
  88.4 11.7 %collective-permute-start.21 = (bf16[128,1536]{1,0:T(8,128)(2,1)S(1)}, bf16[128,1536]{1,0:T(8,128)(2,1)S(1)}, u32[]{:S(2)}, u32[]{:S(2)}) collective-permute-start(bf16[128,1536]{1,0:T(8,128)(2,1)S(1)} %get-tuple-element.83.rest_0_.refs_4_), channel_id=1, source_target_pairs={{0,4},{4,0},{8,12},{12,8},{1,5},{5,1},{9,13},{13,9},{2,6},{6,2},{1... | collective-permute-start | bytes 1179656 | tf_op jit(solution)/shard_map/ppermute | solution.py:62
  93.2 21.7 %collective-permute-start.20 = (bf16[128,1536]{1,0:T(8,128)(2,1)S(1)}, bf16[128,1536]{1,0:T(8,128)(2,1)S(1)}, u32[]{:S(2)}, u32[]{:S(2)}) collective-permute-start(bf16[128,1536]{1,0:T(8,128)(2,1)S(1)} %get-tuple-element.87), channel_id=1, source_target_pairs={{0,1},{1,0},{4,8},{8,4},{5,9},{9,5},{12,13},{13,12},{2,3},{3,2},{6... | collective-permute-start | bytes 1179656 | tf_op jit(solution)/shard_map/ppermute | solution.py:66
  93.3 21.7 %collective-permute-start.19 = (bf16[128,1536]{1,0:T(8,128)(2,1)S(1)}, bf16[128,1536]{1,0:T(8,128)(2,1)S(1)}, u32[]{:S(2)}, u32[]{:S(2)}) collective-permute-start(bf16[128,1536]{1,0:T(8,128)(2,1)S(1)} %get-tuple-element.86.rest_0_.refs_0_), channel_id=1, source_target_pairs={{0,4},{4,0},{8,12},{12,8},{1,5},{5,1},{9,13},{13,9},{2,6},{6,2},{1... | collective-permute-start | bytes 1179656 | tf_op jit(solution)/shard_map/ppermute | solution.py:62
  96.5 3.1 %collective-permute-start.22 = (bf16[128,1024]{1,0:T(8,128)(2,1)S(1)}, bf16[128,1024]{1,0:T(8,128)(2,1)S(1)}, u32[]{:S(2)}, u32[]{:S(2)}) collective-permute-start(bf16[128,1024]{1,0:T(8,128)(2,1)S(1)} %get-tuple-element.88), channel_id=1, source_target_pairs={{0,1},{1,0},{4,8},{8,4},{5,9},{9,5},{12,13},{13,12},{2,3},{3,2},{6... | collective-permute-start | bytes 786440 | tf_op jit(solution)/shard_map/ppermute | solution.py:66
  100.3 15.2 %collective-permute-start.26 = (bf16[128,1536]{1,0:T(8,128)(2,1)S(1)}, bf16[128,1536]{1,0:T(8,128)(2,1)S(1)}, u32[]{:S(2)}, u32[]{:S(2)}) collective-permute-start(bf16[128,1536]{1,0:T(8,128)(2,1)S(1)} %get-tuple-element.97), channel_id=1, source_target_pairs={{0,1},{1,0},{4,8},{8,4},{5,9},{9,5},{12,13},{13,12},{2,3},{3,2},{6... | collective-permute-start | bytes 1179656 | tf_op jit(solution)/shard_map/ppermute | solution.py:66
  100.4 18.9 %collective-permute-start.25 = (bf16[128,1536]{1,0:T(8,128)(2,1)S(1)}, bf16[128,1536]{1,0:T(8,128)(2,1)S(1)}, u32[]{:S(2)}, u32[]{:S(2)}) collective-permute-start(bf16[128,1536]{1,0:T(8,128)(2,1)S(1)} %get-tuple-element.91.rest_0_.refs_4_), channel_id=1, source_target_pairs={{0,4},{4,0},{8,12},{12,8},{1,5},{5,1},{9,13},{13,9},{2,6},{6,2},{1... | collective-permute-start | bytes 1179656 | tf_op jit(solution)/shard_map/ppermute | solution.py:62
  115.2 9.0 %collective-permute-start.24 = (bf16[128,1536]{1,0:T(8,128)(2,1)S(1)}, bf16[128,1536]{1,0:T(8,128)(2,1)S(1)}, u32[]{:S(2)}, u32[]{:S(2)}) collective-permute-start(bf16[128,1536]{1,0:T(8,128)(2,1)S(1)} %get-tuple-element.95), channel_id=1, source_target_pairs={{0,1},{1,0},{4,8},{8,4},{5,9},{9,5},{12,13},{13,12},{2,3},{3,2},{6... | collective-permute-start | bytes 1179656 | tf_op jit(solution)/shard_map/ppermute | solution.py:66
  115.2 12.5 %collective-permute-start.23 = (bf16[128,1536]{1,0:T(8,128)(2,1)S(1)}, bf16[128,1536]{1,0:T(8,128)(2,1)S(1)}, u32[]{:S(2)}, u32[]{:S(2)}) collective-permute-start(bf16[128,1536]{1,0:T(8,128)(2,1)S(1)} %get-tuple-element.94.refs_7_.refs_0_), channel_id=1, source_target_pairs={{0,4},{4,0},{8,12},{12,8},{1,5},{5,1},{9,13},{13,9},{2,6},{6,2},{1... | collective-permute-start | bytes 1179656 | tf_op jit(solution)/shard_map/ppermute | solution.py:62
  119.5 13.1 %collective-permute-start.32 = (bf16[128,1536]{1,0:T(8,128)(2,1)S(1)}, bf16[128,1536]{1,0:T(8,128)(2,1)S(1)}, u32[]{:S(2)}, u32[]{:S(2)}) collective-permute-start(bf16[128,1536]{1,0:T(8,128)(2,1)S(1)} %get-tuple-element.105), channel_id=1, source_target_pairs={{0,1},{1,0},{4,8},{8,4},{5,9},{9,5},{12,13},{13,12},{2,3},{3,2},{6... | collective-permute-start | bytes 1179656 | tf_op jit(solution)/shard_map/ppermute | solution.py:66
  119.5 16.6 %collective-permute-start.29 = (bf16[128,1536]{1,0:T(8,128)(2,1)S(1)}, bf16[128,1536]{1,0:T(8,128)(2,1)S(1)}, u32[]{:S(2)}, u32[]{:S(2)}) collective-permute-start(bf16[128,1536]{1,0:T(8,128)(2,1)S(1)} %get-tuple-element.99.refs_7_.refs_4_), channel_id=1, source_target_pairs={{0,4},{4,0},{8,12},{12,8},{1,5},{5,1},{9,13},{13,9},{2,6},{6,2},{1... | collective-permute-start | bytes 1179656 | tf_op jit(solution)/shard_map/ppermute | solution.py:62
  127.9 15.4 %collective-permute-start.28 = (bf16[128,1536]{1,0:T(8,128)(2,1)S(1)}, bf16[128,1536]{1,0:T(8,128)(2,1)S(1)}, u32[]{:S(2)}, u32[]{:S(2)}) collective-permute-start(bf16[128,1536]{1,0:T(8,128)(2,1)S(1)} %get-tuple-element.101), channel_id=1, source_target_pairs={{0,1},{1,0},{4,8},{8,4},{5,9},{9,5},{12,13},{13,12},{2,3},{3,2},{6... | collective-permute-start | bytes 1179656 | tf_op jit(solution)/shard_map/ppermute | solution.py:66
  128.0 16.6 %collective-permute-start.27 = (bf16[128,1536]{1,0:T(8,128)(2,1)S(1)}, bf16[128,1536]{1,0:T(8,128)(2,1)S(1)}, u32[]{:S(2)}, u32[]{:S(2)}) collective-permute-start(bf16[128,1536]{1,0:T(8,128)(2,1)S(1)} %get-tuple-element.100.refs_6_.refs_0_), channel_id=1, source_target_pairs={{0,4},{4,0},{8,12},{12,8},{1,5},{5,1},{9,13},{13,9},{2,6},{6,2},{1... | collective-permute-start | bytes 1179656 | tf_op jit(solution)/shard_map/ppermute | solution.py:62
  136.3 16.7 %collective-permute-start.33 = (bf16[128,1536]{1,0:T(8,128)(2,1)S(1)}, bf16[128,1536]{1,0:T(8,128)(2,1)S(1)}, u32[]{:S(2)}, u32[]{:S(2)}) collective-permute-start(bf16[128,1536]{1,0:T(8,128)(2,1)S(1)} %get-tuple-element.107.refs_4_), channel_id=1, source_target_pairs={{0,4},{4,0},{8,12},{12,8},{1,5},{5,1},{9,13},{13,9},{2,6},{6,2},{1... | collective-permute-start | bytes 1179656 | tf_op jit(solution)/shard_map/ppermute | solution.py:62
  144.7 16.5 %collective-permute-start.30 = (bf16[128,1536]{1,0:T(8,128)(2,1)S(1)}, bf16[128,1536]{1,0:T(8,128)(2,1)S(1)}, u32[]{:S(2)}, u32[]{:S(2)}) collective-permute-start(bf16[128,1536]{1,0:T(8,128)(2,1)S(1)} %get-tuple-element.103.refs_5_.refs_0_), channel_id=1, source_target_pairs={{0,4},{4,0},{8,12},{12,8},{1,5},{5,1},{9,13},{13,9},{2,6},{6,2},{1... | collective-permute-start | bytes 1179656 | tf_op jit(solution)/shard_map/ppermute | solution.py:62
  147.2 1.3 collective-permute-start.36
  147.2 13.4 %collective-permute-start.31 = (bf16[128,512]{1,0:T(8,128)(2,1)S(1)}, bf16[128,512]{1,0:T(8,128)(2,1)S(1)}, u32[]{:S(2)}, u32[]{:S(2)}) collective-permute-start(bf16[128,512]{1,0:T(8,128)(2,1)S(1)} %get-tuple-element.104), channel_id=1, source_target_pairs={{0,1},{1,0},{4,8},{8,4},{5,9},{9,5},{12,13},{13,12},{2,3},{3,2},{6... | collective-permute-start | bytes 393224 | tf_op jit(solution)/shard_map/ppermute | solution.py:66
  153.2 11.2 %collective-permute-start.40 = (bf16[128,512]{1,0:T(8,128)(2,1)S(1)}, bf16[128,512]{1,0:T(8,128)(2,1)S(1)}, u32[]{:S(2)}, u32[]{:S(2)}) collective-permute-start(bf16[128,512]{1,0:T(8,128)(2,1)S(1)} %get-tuple-element.114), channel_id=1, source_target_pairs={{0,1},{1,0},{4,8},{8,4},{5,9},{9,5},{12,13},{13,12},{2,3},{3,2},{6... | collective-permute-start | bytes 393224 | tf_op jit(solution)/shard_map/ppermute | solution.py:66
  153.3 11.2 %collective-permute-start.37 = (bf16[128,512]{1,0:T(8,128)(2,1)S(1)}, bf16[128,512]{1,0:T(8,128)(2,1)S(1)}, u32[]{:S(2)}, u32[]{:S(2)}) collective-permute-start(bf16[128,512]{1,0:T(8,128)(2,1)S(1)} %get-tuple-element.111.refs_4_), channel_id=1, source_target_pairs={{0,4},{4,0},{8,12},{12,8},{1,5},{5,1},{9,13},{13,9},{2,6},{6,2},{1... | collective-permute-start | bytes 393224 | tf_op jit(solution)/shard_map/ppermute | solution.py:62
  161.5 8.1 %collective-permute-start.35 = (bf16[128,512]{1,0:T(8,128)(2,1)S(1)}, bf16[128,512]{1,0:T(8,128)(2,1)S(1)}, u32[]{:S(2)}, u32[]{:S(2)}) collective-permute-start(bf16[128,512]{1,0:T(8,128)(2,1)S(1)} %get-tuple-element.109), channel_id=1, source_target_pairs={{0,1},{1,0},{4,8},{8,4},{5,9},{9,5},{12,13},{13,12},{2,3},{3,2},{6... | collective-permute-start | bytes 393224 | tf_op jit(solution)/shard_map/ppermute | solution.py:66
  161.5 8.1 %collective-permute-start.34 = (bf16[128,512]{1,0:T(8,128)(2,1)S(1)}, bf16[128,512]{1,0:T(8,128)(2,1)S(1)}, u32[]{:S(2)}, u32[]{:S(2)}) collective-permute-start(bf16[128,512]{1,0:T(8,128)(2,1)S(1)} %get-tuple-element.108.refs_4_.refs_0_), channel_id=1, source_target_pairs={{0,4},{4,0},{8,12},{12,8},{1,5},{5,1},{9,13},{13,9},{2,6},{6,2},{1... | collective-permute-start | bytes 393224 | tf_op jit(solution)/shard_map/ppermute | solution.py:62
  164.4 8.3 %collective-permute-start.41 = (bf16[128,512]{1,0:T(8,128)(2,1)S(1)}, bf16[128,512]{1,0:T(8,128)(2,1)S(1)}, u32[]{:S(2)}, u32[]{:S(2)}) collective-permute-start(bf16[128,512]{1,0:T(8,128)(2,1)S(1)} %get-tuple-element.115), channel_id=1, source_target_pairs={{0,4},{4,0},{8,12},{12,8},{1,5},{5,1},{9,13},{13,9},{2,6},{6,2},{1... | collective-permute-start | bytes 393224 | tf_op jit(solution)/shard_map/ppermute | solution.py:62
  165.5 7.3 %collective-permute-start.43 = (bf16[128,512]{1,0:T(8,128)(2,1)S(1)}, bf16[128,512]{1,0:T(8,128)(2,1)S(1)}, u32[]{:S(2)}, u32[]{:S(2)}) collective-permute-start(bf16[128,512]{1,0:T(8,128)(2,1)S(1)} %get-tuple-element.116), channel_id=1, source_target_pairs={{0,1},{1,0},{4,8},{8,4},{5,9},{9,5},{12,13},{13,12},{2,3},{3,2},{6... | collective-permute-start | bytes 393224 | tf_op jit(solution)/shard_map/ppermute | solution.py:66
  169.6 7.3 %collective-permute-start.38 = (bf16[128,512]{1,0:T(8,128)(2,1)S(1)}, bf16[128,512]{1,0:T(8,128)(2,1)S(1)}, u32[]{:S(2)}, u32[]{:S(2)}) collective-permute-start(bf16[128,512]{1,0:T(8,128)(2,1)S(1)} %get-tuple-element.112), channel_id=1, source_target_pairs={{0,1},{1,0},{4,8},{8,4},{5,9},{9,5},{12,13},{13,12},{2,3},{3,2},{6... | collective-permute-start | bytes 393224 | tf_op jit(solution)/shard_map/ppermute | solution.py:66
  170.2 6.9 %collective-permute-start.39 = (bf16[128,512]{1,0:T(8,128)(2,1)S(1)}, bf16[128,512]{1,0:T(8,128)(2,1)S(1)}, u32[]{:S(2)}, u32[]{:S(2)}) collective-permute-start(bf16[128,512]{1,0:T(8,128)(2,1)S(1)} %get-tuple-element.113.refs_4_), channel_id=1, source_target_pairs={{0,4},{4,0},{8,12},{12,8},{1,5},{5,1},{9,13},{13,9},{2,6},{6,2},{1... | collective-permute-start | bytes 393224 | tf_op jit(solution)/shard_map/ppermute | solution.py:62
  172.7 6.3 %collective-permute-start.44 = (bf16[128,512]{1,0:T(8,128)(2,1)S(1)}, bf16[128,512]{1,0:T(8,128)(2,1)S(1)}, u32[]{:S(2)}, u32[]{:S(2)}) collective-permute-start(bf16[128,512]{1,0:T(8,128)(2,1)S(1)} %hop.37), channel_id=1, source_target_pairs={{0,4},{4,0},{8,12},{12,8},{1,5},{5,1},{9,13},{13,9},{2,6},{6,2},{1... | collective-permute-start | bytes 393224 | tf_op jit(solution)/shard_map/ppermute | solution.py:62
  177.1 6.0 %collective-permute-start.42 = (bf16[128,512]{1,0:T(8,128)(2,1)S(1)}, bf16[128,512]{1,0:T(8,128)(2,1)S(1)}, u32[]{:S(2)}, u32[]{:S(2)}) collective-permute-start(bf16[128,512]{1,0:T(8,128)(2,1)S(1)} %hop.36), channel_id=1, source_target_pairs={{0,4},{4,0},{8,12},{12,8},{1,5},{5,1},{9,13},{13,9},{2,6},{6,2},{1... | collective-permute-start | bytes 393224 | tf_op jit(solution)/shard_map/ppermute | solution.py:62
  183.1 13.9 %copy-start.1 = (f32[64,16,128]{2,1,0:T(8,128)S(1)}, f32[64,16,128]{2,1,0:T(8,128)}, u32[]{:S(2)}) copy-start(f32[64,16,128]{2,1,0:T(8,128)} %copy-done) | copy-start | bytes 1572868
  186.3 2.0 collective-permute-start.45
  188.5 8.4 %collective-permute-start.46 = (bf16[64,2048]{1,0:T(8,128)(2,1)S(1)}, bf16[64,2048]{1,0:T(8,128)(2,1)S(1)}, u32[]{:S(2)}, u32[]{:S(2)}) collective-permute-start(bf16[64,2048]{1,0:T(8,128)(2,1)S(1)} %slice.33), channel_id=1, source_target_pairs={{0,2},{2,0},{1,3},{3,1},{4,6},{6,4},{5,7},{7,5},{8,10},{10,8},{9,1... | collective-permute-start | bytes 786440 | tf_op jit(solution)/shard_map/ppermute | solution.py:70
  (3 other events, 22.5 us)

commit v2 on v1

--- a/solution.py
+++ b/solution.py
@@ -47,6 +47,9 @@
 
 
 WIDTH = 512
+LANES = 128
+TWO = 2 * WIDTH
+SCALE = 4
 OUTWARD = ((0, 1), (1, 0), (2, 3), (3, 2))
 ACROSS = ((0, 2), (2, 0), (1, 3), (3, 1))
 MIDDLE = ((0, 1), (1, 0), (2, 4), (4, 2), (3, 5), (5, 3), (6, 7), (7, 6))
@@ -58,6 +61,10 @@
 VMEM = pl.BlockSpec(memory_space=pltpu.VMEM)
 
 
+def cost(flops, moved):
+    return pl.CostEstimate(flops=int(flops * SCALE), bytes_accessed=int(moved * SCALE), transcendentals=0)
+
+
 def outward(a):
     return lax.ppermute(a, "mix", OUTWARD)
 
@@ -70,17 +77,129 @@
     return lax.ppermute(a, axis, SWAP)
 
 
+def chunk_columns(k):
+    return TWO + (LANES if k == 0 else 0)
+
+
+def in_three(total, shape):
+    lane = lax.broadcasted_iota(jnp.int32, shape, 1)
+    high = total.astype(bf16).astype(f32)
+    middle_part = (total - high).astype(bf16).astype(f32)
+    low = total - high - middle_part
+    three = jnp.where(lane == 0, high, jnp.where(lane == 1, middle_part, jnp.where(lane == 2, low, 0.0)))
+    return three.astype(bf16)
+
+
+def add_in_three(a, b):
+    lane = lax.broadcasted_iota(jnp.int32, a.shape, 1)
+    total = jnp.sum(jnp.where(lane < 3, a.astype(f32) + b.astype(f32), 0.0), axis=1, keepdims=True)
+    return total, in_three(total, a.shape)
+
+
+def attend_rows(query, new_key, new_value, key_cache, value_cache, lengths, residual, norm_gain):
+    rows, features = query.shape
+    heads = features // HD
+    cache_len = key_cache.shape[1]
+    block = 16
+    tall, wide = heads * block, block * cache_len
+    scale = 1.0 / HD**0.5
+    held = functools.partial(pltpu.with_memory_space_constraint, memory_space=pltpu.HBM)
+
+    def kernel(length_ref, q_ref, nk_ref, nv_ref, k_ref, v_ref, res_ref, gain_ref, x_ref, scaled_ref, sparse):
+        @pl.when(pl.program_id(0) == 0)
+        def _():
+            sparse[...] = jnp.zeros_like(sparse)
+
+        for h in range(heads):
+            sparse[h * block : (h + 1) * block, h * HD : (h + 1) * HD] = q_ref[:, h * HD : (h + 1) * HD]
+        q_rows = sparse[...]
+        over = (((1,), (1,)), ((), ()))
+        keys = k_ref[...].reshape(wide, features)
+        scores = lax.dot_general(q_rows, keys, over, preferred_element_type=f32) * scale
+        own = lax.dot_general(q_rows, nk_ref[...], over, preferred_element_type=f32) * scale
+        mine = lax.broadcasted_iota(jnp.int32, own.shape, 0) % block == lax.broadcasted_iota(jnp.int32, own.shape, 1)
+        own = jnp.sum(jnp.where(mine, own, 0.0), axis=1, keepdims=True)
+        column = lax.broadcasted_iota(jnp.int32, scores.shape, 1)
+        owner = lax.broadcasted_iota(jnp.int32, scores.shape, 0) % block
+        offset = column - owner * cache_len
+        candidate = lax.broadcasted_iota(jnp.int32, (tall, 1), 0) % block
+        span = jnp.zeros((tall, 1), jnp.int32)
+        for c in range(block):
+            span = jnp.where(candidate == c, length_ref[pl.program_id(0) * block + c], span)
+        valid = (offset >= 0) & (offset < span)
+        scores = jnp.where(valid, scores, -jnp.inf)
+        top = jnp.maximum(jnp.max(scores, axis=1, keepdims=True), own)
+        weights = jnp.exp(scores - top)
+        own_w = jnp.exp(own - top)
+        total = jnp.sum(weights, axis=1, keepdims=True) + own_w
+        probs = (weights / total).astype(bf16)
+        own_p = (own_w / total).astype(bf16).astype(f32)
+        mixed = jnp.dot(probs, v_ref[...].reshape(wide, features), preferred_element_type=f32)
+        squares = jnp.zeros((block, HD), f32)
+        for h in range(heads):
+            at, rows_at = slice(h * HD, (h + 1) * HD), slice(h * block, (h + 1) * block)
+            x = res_ref[:, at].astype(f32) + mixed[rows_at, at] + own_p[rows_at] * nv_ref[:, at].astype(f32)
+            x_ref[:, at] = x
+            scaled_ref[:, at] = (x * gain_ref[:, at].astype(f32)).astype(bf16)
+            squares = squares + x * x
+        scaled_ref[:, features:] = in_three(jnp.sum(squares, axis=1, keepdims=True), (block, LANES))
+
+    flat = pl.BlockSpec((block, features), lambda i: (i, 0))
+    cache = pl.BlockSpec((block, cache_len, features), lambda i: (i, 0, 0))
+    return pl.pallas_call(
+        kernel,
+        grid=(rows // block,),
+        in_specs=[
+            SMEM,
+            flat,
+            flat,
+            flat,
+            cache,
+            cache,
+            flat,
+            pl.BlockSpec((1, features), lambda i: (0, 0)),
+        ],
+        out_specs=[flat, pl.BlockSpec((block, features + LANES), lambda i: (i, 0))],
+        out_shape=[
+            jax.ShapeDtypeStruct((rows, features), f32),
+            jax.ShapeDtypeStruct((rows, features + LANES), bf16),
+        ],
+        scratch_shapes=[pltpu.VMEM((tall, features), bf16)],
+        compiler_params=pltpu.CompilerParams(vmem_limit_bytes=40 << 20),
+        cost_estimate=pl.CostEstimate(
+            flops=4 * rows // block * tall * wide * features,
+            bytes_accessed=4 * rows * cache_len * features,
+            transcendentals=rows // block * tall * wide,
+        ),
+        name="attend_rows",
+    )(
+        lengths,
+        held(query),
+        held(new_key),
+        held(new_value),
+        held(key_cache),
+        held(value_cache),
+        held(residual),
+        norm_gain.reshape(1, -1),
+    )
+
+
 def partial_products(k, rows, gate_rows, up_rows, after):
-    count, depth = rows.shape
+    count = rows.shape[0]
     units = gate_rows.shape[0]
     half = count // 2
     valid = min(WIDTH, units - k * WIDTH)
     step = 256
     steps = WIDTH // step
+    depth = gate_rows.shape[1]
+    columns = chunk_columns(k)
 
     def kernel(rows_ref, gate_ref, up_ref, *rest):
         out_ref, in_ref = rest[-2:]
         i = pl.program_id(0)
+        if columns > TWO:
+            out_ref[:, TWO:] = rest[0][:half]
+            in_ref[:, TWO:] = rest[0][half:]
         for weight, offset in ((gate_ref, 0), (up_ref, WIDTH)):
             part = lax.dot_general(rows_ref[...], weight[...], (((1,), (1,)), ((), ())), preferred_element_type=f32)
             if valid < WIDTH:
@@ -91,7 +210,7 @@
             out_ref[:, at] = part[:half]
             in_ref[:, at] = part[half:]
 
-    shape = jax.ShapeDtypeStruct((half, 2 * WIDTH), bf16)
+    shape = jax.ShapeDtypeStruct((half, columns), bf16)
     first = k * steps
     return pl.pallas_call(
         kernel,
@@ -101,41 +220,36 @@
             pl.BlockSpec((step, depth), lambda i: (first + i, 0)),
             pl.BlockSpec((step, depth), lambda i: (first + i, 0)),
         ]
+        + ([pl.BlockSpec((count, LANES), lambda i: (0, depth // LANES))] if columns > TWO else [])
         + [ANY] * len(after),
-        out_specs=[pl.BlockSpec((half, 2 * WIDTH), lambda i: (0, 0))] * 2,
+        out_specs=[pl.BlockSpec((half, columns), lambda i: (0, 0))] * 2,
         out_shape=[shape, shape],
         compiler_params=pltpu.CompilerParams(vmem_limit_bytes=24 << 20),
-        cost_estimate=pl.CostEstimate(
-            flops=4 * count * depth * WIDTH, bytes_accessed=4 * depth * WIDTH + 6 * count * WIDTH, transcendentals=0
-        ),
+        cost_estimate=cost(4 * count * depth * WIDTH, 4 * depth * WIDTH + 6 * count * WIDTH),
         name="partial_products",
-    )(rows, gate_rows, up_rows, *after)
-
-
-def hop(outer, inv_in, t, count, got_e, got_m, part_out, part_in, after):
-    half = inv_in.shape[0]
-
-    def inside(k):
-        return 0 <= k < count
-
-    def sums_e(s):
-        return inside(s) or inside(s - 2)
-
-    def hid_e(s):
-        return inside(s - 3) or inside(s - 5)
-
-    two = 2 * WIDTH
-    names = ["outer", "inv"]
-    operands = [outer, inv_in]
-    specs = [SMEM, VMEM]
+    )(rows, gate_rows, up_rows, *([rows] if columns > TWO else []), *after)
+
+
+def hop(outer, inv_in, s, t, count, got_e, got_m, part_out, part_in, after):
+    half = part_out[0].shape[0]
+
+    def inside(j):
+        return 0 <= j < count
+
+    def columns(*js):
+        return max([chunk_columns(2 * j + s) for j in js if inside(j)], default=0)
+
+    def hid_e(step):
+        return inside(step - 3) or inside(step - 5)
+
+    names, operands, specs = ["outer"], [outer], [SMEM]
 
     def add(name, value):
         names.append(name)
         operands.append(value)
         specs.append(VMEM)
 
-    need_sum_in = inside(t - 2)
-    if need_sum_in or hid_e(t) or inside(t):
+    if columns(t, t - 2) or hid_e(t):
         add("got_e", got_e)
     if got_m is not None and (inside(t - 1) or inside(t - 4)):
         add("got_m", got_m)
@@ -145,16 +259,19 @@
         add("out", part_out[t])
     if inside(t - 1):
         add("in1", part_in[t - 1])
+    starts_inv = inside(t - 2) and columns(t - 2) > TWO
     if inside(t - 2):
         add("in2", part_in[t - 2])
+        if not starts_inv:
+            add("inv", inv_in)
     operands += after
     specs += [ANY] * len(after)
     nxt = t + 1
-    hid_at_e = two if sums_e(nxt) else 0
-    hid_at_got_e = two if sums_e(t) else 0
+    hid_at_e = columns(nxt, nxt - 2)
+    hid_at_got_e = columns(t, t - 2)
     width_e = hid_at_e + (WIDTH if hid_e(nxt) else 0)
-    hid_at_m = two if inside(t) else 0
-    hid_at_got_m = two if inside(t - 1) else 0
+    hid_at_m = columns(t)
+    hid_at_got_m = columns(t - 1)
     width_m = hid_at_m + (WIDTH if inside(t - 3) else 0)
     widths = [w for w in (width_e, width_m) if w]
 
@@ -164,40 +281,55 @@
         to_e = outs.pop(0) if width_e else None
         to_m = outs.pop(0) if width_m else None
 
+        def both(own, received, to, j):
+            to[:, :TWO] = (own[:, :TWO].astype(f32) + received[:, :TWO].astype(f32)).astype(bf16)
+            if columns(j) > TWO:
+                to[:, TWO : columns(j)] = add_in_three(own[:, TWO:], received[:, TWO : columns(j)])[1]
+
         @pl.when(r["outer"][0] != 0)
         def _():
             if inside(t + 1):
-                to_e[:, :two] = r["next_out"][...]
+                to_e[:, :TWO] = r["next_out"][:, :TWO]
             if inside(t - 2):
-                inv = r["inv"][...]
+                if starts_inv:
+                    squares, _ = add_in_three(r["in2"][:, TWO:], r["got_e"][:, TWO : TWO + LANES])
+                    inv = lax.rsqrt(squares / D + eps)
+                    outs[0][...] = inv
+                else:
+                    inv = r["inv"][...]
                 gate = (r["in2"][:, :WIDTH].astype(f32) + r["got_e"][:, :WIDTH].astype(f32)) * inv
-                up = (r["in2"][:, WIDTH:].astype(f32) + r["got_e"][:, WIDTH:two].astype(f32)) * inv
+                up = (r["in2"][:, WIDTH:TWO].astype(f32) + r["got_e"][:, WIDTH:TWO].astype(f32)) * inv
                 to_e[:, hid_at_e : hid_at_e + WIDTH] = (gate / (1.0 + jnp.exp(-gate)) * up).astype(bf16)
 
         @pl.when(r["outer"][0] == 0)
         def _():
             if inside(t - 1):
-                to_e[:, :two] = (r["in1"][...].astype(f32) + r["got_m"][:, :two].astype(f32)).astype(bf16)
+                both(r["in1"], r["got_m"], to_e, t - 1)
             if inside(t - 4):
                 to_e[:, hid_at_e : hid_at_e + WIDTH] = r["got_m"][:, hid_at_got_m : hid_at_got_m + WIDTH]
             if inside(t):
-                to_m[:, :two] = (r["out"][...].astype(f32) + r["got_e"][:, :two].astype(f32)).astype(bf16)
+                both(r["out"], r["got_e"], to_m, t)
             if inside(t - 3):
                 to_m[:, hid_at_m : hid_at_m + WIDTH] = r["got_e"][:, hid_at_got_e : hid_at_got_e + WIDTH]
-
+            if starts_inv:
+                outs[0][...] = jnp.zeros(outs[0].shape, f32)
+
+    shapes = [jax.ShapeDtypeStruct((half, w), bf16) for w in widths]
+    if starts_inv:
+        shapes.append(jax.ShapeDtypeStruct((half, 1), f32))
     outs = pl.pallas_call(
         kernel,
         in_specs=specs,
-        out_specs=[VMEM] * len(widths),
-        out_shape=[jax.ShapeDtypeStruct((half, w), bf16) for w in widths],
+        out_specs=[VMEM] * len(shapes),
+        out_shape=shapes,
         compiler_params=pltpu.CompilerParams(vmem_limit_bytes=24 << 20),
-        cost_estimate=pl.CostEstimate(flops=8 * half * two, bytes_accessed=10 * half * two, transcendentals=half * WIDTH),
+        cost_estimate=cost(8 * half * TWO, 10 * half * TWO),
         name="hop",
     )(*operands)
     outs = list(outs)
     to_e = (outs.pop(0), hid_at_e) if width_e else None
     to_m = (outs.pop(0), hid_at_m) if width_m else None
-    return to_e, to_m
+    return to_e, to_m, outs[0] if outs else inv_in
 
 
 def down_product(outer, total, first, chunks, w_down, final):
@@ -257,16 +389,12 @@
         out_shape=jax.ShapeDtypeStruct((2 * half, columns), bf16 if final else f32),
         scratch_shapes=[pltpu.VMEM((2 * half, n * WIDTH), bf16)],
         compiler_params=pltpu.CompilerParams(vmem_limit_bytes=24 << 20),
-        cost_estimate=pl.CostEstimate(
-            flops=4 * half * n * WIDTH * columns,
-            bytes_accessed=2 * n * WIDTH * columns + 16 * half * columns,
-            transcendentals=0,
-        ),
+        cost_estimate=cost(4 * half * n * WIDTH * columns, 2 * n * WIDTH * columns + 16 * half * columns),
         name="down_product",
     )(*operands)
 
 
-def mlp_line(scaled, rows_rms, w_gate, w_up, w_down):
+def mlp_line(scaled, w_gate, w_up, w_down):
     place = lax.axis_index("mix")
     left = place < 2
     outer = ((place == 0) | (place == 3)).astype(jnp.int32).reshape(1)
@@ -279,9 +407,6 @@
     rows = jnp.concatenate([jnp.where(left, here, there), jnp.where(left, there, here)])
     half = here.shape[0]
 
-    inv = jnp.concatenate([rows_rms, swap(rows_rms, "ffn")])
-    inv_in = jnp.where(left, swap(inv, "pair"), inv)
-
     gate_rows = pltpu.with_memory_space_constraint(w_gate.T, pltpu.HBM)
     up_rows = pltpu.with_memory_space_constraint(w_up.T, pltpu.HBM)
     w_down = pltpu.with_memory_space_constraint(w_down, pltpu.HBM)
@@ -307,19 +432,20 @@
         return [sent["e", s, j + 3], got["e", s, j + 3], got["m", s, j + 4], got["e", s, j + 5]]
 
     after = products(0, [])
-    send(0, 0, (part_out[0][0], 2 * WIDTH), None)
+    send(0, 0, (part_out[0][0], TWO), None)
     after = products(1, after)
-    send(1, 0, (part_out[1][0], 2 * WIDTH), None)
+    send(1, 0, (part_out[1][0], TWO), None)
     after = products(2, after)
-    total = None
+    total, inv_in = None, None
     for t in range(counts[0] + 5):
         for s in (0, 1):
             count = counts[s]
             if t < count + 4:
                 got_e, got_m = got["e", s, t], got["m", s, t]
-                to_e, to_m = hop(
+                to_e, to_m, inv_in = hop(
                     outer,
                     inv_in,
+                    s,
                     t,
                     count,
                     got_e and got_e[0],
@@ -373,18 +499,16 @@
     w_up,
     w_down,
 ):
-    mixed = attend(query, new_key, new_value, key_cache, value_cache, lengths)
-    x = residual.astype(jnp.float32) + mixed
-    gain = norm_gain.astype(jnp.float32)
-    squares = jnp.sum(x * x, axis=1, keepdims=True)
     if on_line:
-        squares = squares + outward(squares)
-        squares = squares + lax.ppermute(squares, "mix", ACROSS)
-        inv = lax.rsqrt(squares / D + eps)
-        mlp = mlp_line((x * gain).astype(jnp.bfloat16), inv, w_gate, w_up, w_down)
+        x, scaled = attend_rows(
+            query, new_key, new_value, key_cache, value_cache, lengths, residual, norm_gain
+        )
+        mlp = mlp_line(scaled, w_gate, w_up, w_down)
     else:
-        inv = lax.rsqrt(lax.psum(squares, "mix") / D + eps)
-        mlp = mlp_sums((x * inv * gain).astype(jnp.bfloat16), w_gate, w_up, w_down)
+        x = residual.astype(f32) + attend(query, new_key, new_value, key_cache, value_cache, lengths)
+        inv = lax.rsqrt(lax.psum(jnp.sum(x * x, axis=1, keepdims=True), "mix") / D + eps)
+        normed = (x * inv * norm_gain.astype(f32)).astype(bf16)
+        mlp = mlp_sums(normed, w_gate, w_up, w_down)
     slots = jnp.arange(x.shape[0], dtype=jnp.int32)
     live = slots < counts[0]
     return jnp.where(live[:, None], x + mlp, jnp.zeros_like(x)).astype(jnp.bfloat16)

time: 199 us -> 181 us (0.910)
  matrix products: 13.4 us -> 0 us
  Pallas kernels: 59.6 us -> 72.1 us
  starting transfers between devices: 67.5 us -> 60.6 us
  local copies, waits for them, and re-layouts: 5.39 us -> 1.47 us
  other arithmetic: 4.95 us -> 1.25 us
  waiting for transfers between devices: 45.7 us -> 43.7 us
    dot_general x2 -> x0, matrix products: 13.4 us -> none  [the longest x1 7.78 us: attend(): jnp.einsum('chd,cphd->chp', q_heads, k_all, preferred_element_type=jnp.fl...]
    pallas_call x19 -> x20, Pallas kernels: 2.17 us -> 14.7 us  [the longest x1 12.4 us: attend_rows(): pl.pallas_call(kernel, grid=(rows // block,), in_specs=[SMEM, flat, flat,...]
    ppermute x22 -> x21, starting transfers between devices: 59.1 us -> 54.2 us  [outward(): return lax.ppermute(a, 'mix', OUTWARD)]
    ppermute x7 -> x5, waiting for transfers between devices: 12.4 us -> 16.8 us  [swap(): return lax.ppermute(a, axis, SWAP)]
    ppermute x22 -> x21, waiting for transfers between devices: 30.5 us -> 26.8 us  [outward(): return lax.ppermute(a, 'mix', OUTWARD)]
    ppermute x1 -> x0, starting transfers between devices: 2.59 us -> none  [per_device(): squares = squares + lax.ppermute(squares, 'mix', ACROSS)]
    unnamed x12 -> x4, local copies, waits for them, and re-layouts: 2.9 us -> 0.7 us
    ppermute x7 -> x5, starting transfers between devices: 4.03 us -> 4.72 us  [swap(): return lax.ppermute(a, axis, SWAP)]
  transfers between devices with their start and end apart: 47 -> 43, of which waited for: 17 -> 15; matrix products, arithmetic and copies ran while one was open for 0% -> 0% of each run, Pallas kernels for 28% -> 30%
where the time goes in v2:
time: 181 us; the launch traced here: 180 us
  Pallas kernels  72.1 us (40%)
  starting transfers between devices  60.6 us (33%)
  waiting for transfers between devices  43.7 us (24%)
    ppermute x21, starting transfers between devices, outward(): return lax.ppermute(a, 'mix', OUTWARD)  54.2 us
    pallas_call x11, Pallas kernels, partial_products(): pl.pallas_call(kernel, grid=(steps,), in_specs=[pl.BlockSpec((count, dept...  33.8 us
    ppermute x21, waiting for transfers between devices, outward(): return lax.ppermute(a, 'mix', OUTWARD)  26.8 us
    pallas_call x6, Pallas kernels, down_product(): pl.pallas_call(kernel, grid=(columns // step,), in_specs=specs, out_specs...  23.6 us
    ppermute x5, waiting for transfers between devices, swap(): return lax.ppermute(a, axis, SWAP)  16.8 us
    pallas_call x1, Pallas kernels, attend_rows(): pl.pallas_call(kernel, grid=(rows // block,), in_specs=[SMEM, flat, flat,...  12.4 us
    ppermute x5, starting transfers between devices, swap(): return lax.ppermute(a, axis, SWAP)  4.72 us
  transfers between devices with their start and end apart: 43, of which 15 were waited for; matrix products, arithmetic and copies ran while one was open for 0% of the time, Pallas kernels for 30%

profile of v2, /device:TPU:0, one launch (start us, length us, event | category | flops | bytes accessed | tf_op | source)
XLA Modules:
  0.0 180.3 jit_solution(15427265544804065227)
XLA Ops:
  1.3 12.4 %attend_rows.1 = (f32[64,2048]{1,0:T(8,128)S(1)}, bf16[64,2176]{1,0:T(8,128)(2,1)S(1)}) custom-call(s32[64]{0:T(128)S(1)} %copy-done, bf16[64,2048]{1,0:T(8,128)(2,1)} %q_ref.1, bf16[64,2048]{1,0:T(8,128)(2,1)} %nk_ref.1, bf16[64,2048]{1,0:T(8,128)(2,1)} %nv_ref.1, bf16[64,32,2048]{2,1,0:T(8,128)(2,1)} %k_ref.1, bf16[64,32,2048]{2,1,0:T(8,128)(2,1)} %v_ref.1, ...), custom_call_target="tpu_custom_call" | custom-call | flops 4294967296 | bytes 16777216 | tf_op jit(solution)/shard_map/attend_rows/pallas_call | solution.py:149
  14.3 2.6 %collective-permute-start = (bf16[64,2176]{1,0:T(8,128)(2,1)S(1)}, bf16[64,2176]{1,0:T(8,128)(2,1)S(1)}, u32[]{:S(2)}, u32[]{:S(2)}) collective-permute-start(bf16[64,2176]{1,0:T(8,128)(2,1)S(1)} %get-tuple-element.65), channel_id=1, source_target_pairs={{0,2},{2,0},{1,3},{3,1},{4,6},{6,4},{5,7},{7,5},{8,10},{10,8},{9,1... | collective-permute-start | bytes 835592 | tf_op jit(solution)/shard_map/ppermute | solution.py:77
  17.0 7.2 %collective-permute-done = bf16[64,2176]{1,0:T(8,128)(2,1)S(1)} collective-permute-done((bf16[64,2176]{1,0:T(8,128)(2,1)S(1)}, bf16[64,2176]{1,0:T(8,128)(2,1)S(1)}, u32[]{:S(2)}, u32[]{:S(2)}) %collective-permute-start) | collective-permute-done | bytes 278560 | tf_op jit(solution)/shard_map/ppermute | solution.py:77
  25.9 3.1 %partial_products.11 = (bf16[128,1152]{1,0:T(8,128)(2,1)S(1)}, bf16[128,1152]{1,0:T(8,128)(2,1)S(1)}) custom-call(bf16[256,2176]{1,0:T(8,128)(2,1)S(1)} %pad_maximum_fusion.rows_ref.rest_0_, bf16[5472,2048]{1,0:T(8,128)(2,1)} %bitcast.5, bf16[5472,2048]{1,0:T(8,128)(2,1)} %bitcast.16, bf16[256,2176]{1,0:T(8,128)(2,1)S(1)} %pad_maximum_fusion.rows_ref.rest_0_), custom_call_target="tpu_custom_call" | custom-call | flops 4294967296 | bytes 19922944 | tf_op jit(solution)/shard_map/partial_products/pallas_call | solution.py:215
  29.0 1.9 %collective-permute-start.3 = (bf16[128,1152]{1,0:T(8,128)(2,1)S(1)}, bf16[128,1152]{1,0:T(8,128)(2,1)S(1)}, u32[]{:S(2)}, u32[]{:S(2)}) collective-permute-start(bf16[128,1152]{1,0:T(8,128)(2,1)S(1)} %get-tuple-element.66.rest_0_.refs_3_), channel_id=1, source_target_pairs={{0,4},{4,0},{8,12},{12,8},{1,5},{5,1},{9,13},{13,9},{2,6},{6,2},{1... | collective-permute-start | bytes 884744 | tf_op jit(solution)/shard_map/ppermute | solution.py:69
  30.9 3.1 %partial_products.12 = (bf16[128,1024]{1,0:T(8,128)(2,1)S(1)}, bf16[128,1024]{1,0:T(8,128)(2,1)S(1)}) custom-call(bf16[256,2176]{1,0:T(8,128)(2,1)S(1)} %pad_maximum_fusion.rows_ref.rest_0_, bf16[5472,2048]{1,0:T(8,128)(2,1)} %bitcast.6, bf16[5472,2048]{1,0:T(8,128)(2,1)} %bitcast.17, bf16[128,1152]{1,0:T(8,128)(2,1)S(1)} %get-tuple-element.66.rest_0_.refs_3_), custom_call_target="tpu_custom_call" | custom-call | flops 4294967296 | bytes 19922944 | tf_op jit(solution)/shard_map/partial_products/pallas_call | solution.py:215
  34.3 3.1 %partial_products.13 = (bf16[128,1024]{1,0:T(8,128)(2,1)S(1)}, bf16[128,1024]{1,0:T(8,128)(2,1)S(1)}) custom-call(bf16[256,2176]{1,0:T(8,128)(2,1)S(1)} %pad_maximum_fusion.rows_ref.rest_0_, bf16[5472,2048]{1,0:T(8,128)(2,1)} %bitcast.7, bf16[5472,2048]{1,0:T(8,128)(2,1)} %bitcast.18, bf16[128,1024]{1,0:T(8,128)(2,1)S(1)} %get-tuple-element.67.rest_0_.refs_3_), custom_call_target="tpu_custom_call" | custom-call | flops 4294967296 | bytes 19922944 | tf_op jit(solution)/shard_map/partial_products/pallas_call | solution.py:215
  37.4 1.6 collective-permute-done.3.refs_1_
  39.0 2.0 %collective-permute-start.4 = (bf16[128,1024]{1,0:T(8,128)(2,1)S(1)}, bf16[128,1024]{1,0:T(8,128)(2,1)S(1)}, u32[]{:S(2)}, u32[]{:S(2)}) collective-permute-start(bf16[128,1024]{1,0:T(8,128)(2,1)S(1)} %get-tuple-element.69.rest_0_), channel_id=1, source_target_pairs={{0,4},{4,0},{8,12},{12,8},{1,5},{5,1},{9,13},{13,9},{2,6},{6,2},{1... | collective-permute-start | bytes 786440 | tf_op jit(solution)/shard_map/ppermute | solution.py:69
  41.0 3.1 %partial_products.14 = (bf16[128,1024]{1,0:T(8,128)(2,1)S(1)}, bf16[128,1024]{1,0:T(8,128)(2,1)S(1)}) custom-call(bf16[256,2176]{1,0:T(8,128)(2,1)S(1)} %pad_maximum_fusion.rows_ref.rest_0_, bf16[5472,2048]{1,0:T(8,128)(2,1)} %bitcast.8, bf16[5472,2048]{1,0:T(8,128)(2,1)} %bitcast.19, bf16[128,1024]{1,0:T(8,128)(2,1)S(1)} %get-tuple-element.69.rest_0_), custom_call_target="tpu_custom_call" | custom-call | flops 4294967296 | bytes 19922944 | tf_op jit(solution)/shard_map/partial_products/pallas_call | solution.py:215
  44.7 3.4 %collective-permute-start.9 = (bf16[128,1024]{1,0:T(8,128)(2,1)S(1)}, bf16[128,1024]{1,0:T(8,128)(2,1)S(1)}, u32[]{:S(2)}, u32[]{:S(2)}) collective-permute-start(bf16[128,1024]{1,0:T(8,128)(2,1)S(1)} %get-tuple-element.72.rest_0_), channel_id=1, source_target_pairs={{0,4},{4,0},{8,12},{12,8},{1,5},{5,1},{9,13},{13,9},{2,6},{6,2},{1... | collective-permute-start | bytes 786440 | tf_op jit(solution)/shard_map/ppermute | solution.py:69
  48.1 3.1 %partial_products.15 = (bf16[128,1024]{1,0:T(8,128)(2,1)S(1)}, bf16[128,1024]{1,0:T(8,128)(2,1)S(1)}) custom-call(bf16[256,2176]{1,0:T(8,128)(2,1)S(1)} %pad_maximum_fusion.rows_ref.rest_0_, bf16[5472,2048]{1,0:T(8,128)(2,1)} %bitcast.9, bf16[5472,2048]{1,0:T(8,128)(2,1)} %bitcast.20, bf16[128,1024]{1,0:T(8,128)(2,1)S(1)} %get-tuple-element.72.rest_0_), custom_call_target="tpu_custom_call" | custom-call | flops 4294967296 | bytes 19922944 | tf_op jit(solution)/shard_map/partial_products/pallas_call | solution.py:215
  51.3 2.6 %collective-permute-start.7 = (bf16[128,1152]{1,0:T(8,128)(2,1)S(1)}, bf16[128,1152]{1,0:T(8,128)(2,1)S(1)}, u32[]{:S(2)}, u32[]{:S(2)}) collective-permute-start(bf16[128,1152]{1,0:T(8,128)(2,1)S(1)} %get-tuple-element.75.rest_0_), channel_id=1, source_target_pairs={{0,4},{4,0},{8,12},{12,8},{1,5},{5,1},{9,13},{13,9},{2,6},{6,2},{1... | collective-permute-start | bytes 884744 | tf_op jit(solution)/shard_map/ppermute | solution.py:69
  53.9 3.1 %partial_products.16 = (bf16[128,1024]{1,0:T(8,128)(2,1)S(1)}, bf16[128,1024]{1,0:T(8,128)(2,1)S(1)}) custom-call(bf16[256,2176]{1,0:T(8,128)(2,1)S(1)} %pad_maximum_fusion.rows_ref.rest_0_, bf16[5472,2048]{1,0:T(8,128)(2,1)} %bitcast.10, bf16[5472,2048]{1,0:T(8,128)(2,1)} %bitcast.21, bf16[128,1152]{1,0:T(8,128)(2,1)S(1)} %get-tuple-element.75.rest_0_), custom_call_target="tpu_custom_call" | custom-call | flops 4294967296 | bytes 19922944 | tf_op jit(solution)/shard_map/partial_products/pallas_call | solution.py:215
  57.1 2.3 %collective-permute-start.13 = (bf16[128,1024]{1,0:T(8,128)(2,1)S(1)}, bf16[128,1024]{1,0:T(8,128)(2,1)S(1)}, u32[]{:S(2)}, u32[]{:S(2)}) collective-permute-start(bf16[128,1024]{1,0:T(8,128)(2,1)S(1)} %get-tuple-element.80.rest_0_), channel_id=1, source_target_pairs={{0,4},{4,0},{8,12},{12,8},{1,5},{5,1},{9,13},{13,9},{2,6},{6,2},{1... | collective-permute-start | bytes 786440 | tf_op jit(solution)/shard_map/ppermute | solution.py:69
  59.4 3.1 %partial_products.17 = (bf16[128,1024]{1,0:T(8,128)(2,1)S(1)}, bf16[128,1024]{1,0:T(8,128)(2,1)S(1)}) custom-call(bf16[256,2176]{1,0:T(8,128)(2,1)S(1)} %pad_maximum_fusion.rows_ref.rest_0_, bf16[5472,2048]{1,0:T(8,128)(2,1)} %bitcast.11, bf16[5472,2048]{1,0:T(8,128)(2,1)} %bitcast.22, bf16[128,1024]{1,0:T(8,128)(2,1)S(1)} %get-tuple-element.80.rest_0_), custom_call_target="tpu_custom_call" | custom-call | flops 4294967296 | bytes 19922944 | tf_op jit(solution)/shard_map/partial_products/pallas_call | solution.py:215
  62.8 2.9 %collective-permute-start.11 = (bf16[128,1536]{1,0:T(8,128)(2,1)S(1)}, bf16[128,1536]{1,0:T(8,128)(2,1)S(1)}, u32[]{:S(2)}, u32[]{:S(2)}) collective-permute-start(bf16[128,1536]{1,0:T(8,128)(2,1)S(1)} %get-tuple-element.83.rest_0_.refs_0_), channel_id=1, source_target_pairs={{0,4},{4,0},{8,12},{12,8},{1,5},{5,1},{9,13},{13,9},{2,6},{6,2},{1... | collective-permute-start | bytes 1179656 | tf_op jit(solution)/shard_map/ppermute | solution.py:69
  65.7 3.1 %partial_products.18 = (bf16[128,1024]{1,0:T(8,128)(2,1)S(1)}, bf16[128,1024]{1,0:T(8,128)(2,1)S(1)}) custom-call(bf16[256,2176]{1,0:T(8,128)(2,1)S(1)} %pad_maximum_fusion.rows_ref.rest_0_, bf16[5472,2048]{1,0:T(8,128)(2,1)} %bitcast.12, bf16[5472,2048]{1,0:T(8,128)(2,1)} %bitcast.23, bf16[128,1536]{1,0:T(8,128)(2,1)S(1)} %get-tuple-element.83.rest_0_.refs_0_), custom_call_target="tpu_custom_call" | custom-call | flops 4294967296 | bytes 19922944 | tf_op jit(solution)/shard_map/partial_products/pallas_call | solution.py:215
  69.1 2.2 %collective-permute-start.17 = (bf16[128,1536]{1,0:T(8,128)(2,1)S(1)}, bf16[128,1536]{1,0:T(8,128)(2,1)S(1)}, u32[]{:S(2)}, u32[]{:S(2)}) collective-permute-start(bf16[128,1536]{1,0:T(8,128)(2,1)S(1)} %get-tuple-element.89.rest_0_.refs_4_), channel_id=1, source_target_pairs={{0,4},{4,0},{8,12},{12,8},{1,5},{5,1},{9,13},{13,9},{2,6},{6,2},{1... | collective-permute-start | bytes 1179656 | tf_op jit(solution)/shard_map/ppermute | solution.py:69
  71.3 3.1 %partial_products.19 = (bf16[128,1024]{1,0:T(8,128)(2,1)S(1)}, bf16[128,1024]{1,0:T(8,128)(2,1)S(1)}) custom-call(bf16[256,2176]{1,0:T(8,128)(2,1)S(1)} %pad_maximum_fusion.rows_ref.rest_0_, bf16[5472,2048]{1,0:T(8,128)(2,1)} %bitcast.13, bf16[5472,2048]{1,0:T(8,128)(2,1)} %bitcast.24, bf16[128,1536]{1,0:T(8,128)(2,1)S(1)} %get-tuple-element.89.rest_0_.refs_4_), custom_call_target="tpu_custom_call" | custom-call | flops 4294967296 | bytes 19922944 | tf_op jit(solution)/shard_map/partial_products/pallas_call | solution.py:215
  74.4 1.6 collective-permute-done.11.refs_1_
  76.5 3.5 %collective-permute-start.15 = (bf16[128,1536]{1,0:T(8,128)(2,1)S(1)}, bf16[128,1536]{1,0:T(8,128)(2,1)S(1)}, u32[]{:S(2)}, u32[]{:S(2)}) collective-permute-start(bf16[128,1536]{1,0:T(8,128)(2,1)S(1)} %get-tuple-element.92.rest_0_.refs_0_), channel_id=1, source_target_pairs={{0,4},{4,0},{8,12},{12,8},{1,5},{5,1},{9,13},{13,9},{2,6},{6,2},{1... | collective-permute-start | bytes 1179656 | tf_op jit(solution)/shard_map/ppermute | solution.py:69
  80.0 3.1 %partial_products.20 = (bf16[128,1024]{1,0:T(8,128)(2,1)S(1)}, bf16[128,1024]{1,0:T(8,128)(2,1)S(1)}) custom-call(bf16[256,2176]{1,0:T(8,128)(2,1)S(1)} %pad_maximum_fusion.rows_ref.rest_0_, bf16[5472,2048]{1,0:T(8,128)(2,1)} %bitcast.14, bf16[5472,2048]{1,0:T(8,128)(2,1)} %bitcast.25, bf16[128,1536]{1,0:T(8,128)(2,1)S(1)} %get-tuple-element.92.rest_0_.refs_0_), custom_call_target="tpu_custom_call" | custom-call | flops 4294967296 | bytes 19922944 | tf_op jit(solution)/shard_map/partial_products/pallas_call | solution.py:215
  84.7 3.5 %collective-permute-start.21 = (bf16[128,1536]{1,0:T(8,128)(2,1)S(1)}, bf16[128,1536]{1,0:T(8,128)(2,1)S(1)}, u32[]{:S(2)}, u32[]{:S(2)}) collective-permute-start(bf16[128,1536]{1,0:T(8,128)(2,1)S(1)} %get-tuple-element.97.rest_0_.refs_4_), channel_id=1, source_target_pairs={{0,4},{4,0},{8,12},{12,8},{1,5},{5,1},{9,13},{13,9},{2,6},{6,2},{1... | collective-permute-start | bytes 1179656 | tf_op jit(solution)/shard_map/ppermute | solution.py:69
  88.2 3.1 %partial_products.21 = (bf16[128,1024]{1,0:T(8,128)(2,1)S(1)}, bf16[128,1024]{1,0:T(8,128)(2,1)S(1)}) custom-call(bf16[256,2176]{1,0:T(8,128)(2,1)S(1)} %pad_maximum_fusion.rows_ref.rest_0_, bf16[5472,2048]{1,0:T(8,128)(2,1)} %bitcast.15, bf16[5472,2048]{1,0:T(8,128)(2,1)} %bitcast.26, bf16[128,1536]{1,0:T(8,128)(2,1)S(1)} %get-tuple-element.97.rest_0_.refs_4_), custom_call_target="tpu_custom_call" | custom-call | flops 4294967296 | bytes 19922944 | tf_op jit(solution)/shard_map/partial_products/pallas_call | solution.py:215
  91.3 1.6 collective-permute-done.15.refs_1_
  93.2 3.5 %collective-permute-start.19 = (bf16[128,1536]{1,0:T(8,128)(2,1)S(1)}, bf16[128,1536]{1,0:T(8,128)(2,1)S(1)}, u32[]{:S(2)}, u32[]{:S(2)}) collective-permute-start(bf16[128,1536]{1,0:T(8,128)(2,1)S(1)} %get-tuple-element.100.refs_7_.refs_0_), channel_id=1, source_target_pairs={{0,4},{4,0},{8,12},{12,8},{1,5},{5,1},{9,13},{13,9},{2,6},{6,2},{1... | collective-permute-start | bytes 1179656 | tf_op jit(solution)/shard_map/ppermute | solution.py:69
  96.6 4.7 %collective-permute-done.21.refs_1_.refs_5_ = bf16[128,1536]{1,0:T(8,128)(2,1)S(1)} collective-permute-done((bf16[128,1536]{1,0:T(8,128)(2,1)S(1)}, bf16[128,1536]{1,0:T(8,128)(2,1)S(1)}, u32[]{:S(2)}, u32[]{:S(2)}) %collective-permute-start.21) | collective-permute-done | bytes 393248 | tf_op jit(solution)/shard_map/ppermute | solution.py:69
  101.6 3.5 %collective-permute-start.25 = (bf16[128,1536]{1,0:T(8,128)(2,1)S(1)}, bf16[128,1536]{1,0:T(8,128)(2,1)S(1)}, u32[]{:S(2)}, u32[]{:S(2)}) collective-permute-start(bf16[128,1536]{1,0:T(8,128)(2,1)S(1)} %get-tuple-element.105.refs_7_.refs_4_), channel_id=1, source_target_pairs={{0,4},{4,0},{8,12},{12,8},{1,5},{5,1},{9,13},{13,9},{2,6},{6,2},{1... | collective-permute-start | bytes 1179656 | tf_op jit(solution)/shard_map/ppermute | solution.py:69
  105.1 4.7 %collective-permute-done.19.refs_1_.refs_3_ = bf16[128,1536]{1,0:T(8,128)(2,1)S(1)} collective-permute-done((bf16[128,1536]{1,0:T(8,128)(2,1)S(1)}, bf16[128,1536]{1,0:T(8,128)(2,1)S(1)}, u32[]{:S(2)}, u32[]{:S(2)}) %collective-permute-start.19) | collective-permute-done | bytes 393248 | tf_op jit(solution)/shard_map/ppermute | solution.py:69
  110.0 3.5 %collective-permute-start.23 = (bf16[128,1536]{1,0:T(8,128)(2,1)S(1)}, bf16[128,1536]{1,0:T(8,128)(2,1)S(1)}, u32[]{:S(2)}, u32[]{:S(2)}) collective-permute-start(bf16[128,1536]{1,0:T(8,128)(2,1)S(1)} %get-tuple-element.106.refs_6_.refs_0_), channel_id=1, source_target_pairs={{0,4},{4,0},{8,12},{12,8},{1,5},{5,1},{9,13},{13,9},{2,6},{6,2},{1... | collective-permute-start | bytes 1179656 | tf_op jit(solution)/shard_map/ppermute | solution.py:69
  113.5 4.7 %collective-permute-done.25.refs_7_.refs_1_.refs_5_ = bf16[128,1536]{1,0:T(8,128)(2,1)S(1)} collective-permute-done((bf16[128,1536]{1,0:T(8,128)(2,1)S(1)}, bf16[128,1536]{1,0:T(8,128)(2,1)S(1)}, u32[]{:S(2)}, u32[]{:S(2)}) %collective-permute-start.25) | collective-permute-done | bytes 393248 | tf_op jit(solution)/shard_map/ppermute | solution.py:69
  118.4 3.4 %collective-permute-start.29 = (bf16[128,1536]{1,0:T(8,128)(2,1)S(1)}, bf16[128,1536]{1,0:T(8,128)(2,1)S(1)}, u32[]{:S(2)}, u32[]{:S(2)}) collective-permute-start(bf16[128,1536]{1,0:T(8,128)(2,1)S(1)} %get-tuple-element.113.refs_4_), channel_id=1, source_target_pairs={{0,4},{4,0},{8,12},{12,8},{1,5},{5,1},{9,13},{13,9},{2,6},{6,2},{1... | collective-permute-start | bytes 1179656 | tf_op jit(solution)/shard_map/ppermute | solution.py:69
  121.9 4.1 %down_product.6.refs_6_.refs_9_ = f32[256,2048]{1,0:T(8,128)S(1)} custom-call(s32[1]{0:T(128)} %bitcast.1.refs_0_.outer_ref, bf16[128,1536]{1,0:T(8,128)(2,1)S(1)} %get-tuple-element.83.rest_0_.refs_0_, bf16[128,1536]{1,0:T(8,128)(2,1)S(1)} %collective-permute-done.11.refs_1_, bf16[128,1536]{1,0:T(8,128)(2,1)S(1)} %collective-permute-done.16.refs_2_, ...), custom_call_target="tpu_custom_call" | custom-call | flops 4294967296 | bytes 33554432 | tf_op jit(solution)/shard_map/down_product/pallas_call | solution.py:384
  126.9 3.4 %collective-permute-start.26 = (bf16[128,1536]{1,0:T(8,128)(2,1)S(1)}, bf16[128,1536]{1,0:T(8,128)(2,1)S(1)}, u32[]{:S(2)}, u32[]{:S(2)}) collective-permute-start(bf16[128,1536]{1,0:T(8,128)(2,1)S(1)} %get-tuple-element.109.refs_5_.refs_0_), channel_id=1, source_target_pairs={{0,4},{4,0},{8,12},{12,8},{1,5},{5,1},{9,13},{13,9},{2,6},{6,2},{1... | collective-permute-start | bytes 1179656 | tf_op jit(solution)/shard_map/ppermute | solution.py:69
  130.3 4.7 %collective-permute-done.29.refs_7_.refs_1_.refs_5_ = bf16[128,1536]{1,0:T(8,128)(2,1)S(1)} collective-permute-done((bf16[128,1536]{1,0:T(8,128)(2,1)S(1)}, bf16[128,1536]{1,0:T(8,128)(2,1)S(1)}, u32[]{:S(2)}, u32[]{:S(2)}) %collective-permute-start.29) | collective-permute-done | bytes 393248 | tf_op jit(solution)/shard_map/ppermute | solution.py:69
  135.3 3.4 %collective-permute-start.33 = (bf16[128,512]{1,0:T(8,128)(2,1)S(1)}, bf16[128,512]{1,0:T(8,128)(2,1)S(1)}, u32[]{:S(2)}, u32[]{:S(2)}) collective-permute-start(bf16[128,512]{1,0:T(8,128)(2,1)S(1)} %get-tuple-element.117.refs_4_), channel_id=1, source_target_pairs={{0,4},{4,0},{8,12},{12,8},{1,5},{5,1},{9,13},{13,9},{2,6},{6,2},{1... | collective-permute-start | bytes 393224 | tf_op jit(solution)/shard_map/ppermute | solution.py:69
  138.7 4.1 %down_product.7.refs_5_.refs_9_ = f32[256,2048]{1,0:T(8,128)S(1)} custom-call(s32[1]{0:T(128)} %bitcast.1.refs_0_.outer_ref, bf16[128,1536]{1,0:T(8,128)(2,1)S(1)} %get-tuple-element.92.rest_0_.refs_0_, bf16[128,1536]{1,0:T(8,128)(2,1)S(1)} %collective-permute-done.15.refs_1_, bf16[128,1536]{1,0:T(8,128)(2,1)S(1)} %collective-permute-done.20.refs_2_, ...), custom_call_target="tpu_custom_call" | custom-call | flops 4294967296 | bytes 33554432 | tf_op jit(solution)/shard_map/down_product/pallas_call | solution.py:384
  143.7 3.4 %collective-permute-start.30 = (bf16[128,512]{1,0:T(8,128)(2,1)S(1)}, bf16[128,512]{1,0:T(8,128)(2,1)S(1)}, u32[]{:S(2)}, u32[]{:S(2)}) collective-permute-start(bf16[128,512]{1,0:T(8,128)(2,1)S(1)} %get-tuple-element.114.refs_3_.refs_0_), channel_id=1, source_target_pairs={{0,4},{4,0},{8,12},{12,8},{1,5},{5,1},{9,13},{13,9},{2,6},{6,2},{1... | collective-permute-start | bytes 393224 | tf_op jit(solution)/shard_map/ppermute | solution.py:69
  147.5 4.1 %down_product.8.refs_3_.refs_9_ = f32[256,2048]{1,0:T(8,128)S(1)} custom-call(s32[1]{0:T(128)} %bitcast.1.refs_0_.outer_ref, bf16[128,1536]{1,0:T(8,128)(2,1)S(1)} %get-tuple-element.100.refs_7_.refs_0_, bf16[128,1536]{1,0:T(8,128)(2,1)S(1)} %collective-permute-done.19.refs_1_.refs_3_, bf16[128,1536]{1,0:T(8,128)(2,1)S(1)} %collective-permute-done.24.refs_2_, ...), custom_call_target="tpu_custom_call" | custom-call | flops 4294967296 | bytes 33554432 | tf_op jit(solution)/shard_map/down_product/pallas_call | solution.py:384
  152.2 3.1 %collective-permute-start.35 = (bf16[128,512]{1,0:T(8,128)(2,1)S(1)}, bf16[128,512]{1,0:T(8,128)(2,1)S(1)}, u32[]{:S(2)}, u32[]{:S(2)}) collective-permute-start(bf16[128,512]{1,0:T(8,128)(2,1)S(1)} %get-tuple-element.119.refs_3_), channel_id=1, source_target_pairs={{0,4},{4,0},{8,12},{12,8},{1,5},{5,1},{9,13},{13,9},{2,6},{6,2},{1... | collective-permute-start | bytes 393224 | tf_op jit(solution)/shard_map/ppermute | solution.py:69
  155.5 4.1 %down_product.9.refs_3_.refs_9_ = f32[256,2048]{1,0:T(8,128)S(1)} custom-call(s32[1]{0:T(128)} %bitcast.1.refs_0_.outer_ref, bf16[128,1536]{1,0:T(8,128)(2,1)S(1)} %get-tuple-element.106.refs_6_.refs_0_, bf16[128,1536]{1,0:T(8,128)(2,1)S(1)} %collective-permute-done.23.refs_1_.refs_3_, bf16[128,512]{1,0:T(8,128)(2,1)S(1)} %collective-permute-done.27.refs_2_, ...), custom_call_target="tpu_custom_call" | custom-call | flops 4294967296 | bytes 33554432 | tf_op jit(solution)/shard_map/down_product/pallas_call | solution.py:384
  159.6 2.0 %collective-permute-start.38 = (bf16[128,512]{1,0:T(8,128)(2,1)S(1)}, bf16[128,512]{1,0:T(8,128)(2,1)S(1)}, u32[]{:S(2)}, u32[]{:S(2)}) collective-permute-start(bf16[128,512]{1,0:T(8,128)(2,1)S(1)} %hop.36), channel_id=1, source_target_pairs={{0,4},{4,0},{8,12},{12,8},{1,5},{5,1},{9,13},{13,9},{2,6},{6,2},{1... | collective-permute-start | bytes 393224 | tf_op jit(solution)/shard_map/ppermute | solution.py:69
  161.6 4.1 %down_product.10.refs_5_ = f32[256,2048]{1,0:T(8,128)S(1)} custom-call(s32[1]{0:T(128)} %bitcast.1.refs_0_.outer_ref, bf16[128,1536]{1,0:T(8,128)(2,1)S(1)} %get-tuple-element.109.refs_5_.refs_0_, bf16[128,1536]{1,0:T(8,128)(2,1)S(1)} %collective-permute-done.26.refs_1_.refs_3_, bf16[128,512]{1,0:T(8,128)(2,1)S(1)} %collective-permute-done.31.refs_2_, ...), custom_call_target="tpu_custom_call" | custom-call | flops 4294967296 | bytes 33554432 | tf_op jit(solution)/shard_map/down_product/pallas_call | solution.py:384
  165.8 3.0 %down_product.11 = bf16[256,2048]{1,0:T(8,128)(2,1)S(1)} custom-call(s32[1]{0:T(128)} %bitcast.1.refs_0_.outer_ref, bf16[128,512]{1,0:T(8,128)(2,1)S(1)} %get-tuple-element.114.refs_3_.refs_0_, bf16[128,512]{1,0:T(8,128)(2,1)S(1)} %collective-permute-done.30.refs_1_.refs_3_, bf16[128,512]{1,0:T(8,128)(2,1)S(1)} %collective-permute-done.34.refs_2_, ...), custom_call_target="tpu_custom_call" | custom-call | flops 2147483648 | bytes 25165824 | tf_op jit(solution)/shard_map/down_product/pallas_call | solution.py:384
  169.0 1.9 %collective-permute-done.41 = bf16[128,2048]{1,0:T(8,128)(2,1)S(1)} collective-permute-done((bf16[128,2048]{1,0:T(8,128)(2,1)S(1)}, bf16[128,2048]{1,0:T(8,128)(2,1)S(1)}, u32[]{:S(2)}, u32[]{:S(2)}) %collective-permute-start.41) | collective-permute-done | bytes 524320 | tf_op jit(solution)/shard_map/ppermute | solution.py:77
  171.1 1.6 collective-permute-start.42
  173.3 6.2 %collective-permute-done.42 = bf16[64,2048]{1,0:T(8,128)(2,1)S(1)} collective-permute-done((bf16[64,2048]{1,0:T(8,128)(2,1)S(1)}, bf16[64,2048]{1,0:T(8,128)(2,1)S(1)}, u32[]{:S(2)}, u32[]{:S(2)}) %collective-permute-start.42) | collective-permute-done | bytes 262176 | tf_op jit(solution)/shard_map/ppermute | solution.py:77
  (89 shorter events, 12.7 us)
Async XLA Ops:
  0.7 0.7 copy-start
  13.8 3.1 %collective-permute-start.1 = (bf16[64,2176]{1,0:T(8,128)(2,1)S(1)}, bf16[64,2176]{1,0:T(8,128)(2,1)S(1)}, u32[]{:S(2)}, u32[]{:S(2)}) collective-permute-start(bf16[64,2176]{1,0:T(8,128)(2,1)S(1)} %get-tuple-element.65), channel_id=1, source_target_pairs={{0,1},{1,0},{2,3},{3,2},{4,5},{5,4},{6,7},{7,6},{8,9},{9,8},{10,11... | collective-permute-start | bytes 835592 | tf_op jit(solution)/shard_map/ppermute | solution.py:77
  14.3 9.8 %collective-permute-start = (bf16[64,2176]{1,0:T(8,128)(2,1)S(1)}, bf16[64,2176]{1,0:T(8,128)(2,1)S(1)}, u32[]{:S(2)}, u32[]{:S(2)}) collective-permute-start(bf16[64,2176]{1,0:T(8,128)(2,1)S(1)} %get-tuple-element.65), channel_id=1, source_target_pairs={{0,2},{2,0},{1,3},{3,1},{4,6},{6,4},{5,7},{7,5},{8,10},{10,8},{9,1... | collective-permute-start | bytes 835592 | tf_op jit(solution)/shard_map/ppermute | solution.py:77
  24.1 1.6 collective-permute-start.2
  29.0 9.9 %collective-permute-start.3 = (bf16[128,1152]{1,0:T(8,128)(2,1)S(1)}, bf16[128,1152]{1,0:T(8,128)(2,1)S(1)}, u32[]{:S(2)}, u32[]{:S(2)}) collective-permute-start(bf16[128,1152]{1,0:T(8,128)(2,1)S(1)} %get-tuple-element.66.rest_0_.refs_3_), channel_id=1, source_target_pairs={{0,4},{4,0},{8,12},{12,8},{1,5},{5,1},{9,13},{13,9},{2,6},{6,2},{1... | collective-permute-start | bytes 884744 | tf_op jit(solution)/shard_map/ppermute | solution.py:69
  34.0 10.5 %collective-permute-start.6 = (bf16[128,1024]{1,0:T(8,128)(2,1)S(1)}, bf16[128,1024]{1,0:T(8,128)(2,1)S(1)}, u32[]{:S(2)}, u32[]{:S(2)}) collective-permute-start(bf16[128,1024]{1,0:T(8,128)(2,1)S(1)} %get-tuple-element.67.rest_0_.refs_3_), channel_id=1, source_target_pairs={{0,4},{4,0},{8,12},{12,8},{1,5},{5,1},{9,13},{13,9},{2,6},{6,2},{1... | collective-permute-start | bytes 786440 | tf_op jit(solution)/shard_map/ppermute | solution.py:69
  39.0 12.2 %collective-permute-start.4 = (bf16[128,1024]{1,0:T(8,128)(2,1)S(1)}, bf16[128,1024]{1,0:T(8,128)(2,1)S(1)}, u32[]{:S(2)}, u32[]{:S(2)}) collective-permute-start(bf16[128,1024]{1,0:T(8,128)(2,1)S(1)} %get-tuple-element.69.rest_0_), channel_id=1, source_target_pairs={{0,4},{4,0},{8,12},{12,8},{1,5},{5,1},{9,13},{13,9},{2,6},{6,2},{1... | collective-permute-start | bytes 786440 | tf_op jit(solution)/shard_map/ppermute | solution.py:69
  41.0 10.2 %collective-permute-start.5 = (bf16[128,1152]{1,0:T(8,128)(2,1)S(1)}, bf16[128,1152]{1,0:T(8,128)(2,1)S(1)}, u32[]{:S(2)}, u32[]{:S(2)}) collective-permute-start(bf16[128,1152]{1,0:T(8,128)(2,1)S(1)} %get-tuple-element.70), channel_id=1, source_target_pairs={{0,1},{1,0},{4,8},{8,4},{5,9},{9,5},{12,13},{13,12},{2,3},{3,2},{6... | collective-permute-start | bytes 884744 | tf_op jit(solution)/shard_map/ppermute | solution.py:73
  44.6 12.4 %collective-permute-start.10 = (bf16[128,1024]{1,0:T(8,128)(2,1)S(1)}, bf16[128,1024]{1,0:T(8,128)(2,1)S(1)}, u32[]{:S(2)}, u32[]{:S(2)}) collective-permute-start(bf16[128,1024]{1,0:T(8,128)(2,1)S(1)} %get-tuple-element.77), channel_id=1, source_target_pairs={{0,1},{1,0},{4,8},{8,4},{5,9},{9,5},{12,13},{13,12},{2,3},{3,2},{6... | collective-permute-start | bytes 786440 | tf_op jit(solution)/shard_map/ppermute | solution.py:73
  44.7 12.3 %collective-permute-start.9 = (bf16[128,1024]{1,0:T(8,128)(2,1)S(1)}, bf16[128,1024]{1,0:T(8,128)(2,1)S(1)}, u32[]{:S(2)}, u32[]{:S(2)}) collective-permute-start(bf16[128,1024]{1,0:T(8,128)(2,1)S(1)} %get-tuple-element.72.rest_0_), channel_id=1, source_target_pairs={{0,4},{4,0},{8,12},{12,8},{1,5},{5,1},{9,13},{13,9},{2,6},{6,2},{1... | collective-permute-start | bytes 786440 | tf_op jit(solution)/shard_map/ppermute | solution.py:69
  51.3 11.2 %collective-permute-start.8 = (bf16[128,1024]{1,0:T(8,128)(2,1)S(1)}, bf16[128,1024]{1,0:T(8,128)(2,1)S(1)}, u32[]{:S(2)}, u32[]{:S(2)}) collective-permute-start(bf16[128,1024]{1,0:T(8,128)(2,1)S(1)} %get-tuple-element.76), channel_id=1, source_target_pairs={{0,1},{1,0},{4,8},{8,4},{5,9},{9,5},{12,13},{13,12},{2,3},{3,2},{6... | collective-permute-start | bytes 786440 | tf_op jit(solution)/shard_map/ppermute | solution.py:73
  51.3 11.2 %collective-permute-start.7 = (bf16[128,1152]{1,0:T(8,128)(2,1)S(1)}, bf16[128,1152]{1,0:T(8,128)(2,1)S(1)}, u32[]{:S(2)}, u32[]{:S(2)}) collective-permute-start(bf16[128,1152]{1,0:T(8,128)(2,1)S(1)} %get-tuple-element.75.rest_0_), channel_id=1, source_target_pairs={{0,4},{4,0},{8,12},{12,8},{1,5},{5,1},{9,13},{13,9},{2,6},{6,2},{1... | collective-permute-start | bytes 884744 | tf_op jit(solution)/shard_map/ppermute | solution.py:69
  57.1 11.7 %collective-permute-start.14 = (bf16[128,1024]{1,0:T(8,128)(2,1)S(1)}, bf16[128,1024]{1,0:T(8,128)(2,1)S(1)}, u32[]{:S(2)}, u32[]{:S(2)}) collective-permute-start(bf16[128,1024]{1,0:T(8,128)(2,1)S(1)} %get-tuple-element.85), channel_id=1, source_target_pairs={{0,1},{1,0},{4,8},{8,4},{5,9},{9,5},{12,13},{13,12},{2,3},{3,2},{6... | collective-permute-start | bytes 786440 | tf_op jit(solution)/shard_map/ppermute | solution.py:73
  57.1 11.7 %collective-permute-start.13 = (bf16[128,1024]{1,0:T(8,128)(2,1)S(1)}, bf16[128,1024]{1,0:T(8,128)(2,1)S(1)}, u32[]{:S(2)}, u32[]{:S(2)}) collective-permute-start(bf16[128,1024]{1,0:T(8,128)(2,1)S(1)} %get-tuple-element.80.rest_0_), channel_id=1, source_target_pairs={{0,4},{4,0},{8,12},{12,8},{1,5},{5,1},{9,13},{13,9},{2,6},{6,2},{1... | collective-permute-start | bytes 786440 | tf_op jit(solution)/shard_map/ppermute | solution.py:69
  62.7 11.7 %collective-permute-start.12 = (bf16[128,1024]{1,0:T(8,128)(2,1)S(1)}, bf16[128,1024]{1,0:T(8,128)(2,1)S(1)}, u32[]{:S(2)}, u32[]{:S(2)}) collective-permute-start(bf16[128,1024]{1,0:T(8,128)(2,1)S(1)} %get-tuple-element.84), channel_id=1, source_target_pairs={{0,1},{1,0},{4,8},{8,4},{5,9},{9,5},{12,13},{13,12},{2,3},{3,2},{6... | collective-permute-start | bytes 786440 | tf_op jit(solution)/shard_map/ppermute | solution.py:73
  62.8 13.2 %collective-permute-start.11 = (bf16[128,1536]{1,0:T(8,128)(2,1)S(1)}, bf16[128,1536]{1,0:T(8,128)(2,1)S(1)}, u32[]{:S(2)}, u32[]{:S(2)}) collective-permute-start(bf16[128,1536]{1,0:T(8,128)(2,1)S(1)} %get-tuple-element.83.rest_0_.refs_0_), channel_id=1, source_target_pairs={{0,4},{4,0},{8,12},{12,8},{1,5},{5,1},{9,13},{13,9},{2,6},{6,2},{1... | collective-permute-start | bytes 1179656 | tf_op jit(solution)/shard_map/ppermute | solution.py:69
  69.0 14.0 %collective-permute-start.18 = (bf16[128,1024]{1,0:T(8,128)(2,1)S(1)}, bf16[128,1024]{1,0:T(8,128)(2,1)S(1)}, u32[]{:S(2)}, u32[]{:S(2)}) collective-permute-start(bf16[128,1024]{1,0:T(8,128)(2,1)S(1)} %get-tuple-element.94), channel_id=1, source_target_pairs={{0,1},{1,0},{4,8},{8,4},{5,9},{9,5},{12,13},{13,12},{2,3},{3,2},{6... | collective-permute-start | bytes 786440 | tf_op jit(solution)/shard_map/ppermute | solution.py:73
  69.1 15.4 %collective-permute-start.17 = (bf16[128,1536]{1,0:T(8,128)(2,1)S(1)}, bf16[128,1536]{1,0:T(8,128)(2,1)S(1)}, u32[]{:S(2)}, u32[]{:S(2)}) collective-permute-start(bf16[128,1536]{1,0:T(8,128)(2,1)S(1)} %get-tuple-element.89.rest_0_.refs_4_), channel_id=1, source_target_pairs={{0,4},{4,0},{8,12},{12,8},{1,5},{5,1},{9,13},{13,9},{2,6},{6,2},{1... | collective-permute-start | bytes 1179656 | tf_op jit(solution)/shard_map/ppermute | solution.py:69
  76.4 14.9 %collective-permute-start.16 = (bf16[128,1536]{1,0:T(8,128)(2,1)S(1)}, bf16[128,1536]{1,0:T(8,128)(2,1)S(1)}, u32[]{:S(2)}, u32[]{:S(2)}) collective-permute-start(bf16[128,1536]{1,0:T(8,128)(2,1)S(1)} %get-tuple-element.93), channel_id=1, source_target_pairs={{0,1},{1,0},{4,8},{8,4},{5,9},{9,5},{12,13},{13,12},{2,3},{3,2},{6... | collective-permute-start | bytes 1179656 | tf_op jit(solution)/shard_map/ppermute | solution.py:73
  76.5 16.4 %collective-permute-start.15 = (bf16[128,1536]{1,0:T(8,128)(2,1)S(1)}, bf16[128,1536]{1,0:T(8,128)(2,1)S(1)}, u32[]{:S(2)}, u32[]{:S(2)}) collective-permute-start(bf16[128,1536]{1,0:T(8,128)(2,1)S(1)} %get-tuple-element.92.rest_0_.refs_0_), channel_id=1, source_target_pairs={{0,4},{4,0},{8,12},{12,8},{1,5},{5,1},{9,13},{13,9},{2,6},{6,2},{1... | collective-permute-start | bytes 1179656 | tf_op jit(solution)/shard_map/ppermute | solution.py:69
  84.7 12.0 %collective-permute-start.22 = (bf16[128,1536]{1,0:T(8,128)(2,1)S(1)}, bf16[128,1536]{1,0:T(8,128)(2,1)S(1)}, u32[]{:S(2)}, u32[]{:S(2)}) collective-permute-start(bf16[128,1536]{1,0:T(8,128)(2,1)S(1)} %get-tuple-element.103), channel_id=1, source_target_pairs={{0,1},{1,0},{4,8},{8,4},{5,9},{9,5},{12,13},{13,12},{2,3},{3,2},{6... | collective-permute-start | bytes 1179656 | tf_op jit(solution)/shard_map/ppermute | solution.py:73
  84.7 16.6 %collective-permute-start.21 = (bf16[128,1536]{1,0:T(8,128)(2,1)S(1)}, bf16[128,1536]{1,0:T(8,128)(2,1)S(1)}, u32[]{:S(2)}, u32[]{:S(2)}) collective-permute-start(bf16[128,1536]{1,0:T(8,128)(2,1)S(1)} %get-tuple-element.97.rest_0_.refs_4_), channel_id=1, source_target_pairs={{0,4},{4,0},{8,12},{12,8},{1,5},{5,1},{9,13},{13,9},{2,6},{6,2},{1... | collective-permute-start | bytes 1179656 | tf_op jit(solution)/shard_map/ppermute | solution.py:69
  93.1 12.0 %collective-permute-start.20 = (bf16[128,1536]{1,0:T(8,128)(2,1)S(1)}, bf16[128,1536]{1,0:T(8,128)(2,1)S(1)}, u32[]{:S(2)}, u32[]{:S(2)}) collective-permute-start(bf16[128,1536]{1,0:T(8,128)(2,1)S(1)} %get-tuple-element.101), channel_id=1, source_target_pairs={{0,1},{1,0},{4,8},{8,4},{5,9},{9,5},{12,13},{13,12},{2,3},{3,2},{6... | collective-permute-start | bytes 1179656 | tf_op jit(solution)/shard_map/ppermute | solution.py:73
  93.2 16.6 %collective-permute-start.19 = (bf16[128,1536]{1,0:T(8,128)(2,1)S(1)}, bf16[128,1536]{1,0:T(8,128)(2,1)S(1)}, u32[]{:S(2)}, u32[]{:S(2)}) collective-permute-start(bf16[128,1536]{1,0:T(8,128)(2,1)S(1)} %get-tuple-element.100.refs_7_.refs_0_), channel_id=1, source_target_pairs={{0,4},{4,0},{8,12},{12,8},{1,5},{5,1},{9,13},{13,9},{2,6},{6,2},{1... | collective-permute-start | bytes 1179656 | tf_op jit(solution)/shard_map/ppermute | solution.py:69
  101.5 12.0 %collective-permute-start.28 = (bf16[128,1536]{1,0:T(8,128)(2,1)S(1)}, bf16[128,1536]{1,0:T(8,128)(2,1)S(1)}, u32[]{:S(2)}, u32[]{:S(2)}) collective-permute-start(bf16[128,1536]{1,0:T(8,128)(2,1)S(1)} %get-tuple-element.111), channel_id=1, source_target_pairs={{0,1},{1,0},{4,8},{8,4},{5,9},{9,5},{12,13},{13,12},{2,3},{3,2},{6... | collective-permute-start | bytes 1179656 | tf_op jit(solution)/shard_map/ppermute | solution.py:73
  101.6 16.6 %collective-permute-start.25 = (bf16[128,1536]{1,0:T(8,128)(2,1)S(1)}, bf16[128,1536]{1,0:T(8,128)(2,1)S(1)}, u32[]{:S(2)}, u32[]{:S(2)}) collective-permute-start(bf16[128,1536]{1,0:T(8,128)(2,1)S(1)} %get-tuple-element.105.refs_7_.refs_4_), channel_id=1, source_target_pairs={{0,4},{4,0},{8,12},{12,8},{1,5},{5,1},{9,13},{13,9},{2,6},{6,2},{1... | collective-permute-start | bytes 1179656 | tf_op jit(solution)/shard_map/ppermute | solution.py:69
  109.9 16.0 %collective-permute-start.24 = (bf16[128,1536]{1,0:T(8,128)(2,1)S(1)}, bf16[128,1536]{1,0:T(8,128)(2,1)S(1)}, u32[]{:S(2)}, u32[]{:S(2)}) collective-permute-start(bf16[128,1536]{1,0:T(8,128)(2,1)S(1)} %get-tuple-element.107), channel_id=1, source_target_pairs={{0,1},{1,0},{4,8},{8,4},{5,9},{9,5},{12,13},{13,12},{2,3},{3,2},{6... | collective-permute-start | bytes 1179656 | tf_op jit(solution)/shard_map/ppermute | solution.py:73
  110.0 16.6 %collective-permute-start.23 = (bf16[128,1536]{1,0:T(8,128)(2,1)S(1)}, bf16[128,1536]{1,0:T(8,128)(2,1)S(1)}, u32[]{:S(2)}, u32[]{:S(2)}) collective-permute-start(bf16[128,1536]{1,0:T(8,128)(2,1)S(1)} %get-tuple-element.106.refs_6_.refs_0_), channel_id=1, source_target_pairs={{0,4},{4,0},{8,12},{12,8},{1,5},{5,1},{9,13},{13,9},{2,6},{6,2},{1... | collective-permute-start | bytes 1179656 | tf_op jit(solution)/shard_map/ppermute | solution.py:69
  118.3 11.9 %collective-permute-start.32 = (bf16[128,512]{1,0:T(8,128)(2,1)S(1)}, bf16[128,512]{1,0:T(8,128)(2,1)S(1)}, u32[]{:S(2)}, u32[]{:S(2)}) collective-permute-start(bf16[128,512]{1,0:T(8,128)(2,1)S(1)} %get-tuple-element.116), channel_id=1, source_target_pairs={{0,1},{1,0},{4,8},{8,4},{5,9},{9,5},{12,13},{13,12},{2,3},{3,2},{6... | collective-permute-start | bytes 393224 | tf_op jit(solution)/shard_map/ppermute | solution.py:73
  118.4 16.6 %collective-permute-start.29 = (bf16[128,1536]{1,0:T(8,128)(2,1)S(1)}, bf16[128,1536]{1,0:T(8,128)(2,1)S(1)}, u32[]{:S(2)}, u32[]{:S(2)}) collective-permute-start(bf16[128,1536]{1,0:T(8,128)(2,1)S(1)} %get-tuple-element.113.refs_4_), channel_id=1, source_target_pairs={{0,4},{4,0},{8,12},{12,8},{1,5},{5,1},{9,13},{13,9},{2,6},{6,2},{1... | collective-permute-start | bytes 1179656 | tf_op jit(solution)/shard_map/ppermute | solution.py:69
  126.8 16.0 %collective-permute-start.27 = (bf16[128,512]{1,0:T(8,128)(2,1)S(1)}, bf16[128,512]{1,0:T(8,128)(2,1)S(1)}, u32[]{:S(2)}, u32[]{:S(2)}) collective-permute-start(bf16[128,512]{1,0:T(8,128)(2,1)S(1)} %get-tuple-element.110), channel_id=1, source_target_pairs={{0,1},{1,0},{4,8},{8,4},{5,9},{9,5},{12,13},{13,12},{2,3},{3,2},{6... | collective-permute-start | bytes 393224 | tf_op jit(solution)/shard_map/ppermute | solution.py:73
  126.9 16.6 %collective-permute-start.26 = (bf16[128,1536]{1,0:T(8,128)(2,1)S(1)}, bf16[128,1536]{1,0:T(8,128)(2,1)S(1)}, u32[]{:S(2)}, u32[]{:S(2)}) collective-permute-start(bf16[128,1536]{1,0:T(8,128)(2,1)S(1)} %get-tuple-element.109.refs_5_.refs_0_), channel_id=1, source_target_pairs={{0,4},{4,0},{8,12},{12,8},{1,5},{5,1},{9,13},{13,9},{2,6},{6,2},{1... | collective-permute-start | bytes 1179656 | tf_op jit(solution)/shard_map/ppermute | solution.py:69
  135.2 11.9 %collective-permute-start.36 = (bf16[128,512]{1,0:T(8,128)(2,1)S(1)}, bf16[128,512]{1,0:T(8,128)(2,1)S(1)}, u32[]{:S(2)}, u32[]{:S(2)}) collective-permute-start(bf16[128,512]{1,0:T(8,128)(2,1)S(1)} %get-tuple-element.120), channel_id=1, source_target_pairs={{0,1},{1,0},{4,8},{8,4},{5,9},{9,5},{12,13},{13,12},{2,3},{3,2},{6... | collective-permute-start | bytes 393224 | tf_op jit(solution)/shard_map/ppermute | solution.py:73
  135.3 11.8 %collective-permute-start.33 = (bf16[128,512]{1,0:T(8,128)(2,1)S(1)}, bf16[128,512]{1,0:T(8,128)(2,1)S(1)}, u32[]{:S(2)}, u32[]{:S(2)}) collective-permute-start(bf16[128,512]{1,0:T(8,128)(2,1)S(1)} %get-tuple-element.117.refs_4_), channel_id=1, source_target_pairs={{0,4},{4,0},{8,12},{12,8},{1,5},{5,1},{9,13},{13,9},{2,6},{6,2},{1... | collective-permute-start | bytes 393224 | tf_op jit(solution)/shard_map/ppermute | solution.py:69
  143.6 8.0 %collective-permute-start.31 = (bf16[128,512]{1,0:T(8,128)(2,1)S(1)}, bf16[128,512]{1,0:T(8,128)(2,1)S(1)}, u32[]{:S(2)}, u32[]{:S(2)}) collective-permute-start(bf16[128,512]{1,0:T(8,128)(2,1)S(1)} %get-tuple-element.115), channel_id=1, source_target_pairs={{0,1},{1,0},{4,8},{8,4},{5,9},{9,5},{12,13},{13,12},{2,3},{3,2},{6... | collective-permute-start | bytes 393224 | tf_op jit(solution)/shard_map/ppermute | solution.py:73
  143.7 7.9 %collective-permute-start.30 = (bf16[128,512]{1,0:T(8,128)(2,1)S(1)}, bf16[128,512]{1,0:T(8,128)(2,1)S(1)}, u32[]{:S(2)}, u32[]{:S(2)}) collective-permute-start(bf16[128,512]{1,0:T(8,128)(2,1)S(1)} %get-tuple-element.114.refs_3_.refs_0_), channel_id=1, source_target_pairs={{0,4},{4,0},{8,12},{12,8},{1,5},{5,1},{9,13},{13,9},{2,6},{6,2},{1... | collective-permute-start | bytes 393224 | tf_op jit(solution)/shard_map/ppermute | solution.py:69
  147.1 8.3 %collective-permute-start.37 = (bf16[128,512]{1,0:T(8,128)(2,1)S(1)}, bf16[128,512]{1,0:T(8,128)(2,1)S(1)}, u32[]{:S(2)}, u32[]{:S(2)}) collective-permute-start(bf16[128,512]{1,0:T(8,128)(2,1)S(1)} %get-tuple-element.121), channel_id=1, source_target_pairs={{0,4},{4,0},{8,12},{12,8},{1,5},{5,1},{9,13},{13,9},{2,6},{6,2},{1... | collective-permute-start | bytes 393224 | tf_op jit(solution)/shard_map/ppermute | solution.py:69
  147.5 7.9 %collective-permute-start.39 = (bf16[128,512]{1,0:T(8,128)(2,1)S(1)}, bf16[128,512]{1,0:T(8,128)(2,1)S(1)}, u32[]{:S(2)}, u32[]{:S(2)}) collective-permute-start(bf16[128,512]{1,0:T(8,128)(2,1)S(1)} %get-tuple-element.122), channel_id=1, source_target_pairs={{0,1},{1,0},{4,8},{8,4},{5,9},{9,5},{12,13},{13,12},{2,3},{3,2},{6... | collective-permute-start | bytes 393224 | tf_op jit(solution)/shard_map/ppermute | solution.py:73
  151.7 7.9 %collective-permute-start.34 = (bf16[128,512]{1,0:T(8,128)(2,1)S(1)}, bf16[128,512]{1,0:T(8,128)(2,1)S(1)}, u32[]{:S(2)}, u32[]{:S(2)}) collective-permute-start(bf16[128,512]{1,0:T(8,128)(2,1)S(1)} %get-tuple-element.118), channel_id=1, source_target_pairs={{0,1},{1,0},{4,8},{8,4},{5,9},{9,5},{12,13},{13,12},{2,3},{3,2},{6... | collective-permute-start | bytes 393224 | tf_op jit(solution)/shard_map/ppermute | solution.py:73
  152.2 7.4 %collective-permute-start.35 = (bf16[128,512]{1,0:T(8,128)(2,1)S(1)}, bf16[128,512]{1,0:T(8,128)(2,1)S(1)}, u32[]{:S(2)}, u32[]{:S(2)}) collective-permute-start(bf16[128,512]{1,0:T(8,128)(2,1)S(1)} %get-tuple-element.119.refs_3_), channel_id=1, source_target_pairs={{0,4},{4,0},{8,12},{12,8},{1,5},{5,1},{9,13},{13,9},{2,6},{6,2},{1... | collective-permute-start | bytes 393224 | tf_op jit(solution)/shard_map/ppermute | solution.py:69
  155.4 6.3 %collective-permute-start.40 = (bf16[128,512]{1,0:T(8,128)(2,1)S(1)}, bf16[128,512]{1,0:T(8,128)(2,1)S(1)}, u32[]{:S(2)}, u32[]{:S(2)}) collective-permute-start(bf16[128,512]{1,0:T(8,128)(2,1)S(1)} %hop.37), channel_id=1, source_target_pairs={{0,4},{4,0},{8,12},{12,8},{1,5},{5,1},{9,13},{13,9},{2,6},{6,2},{1... | collective-permute-start | bytes 393224 | tf_op jit(solution)/shard_map/ppermute | solution.py:69
  159.6 6.1 %collective-permute-start.38 = (bf16[128,512]{1,0:T(8,128)(2,1)S(1)}, bf16[128,512]{1,0:T(8,128)(2,1)S(1)}, u32[]{:S(2)}, u32[]{:S(2)}) collective-permute-start(bf16[128,512]{1,0:T(8,128)(2,1)S(1)} %hop.36), channel_id=1, source_target_pairs={{0,4},{4,0},{8,12},{12,8},{1,5},{5,1},{9,13},{13,9},{2,6},{6,2},{1... | collective-permute-start | bytes 393224 | tf_op jit(solution)/shard_map/ppermute | solution.py:69
  168.9 2.0 %collective-permute-start.41 = (bf16[128,2048]{1,0:T(8,128)(2,1)S(1)}, bf16[128,2048]{1,0:T(8,128)(2,1)S(1)}, u32[]{:S(2)}, u32[]{:S(2)}) collective-permute-start(bf16[128,2048]{1,0:T(8,128)(2,1)S(1)} %broadcast_select_fusion.2), channel_id=1, source_target_pairs={{0,1},{1,0},{2,3},{3,2},{4,5},{5,4},{6,7},{7,6},{8,9},{9,8},{10,11... | collective-permute-start | bytes 1572872 | tf_op jit(solution)/shard_map/ppermute | solution.py:77
  171.1 8.4 %collective-permute-start.42 = (bf16[64,2048]{1,0:T(8,128)(2,1)S(1)}, bf16[64,2048]{1,0:T(8,128)(2,1)S(1)}, u32[]{:S(2)}, u32[]{:S(2)}) collective-permute-start(bf16[64,2048]{1,0:T(8,128)(2,1)S(1)} %slice.33), channel_id=1, source_target_pairs={{0,2},{2,0},{1,3},{3,1},{4,6},{6,4},{5,7},{7,5},{8,10},{10,8},{9,1... | collective-permute-start | bytes 786440 | tf_op jit(solution)/shard_map/ppermute | solution.py:77

commit v3 on v2

--- a/solution.py
+++ b/solution.py
@@ -332,66 +332,36 @@
     return to_e, to_m, outs[0] if outs else inv_in
 
 
-def down_product(outer, total, first, chunks, w_down, final):
-    units, columns = w_down.shape
-    half = chunks[0][0][0].shape[0]
-    n = len(chunks)
-    valid = min(n * WIDTH, units - first * WIDTH)
-    step = 512
-
-    def kernel(outer_ref, *refs):
-        hids = refs[: 4 * n]
-        w_ref = refs[4 * n]
-        total_ref = refs[4 * n + 1] if total is not None else None
-        out_ref, hid = refs[-2:]
-
-        @pl.when(pl.program_id(0) == 0)
+def hidden_rows(outer, buffers, after):
+    half = buffers[0][0].shape[0]
+
+    def kernel(outer_ref, sent, got, from_m, late, *rest):
+        hid = rest[-1]
+
+        @pl.when(outer_ref[0] != 0)
         def _():
-            for c in range(n):
-                sent, got, from_m, late = hids[4 * c : 4 * c + 4]
-                at = pl.ds(c * WIDTH, WIDTH)
-
-                @pl.when(outer_ref[0] != 0)
-                def _():
-                    hid[:half, at] = late[...]
-                    hid[half:, at] = sent[...]
-
-                @pl.when(outer_ref[0] == 0)
-                def _():
-                    hid[:half, at] = from_m[...]
-                    hid[half:, at] = got[...]
-
-        weight = w_ref[...]
-        if valid < n * WIDTH:
-            unit = lax.broadcasted_iota(jnp.int32, weight.shape, 0)
-            weight = jnp.where(unit < valid, weight.astype(f32), 0.0).astype(bf16)
-        term = jnp.dot(hid[...], weight, preferred_element_type=f32)
-        if total_ref is not None:
-            term = term + total_ref[...]
-        out_ref[...] = term.astype(out_ref.dtype)
-
-    operands, specs = [outer], [SMEM]
-    for chunk in chunks:
-        for buffer, offset in chunk:
-            operands.append(buffer)
-            specs.append(pl.BlockSpec((half, WIDTH), functools.partial(lambda at, i: (0, at), offset // WIDTH)))
-    operands.append(w_down)
-    block = first // n
-    specs.append(pl.BlockSpec((n * WIDTH, step), lambda i: (block, i)))
-    if total is not None:
-        operands.append(total)
-        specs.append(pl.BlockSpec((2 * half, step), lambda i: (0, i)))
+            hid[:half] = late[:, buffers[3][1] : buffers[3][1] + WIDTH]
+            hid[half:] = sent[:, buffers[0][1] : buffers[0][1] + WIDTH]
+
+        @pl.when(outer_ref[0] == 0)
+        def _():
+            hid[:half] = from_m[:, buffers[2][1] : buffers[2][1] + WIDTH]
+            hid[half:] = got[:, buffers[1][1] : buffers[1][1] + WIDTH]
+
     return pl.pallas_call(
         kernel,
-        grid=(columns // step,),
-        in_specs=specs,
-        out_specs=pl.BlockSpec((2 * half, step), lambda i: (0, i)),
-        out_shape=jax.ShapeDtypeStruct((2 * half, columns), bf16 if final else f32),
-        scratch_shapes=[pltpu.VMEM((2 * half, n * WIDTH), bf16)],
+        in_specs=[SMEM] + [VMEM] * 4 + [ANY] * len(after),
+        out_specs=VMEM,
+        out_shape=jax.ShapeDtypeStruct((2 * half, WIDTH), bf16),
         compiler_params=pltpu.CompilerParams(vmem_limit_bytes=24 << 20),
-        cost_estimate=cost(4 * half * n * WIDTH * columns, 2 * n * WIDTH * columns + 16 * half * columns),
-        name="down_product",
-    )(*operands)
+        name="hidden_rows",
+    )(outer, *[buffer for buffer, _ in buffers], *after)
+
+
+def down_product(total, k, hidden, w_down):
+    first, last = k * WIDTH, min((k + 1) * WIDTH, w_down.shape[0])
+    term = jnp.dot(hidden[:, : last - first], w_down[first:last], preferred_element_type=f32)
+    return term if total is None else total + term
 
 
 def mlp_line(scaled, w_gate, w_up, w_down):
@@ -409,7 +379,6 @@
 
     gate_rows = pltpu.with_memory_space_constraint(w_gate.T, pltpu.HBM)
     up_rows = pltpu.with_memory_space_constraint(w_up.T, pltpu.HBM)
-    w_down = pltpu.with_memory_space_constraint(w_down, pltpu.HBM)
     chunks = -(-gate_rows.shape[0] // WIDTH)
     counts = (-(-chunks // 2), chunks // 2)
     part_out, part_in = ({}, {}), ({}, {})
@@ -457,11 +426,12 @@
                 send(s, t + 1, to_e, to_m)
                 after = [(to_e or to_m)[0]]
             after = products(2 * t + s + 3, after)
-            first = 2 * (t - 5)
-            if first >= 0 and ((s == 1 and first + 1 < chunks) or (s == 0 and first + 1 == chunks)):
-                pair = [hidden_of(k) for k in range(first, min(first + 2, chunks))]
-                total = down_product(outer, total, first, pair, w_down, first + 2 >= chunks)
-                after = [total]
+            if 0 <= t - 5 < count:
+                k = 2 * (t - 5) + s
+                hidden = hidden_rows(outer, hidden_of(k), after + ([] if total is None else [total]))
+                total = down_product(total, k, hidden, w_down)
+                after = [hidden]
+    total = total.astype(bf16)
     far, near = total[:half], total[half:]
     for_here = jnp.where(left, far, near)
     for_there = jnp.where(left, near, far)

time: 181 us -> 178 us (0.983)
  Pallas kernels: 72.1 us -> 49.1 us
  waiting for transfers between devices: 43.7 us -> 64.1 us
  starting transfers between devices: 60.6 us -> 52.3 us
  matrix products: 0 us -> 7.86 us
    pallas_call x6 -> x11, Pallas kernels: 23.6 us -> 0.24 us  [hidden_rows(): pl.pallas_call(kernel, in_specs=[SMEM] + [VMEM] * 4 + [ANY] * len(after),...]
    ppermute x21, waiting for transfers between devices: 26.8 us -> 47.8 us  [outward(): return lax.ppermute(a, 'mix', OUTWARD)]
    dot_general x0 -> x11, matrix products: none -> 7.86 us  [down_product(): jnp.dot(hidden[:, :last - first], w_down[first:last], preferred_element_t...]
    ppermute x21, starting transfers between devices: 54.2 us -> 47 us  [outward(): return lax.ppermute(a, 'mix', OUTWARD)]
  transfers between devices with their start and end apart: 43 -> 43, of which waited for: 15 -> 19; matrix products, arithmetic and copies ran while one was open for 0% -> 4% of each run, Pallas kernels for 30% -> 17%
where the time goes in v3:
time: 178 us
  waiting for transfers between devices  64.1 us (36%)
  starting transfers between devices  52.3 us (29%)
  Pallas kernels  49.1 us (28%)
  matrix products  7.86 us (4%)
    ppermute x21, waiting for transfers between devices, outward(): return lax.ppermute(a, 'mix', OUTWARD)  47.8 us
    ppermute x21, starting transfers between devices, outward(): return lax.ppermute(a, 'mix', OUTWARD)  47 us
    pallas_call x11, Pallas kernels, partial_products(): pl.pallas_call(kernel, grid=(steps,), in_specs=[pl.BlockSpec((count, dept...  34.2 us
    ppermute x5, waiting for transfers between devices, swap(): return lax.ppermute(a, axis, SWAP)  16.2 us
    pallas_call x1, Pallas kernels, attend_rows(): pl.pallas_call(kernel, grid=(rows // block,), in_specs=[SMEM, flat, flat,...  12.4 us
    dot_general x11, matrix products, down_product(): jnp.dot(hidden[:, :last - first], w_down[first:last], preferred_element_t...  7.86 us
    ppermute x5, starting transfers between devices, swap(): return lax.ppermute(a, axis, SWAP)  4.66 us
  transfers between devices with their start and end apart: 43, of which 19 were waited for; matrix products, arithmetic and copies ran while one was open for 4% of the time, Pallas kernels for 17%

profile of v3, /device:TPU:0, one launch (start us, length us, event | category | flops | bytes accessed | tf_op | source)
XLA Modules:
  0.0 177.5 jit_solution(5281234246887164119)
XLA Ops:
  1.3 12.4 %attend_rows.1 = (f32[64,2048]{1,0:T(8,128)S(1)}, bf16[64,2176]{1,0:T(8,128)(2,1)S(1)}) custom-call(s32[64]{0:T(128)S(1)} %copy-done, bf16[64,2048]{1,0:T(8,128)(2,1)} %q_ref.1, bf16[64,2048]{1,0:T(8,128)(2,1)} %nk_ref.1, bf16[64,2048]{1,0:T(8,128)(2,1)} %nv_ref.1, bf16[64,32,2048]{2,1,0:T(8,128)(2,1)} %k_ref.1, bf16[64,32,2048]{2,1,0:T(8,128)(2,1)} %v_ref.1, ...), custom_call_target="tpu_custom_call" | custom-call | flops 4294967296 | bytes 16777216 | tf_op jit(solution)/shard_map/attend_rows/pallas_call | solution.py:149
  13.8 3.0 %collective-permute-start = (bf16[64,2176]{1,0:T(8,128)(2,1)S(1)}, bf16[64,2176]{1,0:T(8,128)(2,1)S(1)}, u32[]{:S(2)}, u32[]{:S(2)}) collective-permute-start(bf16[64,2176]{1,0:T(8,128)(2,1)S(1)} %get-tuple-element.65), channel_id=1, source_target_pairs={{0,2},{2,0},{1,3},{3,1},{4,6},{6,4},{5,7},{7,5},{8,10},{10,8},{9,1... | collective-permute-start | bytes 835592 | tf_op jit(solution)/shard_map/ppermute | solution.py:77
  16.8 6.6 %collective-permute-done = bf16[64,2176]{1,0:T(8,128)(2,1)S(1)} collective-permute-done((bf16[64,2176]{1,0:T(8,128)(2,1)S(1)}, bf16[64,2176]{1,0:T(8,128)(2,1)S(1)}, u32[]{:S(2)}, u32[]{:S(2)}) %collective-permute-start) | collective-permute-done | bytes 278560 | tf_op jit(solution)/shard_map/ppermute | solution.py:77
  23.5 1.5 collective-permute-done.2
  25.2 3.1 %partial_products.11 = (bf16[128,1152]{1,0:T(8,128)(2,1)S(1)}, bf16[128,1152]{1,0:T(8,128)(2,1)S(1)}) custom-call(bf16[256,2176]{1,0:T(8,128)(2,1)S(1)} %pad_maximum_fusion.rows_ref.rest_0_, bf16[5472,2048]{1,0:T(8,128)(2,1)} %bitcast.15, bf16[5472,2048]{1,0:T(8,128)(2,1)} %bitcast.26, bf16[256,2176]{1,0:T(8,128)(2,1)S(1)} %pad_maximum_fusion.rows_ref.rest_0_), custom_call_target="tpu_custom_call" | custom-call | flops 4294967296 | bytes 19922944 | tf_op jit(solution)/shard_map/partial_products/pallas_call | solution.py:215
  28.4 3.1 %partial_products.12 = (bf16[128,1024]{1,0:T(8,128)(2,1)S(1)}, bf16[128,1024]{1,0:T(8,128)(2,1)S(1)}) custom-call(bf16[256,2176]{1,0:T(8,128)(2,1)S(1)} %pad_maximum_fusion.rows_ref.rest_0_, bf16[5472,2048]{1,0:T(8,128)(2,1)} %bitcast.16, bf16[5472,2048]{1,0:T(8,128)(2,1)} %bitcast.27, bf16[128,1152]{1,0:T(8,128)(2,1)S(1)} %get-tuple-element.66.rest_0_.refs_3_), custom_call_target="tpu_custom_call" | custom-call | flops 4294967296 | bytes 19922944 | tf_op jit(solution)/shard_map/partial_products/pallas_call | solution.py:215
  31.5 1.9 %collective-permute-start.3 = (bf16[128,1152]{1,0:T(8,128)(2,1)S(1)}, bf16[128,1152]{1,0:T(8,128)(2,1)S(1)}, u32[]{:S(2)}, u32[]{:S(2)}) collective-permute-start(bf16[128,1152]{1,0:T(8,128)(2,1)S(1)} %get-tuple-element.66.rest_0_.refs_3_), channel_id=1, source_target_pairs={{0,4},{4,0},{8,12},{12,8},{1,5},{5,1},{9,13},{13,9},{2,6},{6,2},{1... | collective-permute-start | bytes 884744 | tf_op jit(solution)/shard_map/ppermute | solution.py:69
  33.6 3.1 %partial_products.13 = (bf16[128,1024]{1,0:T(8,128)(2,1)S(1)}, bf16[128,1024]{1,0:T(8,128)(2,1)S(1)}) custom-call(bf16[256,2176]{1,0:T(8,128)(2,1)S(1)} %pad_maximum_fusion.rows_ref.rest_0_, bf16[5472,2048]{1,0:T(8,128)(2,1)} %bitcast.17, bf16[5472,2048]{1,0:T(8,128)(2,1)} %bitcast.28, bf16[128,1024]{1,0:T(8,128)(2,1)S(1)} %get-tuple-element.67.rest_0_.refs_3_), custom_call_target="tpu_custom_call" | custom-call | flops 4294967296 | bytes 19922944 | tf_op jit(solution)/shard_map/partial_products/pallas_call | solution.py:215
  36.6 4.7 %collective-permute-done.3.refs_1_ = bf16[128,1152]{1,0:T(8,128)(2,1)S(1)} collective-permute-done((bf16[128,1152]{1,0:T(8,128)(2,1)S(1)}, bf16[128,1152]{1,0:T(8,128)(2,1)S(1)}, u32[]{:S(2)}, u32[]{:S(2)}) %collective-permute-start.3) | collective-permute-done | bytes 294944 | tf_op jit(solution)/shard_map/ppermute | solution.py:69
  41.5 3.5 %collective-permute-start.4 = (bf16[128,1024]{1,0:T(8,128)(2,1)S(1)}, bf16[128,1024]{1,0:T(8,128)(2,1)S(1)}, u32[]{:S(2)}, u32[]{:S(2)}) collective-permute-start(bf16[128,1024]{1,0:T(8,128)(2,1)S(1)} %get-tuple-element.69.rest_0_), channel_id=1, source_target_pairs={{0,4},{4,0},{8,12},{12,8},{1,5},{5,1},{9,13},{13,9},{2,6},{6,2},{1... | collective-permute-start | bytes 786440 | tf_op jit(solution)/shard_map/ppermute | solution.py:69
  45.0 3.1 %partial_products.14 = (bf16[128,1024]{1,0:T(8,128)(2,1)S(1)}, bf16[128,1024]{1,0:T(8,128)(2,1)S(1)}) custom-call(bf16[256,2176]{1,0:T(8,128)(2,1)S(1)} %pad_maximum_fusion.rows_ref.rest_0_, bf16[5472,2048]{1,0:T(8,128)(2,1)} %bitcast.18, bf16[5472,2048]{1,0:T(8,128)(2,1)} %bitcast.29, bf16[128,1024]{1,0:T(8,128)(2,1)S(1)} %get-tuple-element.69.rest_0_), custom_call_target="tpu_custom_call" | custom-call | flops 4294967296 | bytes 19922944 | tf_op jit(solution)/shard_map/partial_products/pallas_call | solution.py:215
  48.2 2.3 %collective-permute-start.9 = (bf16[128,1024]{1,0:T(8,128)(2,1)S(1)}, bf16[128,1024]{1,0:T(8,128)(2,1)S(1)}, u32[]{:S(2)}, u32[]{:S(2)}) collective-permute-start(bf16[128,1024]{1,0:T(8,128)(2,1)S(1)} %get-tuple-element.72.rest_0_), channel_id=1, source_target_pairs={{0,4},{4,0},{8,12},{12,8},{1,5},{5,1},{9,13},{13,9},{2,6},{6,2},{1... | collective-permute-start | bytes 786440 | tf_op jit(solution)/shard_map/ppermute | solution.py:69
  50.5 3.1 %partial_products.15 = (bf16[128,1024]{1,0:T(8,128)(2,1)S(1)}, bf16[128,1024]{1,0:T(8,128)(2,1)S(1)}) custom-call(bf16[256,2176]{1,0:T(8,128)(2,1)S(1)} %pad_maximum_fusion.rows_ref.rest_0_, bf16[5472,2048]{1,0:T(8,128)(2,1)} %bitcast.19, bf16[5472,2048]{1,0:T(8,128)(2,1)} %bitcast.30, bf16[128,1024]{1,0:T(8,128)(2,1)S(1)} %get-tuple-element.72.rest_0_), custom_call_target="tpu_custom_call" | custom-call | flops 4294967296 | bytes 19922944 | tf_op jit(solution)/shard_map/partial_products/pallas_call | solution.py:215
  53.7 1.1 collective-permute-start.7
  54.8 3.1 %partial_products.16 = (bf16[128,1024]{1,0:T(8,128)(2,1)S(1)}, bf16[128,1024]{1,0:T(8,128)(2,1)S(1)}) custom-call(bf16[256,2176]{1,0:T(8,128)(2,1)S(1)} %pad_maximum_fusion.rows_ref.rest_0_, bf16[5472,2048]{1,0:T(8,128)(2,1)} %bitcast.20, bf16[5472,2048]{1,0:T(8,128)(2,1)} %bitcast.31, bf16[128,1152]{1,0:T(8,128)(2,1)S(1)} %get-tuple-element.75.rest_0_), custom_call_target="tpu_custom_call" | custom-call | flops 4294967296 | bytes 19922944 | tf_op jit(solution)/shard_map/partial_products/pallas_call | solution.py:215
  58.1 2.9 %collective-permute-start.13 = (bf16[128,1024]{1,0:T(8,128)(2,1)S(1)}, bf16[128,1024]{1,0:T(8,128)(2,1)S(1)}, u32[]{:S(2)}, u32[]{:S(2)}) collective-permute-start(bf16[128,1024]{1,0:T(8,128)(2,1)S(1)} %get-tuple-element.80.rest_0_), channel_id=1, source_target_pairs={{0,4},{4,0},{8,12},{12,8},{1,5},{5,1},{9,13},{13,9},{2,6},{6,2},{1... | collective-permute-start | bytes 786440 | tf_op jit(solution)/shard_map/ppermute | solution.py:69
  61.0 3.1 %partial_products.17 = (bf16[128,1024]{1,0:T(8,128)(2,1)S(1)}, bf16[128,1024]{1,0:T(8,128)(2,1)S(1)}) custom-call(bf16[256,2176]{1,0:T(8,128)(2,1)S(1)} %pad_maximum_fusion.rows_ref.rest_0_, bf16[5472,2048]{1,0:T(8,128)(2,1)} %bitcast.21, bf16[5472,2048]{1,0:T(8,128)(2,1)} %bitcast.32, bf16[128,1024]{1,0:T(8,128)(2,1)S(1)} %get-tuple-element.80.rest_0_), custom_call_target="tpu_custom_call" | custom-call | flops 4294967296 | bytes 19922944 | tf_op jit(solution)/shard_map/partial_products/pallas_call | solution.py:215
  64.6 2.0 %collective-permute-start.11 = (bf16[128,1536]{1,0:T(8,128)(2,1)S(1)}, bf16[128,1536]{1,0:T(8,128)(2,1)S(1)}, u32[]{:S(2)}, u32[]{:S(2)}) collective-permute-start(bf16[128,1536]{1,0:T(8,128)(2,1)S(1)} %get-tuple-element.83.rest_0_.sent), channel_id=1, source_target_pairs={{0,4},{4,0},{8,12},{12,8},{1,5},{5,1},{9,13},{13,9},{2,6},{6,2},{1... | collective-permute-start | bytes 1179656 | tf_op jit(solution)/shard_map/ppermute | solution.py:69
  66.6 3.1 %partial_products.18 = (bf16[128,1024]{1,0:T(8,128)(2,1)S(1)}, bf16[128,1024]{1,0:T(8,128)(2,1)S(1)}) custom-call(bf16[256,2176]{1,0:T(8,128)(2,1)S(1)} %pad_maximum_fusion.rows_ref.rest_0_, bf16[5472,2048]{1,0:T(8,128)(2,1)} %bitcast.22, bf16[5472,2048]{1,0:T(8,128)(2,1)} %bitcast.33, bf16[128,1536]{1,0:T(8,128)(2,1)S(1)} %get-tuple-element.83.rest_0_.sent), custom_call_target="tpu_custom_call" | custom-call | flops 4294967296 | bytes 19922944 | tf_op jit(solution)/shard_map/partial_products/pallas_call | solution.py:215
  70.2 2.9 %collective-permute-start.17 = (bf16[128,1536]{1,0:T(8,128)(2,1)S(1)}, bf16[128,1536]{1,0:T(8,128)(2,1)S(1)}, u32[]{:S(2)}, u32[]{:S(2)}) collective-permute-start(bf16[128,1536]{1,0:T(8,128)(2,1)S(1)} %get-tuple-element.89.rest_0_.sent), channel_id=1, source_target_pairs={{0,4},{4,0},{8,12},{12,8},{1,5},{5,1},{9,13},{13,9},{2,6},{6,2},{1... | collective-permute-start | bytes 1179656 | tf_op jit(solution)/shard_map/ppermute | solution.py:69
  73.1 3.1 %partial_products.19 = (bf16[128,1024]{1,0:T(8,128)(2,1)S(1)}, bf16[128,1024]{1,0:T(8,128)(2,1)S(1)}) custom-call(bf16[256,2176]{1,0:T(8,128)(2,1)S(1)} %pad_maximum_fusion.rows_ref.rest_0_, bf16[5472,2048]{1,0:T(8,128)(2,1)} %bitcast.23, bf16[5472,2048]{1,0:T(8,128)(2,1)} %bitcast.34, bf16[128,1536]{1,0:T(8,128)(2,1)S(1)} %get-tuple-element.89.rest_0_.sent), custom_call_target="tpu_custom_call" | custom-call | flops 4294967296 | bytes 19922944 | tf_op jit(solution)/shard_map/partial_products/pallas_call | solution.py:215
  76.2 2.2 %collective-permute-done.11.refs_1_.got = bf16[128,1536]{1,0:T(8,128)(2,1)S(1)} collective-permute-done((bf16[128,1536]{1,0:T(8,128)(2,1)S(1)}, bf16[128,1536]{1,0:T(8,128)(2,1)S(1)}, u32[]{:S(2)}, u32[]{:S(2)}) %collective-permute-start.11) | collective-permute-done | bytes 393248 | tf_op jit(solution)/shard_map/ppermute | solution.py:69
  78.9 3.5 %collective-permute-start.16 = (bf16[128,1536]{1,0:T(8,128)(2,1)S(1)}, bf16[128,1536]{1,0:T(8,128)(2,1)S(1)}, u32[]{:S(2)}, u32[]{:S(2)}) collective-permute-start(bf16[128,1536]{1,0:T(8,128)(2,1)S(1)} %get-tuple-element.93.rest_0_.sent), channel_id=1, source_target_pairs={{0,4},{4,0},{8,12},{12,8},{1,5},{5,1},{9,13},{13,9},{2,6},{6,2},{1... | collective-permute-start | bytes 1179656 | tf_op jit(solution)/shard_map/ppermute | solution.py:69
  82.4 3.2 %partial_products.20 = (bf16[128,1024]{1,0:T(8,128)(2,1)S(1)}, bf16[128,1024]{1,0:T(8,128)(2,1)S(1)}) custom-call(bf16[256,2176]{1,0:T(8,128)(2,1)S(1)} %pad_maximum_fusion.rows_ref.rest_0_, bf16[5472,2048]{1,0:T(8,128)(2,1)} %bitcast.24, bf16[5472,2048]{1,0:T(8,128)(2,1)} %bitcast.35, bf16[128,1536]{1,0:T(8,128)(2,1)S(1)} %get-tuple-element.93.rest_0_.sent), custom_call_target="tpu_custom_call" | custom-call | flops 4294967296 | bytes 19922944 | tf_op jit(solution)/shard_map/partial_products/pallas_call | solution.py:215
  85.6 1.2 collective-permute-done.17.refs_1_.got
  87.0 2.0 %collective-permute-start.21 = (bf16[128,1536]{1,0:T(8,128)(2,1)S(1)}, bf16[128,1536]{1,0:T(8,128)(2,1)S(1)}, u32[]{:S(2)}, u32[]{:S(2)}) collective-permute-start(bf16[128,1536]{1,0:T(8,128)(2,1)S(1)} %get-tuple-element.97.rest_0_.sent), channel_id=1, source_target_pairs={{0,4},{4,0},{8,12},{12,8},{1,5},{5,1},{9,13},{13,9},{2,6},{6,2},{1... | collective-permute-start | bytes 1179656 | tf_op jit(solution)/shard_map/ppermute | solution.py:69
  89.1 3.2 %partial_products.21 = (bf16[128,1024]{1,0:T(8,128)(2,1)S(1)}, bf16[128,1024]{1,0:T(8,128)(2,1)S(1)}) custom-call(bf16[256,2176]{1,0:T(8,128)(2,1)S(1)} %pad_maximum_fusion.rows_ref.rest_0_, bf16[5472,2048]{1,0:T(8,128)(2,1)} %bitcast.25, bf16[5472,2048]{1,0:T(8,128)(2,1)} %bitcast.36, bf16[128,1536]{1,0:T(8,128)(2,1)S(1)} %get-tuple-element.97.rest_0_.sent), custom_call_target="tpu_custom_call" | custom-call | flops 4294967296 | bytes 19922944 | tf_op jit(solution)/shard_map/partial_products/pallas_call | solution.py:215
  92.3 2.9 %collective-permute-done.16.refs_1_.got = bf16[128,1536]{1,0:T(8,128)(2,1)S(1)} collective-permute-done((bf16[128,1536]{1,0:T(8,128)(2,1)S(1)}, bf16[128,1536]{1,0:T(8,128)(2,1)S(1)}, u32[]{:S(2)}, u32[]{:S(2)}) %collective-permute-start.16) | collective-permute-done | bytes 393248 | tf_op jit(solution)/shard_map/ppermute | solution.py:69
  95.5 2.0 %collective-permute-start.19 = (bf16[128,1536]{1,0:T(8,128)(2,1)S(1)}, bf16[128,1536]{1,0:T(8,128)(2,1)S(1)}, u32[]{:S(2)}, u32[]{:S(2)}) collective-permute-start(bf16[128,1536]{1,0:T(8,128)(2,1)S(1)} %get-tuple-element.100.refs_7_.sent), channel_id=1, source_target_pairs={{0,4},{4,0},{8,12},{12,8},{1,5},{5,1},{9,13},{13,9},{2,6},{6,2},{1... | collective-permute-start | bytes 1179656 | tf_op jit(solution)/shard_map/ppermute | solution.py:69
  97.5 6.2 %collective-permute-done.21.refs_1_.got = bf16[128,1536]{1,0:T(8,128)(2,1)S(1)} collective-permute-done((bf16[128,1536]{1,0:T(8,128)(2,1)S(1)}, bf16[128,1536]{1,0:T(8,128)(2,1)S(1)}, u32[]{:S(2)}, u32[]{:S(2)}) %collective-permute-start.21) | collective-permute-done | bytes 393248 | tf_op jit(solution)/shard_map/ppermute | solution.py:69
  103.9 2.0 %collective-permute-start.23 = (bf16[128,1536]{1,0:T(8,128)(2,1)S(1)}, bf16[128,1536]{1,0:T(8,128)(2,1)S(1)}, u32[]{:S(2)}, u32[]{:S(2)}) collective-permute-start(bf16[128,1536]{1,0:T(8,128)(2,1)S(1)} %get-tuple-element.105.refs_7_.sent), channel_id=1, source_target_pairs={{0,4},{4,0},{8,12},{12,8},{1,5},{5,1},{9,13},{13,9},{2,6},{6,2},{1... | collective-permute-start | bytes 1179656 | tf_op jit(solution)/shard_map/ppermute | solution.py:69
  105.9 6.2 %collective-permute-done.19.refs_1_.late.got = bf16[128,1536]{1,0:T(8,128)(2,1)S(1)} collective-permute-done((bf16[128,1536]{1,0:T(8,128)(2,1)S(1)}, bf16[128,1536]{1,0:T(8,128)(2,1)S(1)}, u32[]{:S(2)}, u32[]{:S(2)}) %collective-permute-start.19) | collective-permute-done | bytes 393248 | tf_op jit(solution)/shard_map/ppermute | solution.py:69
  112.3 2.0 %collective-permute-start.25 = (bf16[128,1536]{1,0:T(8,128)(2,1)S(1)}, bf16[128,1536]{1,0:T(8,128)(2,1)S(1)}, u32[]{:S(2)}, u32[]{:S(2)}) collective-permute-start(bf16[128,1536]{1,0:T(8,128)(2,1)S(1)} %get-tuple-element.106.rest_0_.sent), channel_id=1, source_target_pairs={{0,4},{4,0},{8,12},{12,8},{1,5},{5,1},{9,13},{13,9},{2,6},{6,2},{1... | collective-permute-start | bytes 1179656 | tf_op jit(solution)/shard_map/ppermute | solution.py:69
  115.2 5.4 %collective-permute-done.23.refs_1_.late.got = bf16[128,1536]{1,0:T(8,128)(2,1)S(1)} collective-permute-done((bf16[128,1536]{1,0:T(8,128)(2,1)S(1)}, bf16[128,1536]{1,0:T(8,128)(2,1)S(1)}, u32[]{:S(2)}, u32[]{:S(2)}) %collective-permute-start.23) | collective-permute-done | bytes 393248 | tf_op jit(solution)/shard_map/ppermute | solution.py:69
  120.7 2.0 %collective-permute-start.27 = (bf16[128,1536]{1,0:T(8,128)(2,1)S(1)}, bf16[128,1536]{1,0:T(8,128)(2,1)S(1)}, u32[]{:S(2)}, u32[]{:S(2)}) collective-permute-start(bf16[128,1536]{1,0:T(8,128)(2,1)S(1)} %get-tuple-element.109.rest_0_.sent), channel_id=1, source_target_pairs={{0,4},{4,0},{8,12},{12,8},{1,5},{5,1},{9,13},{13,9},{2,6},{6,2},{1... | collective-permute-start | bytes 1179656 | tf_op jit(solution)/shard_map/ppermute | solution.py:69
  123.5 5.4 %collective-permute-done.25.refs_1_.late.got = bf16[128,1536]{1,0:T(8,128)(2,1)S(1)} collective-permute-done((bf16[128,1536]{1,0:T(8,128)(2,1)S(1)}, bf16[128,1536]{1,0:T(8,128)(2,1)S(1)}, u32[]{:S(2)}, u32[]{:S(2)}) %collective-permute-start.25) | collective-permute-done | bytes 393248 | tf_op jit(solution)/shard_map/ppermute | solution.py:69
  129.2 2.0 %collective-permute-start.29 = (bf16[128,1536]{1,0:T(8,128)(2,1)S(1)}, bf16[128,1536]{1,0:T(8,128)(2,1)S(1)}, u32[]{:S(2)}, u32[]{:S(2)}) collective-permute-start(bf16[128,1536]{1,0:T(8,128)(2,1)S(1)} %get-tuple-element.112.rest_0_.sent), channel_id=1, source_target_pairs={{0,4},{4,0},{8,12},{12,8},{1,5},{5,1},{9,13},{13,9},{2,6},{6,2},{1... | collective-permute-start | bytes 1179656 | tf_op jit(solution)/shard_map/ppermute | solution.py:69
  132.0 5.4 %collective-permute-done.27.refs_1_.late.got = bf16[128,1536]{1,0:T(8,128)(2,1)S(1)} collective-permute-done((bf16[128,1536]{1,0:T(8,128)(2,1)S(1)}, bf16[128,1536]{1,0:T(8,128)(2,1)S(1)}, u32[]{:S(2)}, u32[]{:S(2)}) %collective-permute-start.27) | collective-permute-done | bytes 393248 | tf_op jit(solution)/shard_map/ppermute | solution.py:69
  137.6 1.9 %collective-permute-start.31 = (bf16[128,512]{1,0:T(8,128)(2,1)S(1)}, bf16[128,512]{1,0:T(8,128)(2,1)S(1)}, u32[]{:S(2)}, u32[]{:S(2)}) collective-permute-start(bf16[128,512]{1,0:T(8,128)(2,1)S(1)} %get-tuple-element.114.rest_0_.sent), channel_id=1, source_target_pairs={{0,4},{4,0},{8,12},{12,8},{1,5},{5,1},{9,13},{13,9},{2,6},{6,2},{1... | collective-permute-start | bytes 393224 | tf_op jit(solution)/shard_map/ppermute | solution.py:69
  140.3 5.5 %collective-permute-done.29.refs_1_.late.got = bf16[128,1536]{1,0:T(8,128)(2,1)S(1)} collective-permute-done((bf16[128,1536]{1,0:T(8,128)(2,1)S(1)}, bf16[128,1536]{1,0:T(8,128)(2,1)S(1)}, u32[]{:S(2)}, u32[]{:S(2)}) %collective-permute-start.29) | collective-permute-done | bytes 393248 | tf_op jit(solution)/shard_map/ppermute | solution.py:69
  146.0 1.9 %collective-permute-start.33 = (bf16[128,512]{1,0:T(8,128)(2,1)S(1)}, bf16[128,512]{1,0:T(8,128)(2,1)S(1)}, u32[]{:S(2)}, u32[]{:S(2)}) collective-permute-start(bf16[128,512]{1,0:T(8,128)(2,1)S(1)} %get-tuple-element.116.rest_0_.sent), channel_id=1, source_target_pairs={{0,4},{4,0},{8,12},{12,8},{1,5},{5,1},{9,13},{13,9},{2,6},{6,2},{1... | collective-permute-start | bytes 393224 | tf_op jit(solution)/shard_map/ppermute | solution.py:69
  148.8 3.3 %collective-permute-start.35 = (bf16[128,512]{1,0:T(8,128)(2,1)S(1)}, bf16[128,512]{1,0:T(8,128)(2,1)S(1)}, u32[]{:S(2)}, u32[]{:S(2)}) collective-permute-start(bf16[128,512]{1,0:T(8,128)(2,1)S(1)} %get-tuple-element.118.rest_0_), channel_id=1, source_target_pairs={{0,4},{4,0},{8,12},{12,8},{1,5},{5,1},{9,13},{13,9},{2,6},{6,2},{1... | collective-permute-start | bytes 393224 | tf_op jit(solution)/shard_map/ppermute | solution.py:69
  153.0 2.7 %collective-permute-start.37 = (bf16[128,512]{1,0:T(8,128)(2,1)S(1)}, bf16[128,512]{1,0:T(8,128)(2,1)S(1)}, u32[]{:S(2)}, u32[]{:S(2)}) collective-permute-start(bf16[128,512]{1,0:T(8,128)(2,1)S(1)} %get-tuple-element.120.rest_0_), channel_id=1, source_target_pairs={{0,4},{4,0},{8,12},{12,8},{1,5},{5,1},{9,13},{13,9},{2,6},{6,2},{1... | collective-permute-start | bytes 393224 | tf_op jit(solution)/shard_map/ppermute | solution.py:69
  156.6 2.5 %collective-permute-start.39 = (bf16[128,512]{1,0:T(8,128)(2,1)S(1)}, bf16[128,512]{1,0:T(8,128)(2,1)S(1)}, u32[]{:S(2)}, u32[]{:S(2)}) collective-permute-start(bf16[128,512]{1,0:T(8,128)(2,1)S(1)} %hop.36.rest_0_), channel_id=1, source_target_pairs={{0,4},{4,0},{8,12},{12,8},{1,5},{5,1},{9,13},{13,9},{2,6},{6,2},{1... | collective-permute-start | bytes 393224 | tf_op jit(solution)/shard_map/ppermute | solution.py:69
  159.9 2.1 %collective-permute-start.40 = (bf16[128,512]{1,0:T(8,128)(2,1)S(1)}, bf16[128,512]{1,0:T(8,128)(2,1)S(1)}, u32[]{:S(2)}, u32[]{:S(2)}) collective-permute-start(bf16[128,512]{1,0:T(8,128)(2,1)S(1)} %hop.37.rest_0_), channel_id=1, source_target_pairs={{0,4},{4,0},{8,12},{12,8},{1,5},{5,1},{9,13},{13,9},{2,6},{6,2},{1... | collective-permute-start | bytes 393224 | tf_op jit(solution)/shard_map/ppermute | solution.py:69
  166.2 1.9 %collective-permute-done.41 = bf16[128,2048]{1,0:T(8,128)(2,1)S(1)} collective-permute-done((bf16[128,2048]{1,0:T(8,128)(2,1)S(1)}, bf16[128,2048]{1,0:T(8,128)(2,1)S(1)}, u32[]{:S(2)}, u32[]{:S(2)}) %collective-permute-start.41) | collective-permute-done | bytes 524320 | tf_op jit(solution)/shard_map/ppermute | solution.py:77
  168.3 1.6 collective-permute-start.42
  170.6 6.2 %collective-permute-done.42 = bf16[64,2048]{1,0:T(8,128)(2,1)S(1)} collective-permute-done((bf16[64,2048]{1,0:T(8,128)(2,1)S(1)}, bf16[64,2048]{1,0:T(8,128)(2,1)S(1)}, u32[]{:S(2)}, u32[]{:S(2)}) %collective-permute-start.42) | collective-permute-done | bytes 262176 | tf_op jit(solution)/shard_map/ppermute | solution.py:77
  (118 shorter events, 16.6 us)
Async XLA Ops:
  13.8 9.7 %collective-permute-start = (bf16[64,2176]{1,0:T(8,128)(2,1)S(1)}, bf16[64,2176]{1,0:T(8,128)(2,1)S(1)}, u32[]{:S(2)}, u32[]{:S(2)}) collective-permute-start(bf16[64,2176]{1,0:T(8,128)(2,1)S(1)} %get-tuple-element.65), channel_id=1, source_target_pairs={{0,2},{2,0},{1,3},{3,1},{4,6},{6,4},{5,7},{7,5},{8,10},{10,8},{9,1... | collective-permute-start | bytes 835592 | tf_op jit(solution)/shard_map/ppermute | solution.py:77
  16.8 6.7 %collective-permute-start.1 = (bf16[64,2176]{1,0:T(8,128)(2,1)S(1)}, bf16[64,2176]{1,0:T(8,128)(2,1)S(1)}, u32[]{:S(2)}, u32[]{:S(2)}) collective-permute-start(bf16[64,2176]{1,0:T(8,128)(2,1)S(1)} %get-tuple-element.65), channel_id=1, source_target_pairs={{0,1},{1,0},{2,3},{3,2},{4,5},{5,4},{6,7},{7,6},{8,9},{9,8},{10,11... | collective-permute-start | bytes 835592 | tf_op jit(solution)/shard_map/ppermute | solution.py:77
  23.5 1.6 collective-permute-start.2
  31.5 9.9 %collective-permute-start.3 = (bf16[128,1152]{1,0:T(8,128)(2,1)S(1)}, bf16[128,1152]{1,0:T(8,128)(2,1)S(1)}, u32[]{:S(2)}, u32[]{:S(2)}) collective-permute-start(bf16[128,1152]{1,0:T(8,128)(2,1)S(1)} %get-tuple-element.66.rest_0_.refs_3_), channel_id=1, source_target_pairs={{0,4},{4,0},{8,12},{12,8},{1,5},{5,1},{9,13},{13,9},{2,6},{6,2},{1... | collective-permute-start | bytes 884744 | tf_op jit(solution)/shard_map/ppermute | solution.py:69
  33.4 14.7 %collective-permute-start.6 = (bf16[128,1024]{1,0:T(8,128)(2,1)S(1)}, bf16[128,1024]{1,0:T(8,128)(2,1)S(1)}, u32[]{:S(2)}, u32[]{:S(2)}) collective-permute-start(bf16[128,1024]{1,0:T(8,128)(2,1)S(1)} %get-tuple-element.67.rest_0_.refs_3_), channel_id=1, source_target_pairs={{0,4},{4,0},{8,12},{12,8},{1,5},{5,1},{9,13},{13,9},{2,6},{6,2},{1... | collective-permute-start | bytes 786440 | tf_op jit(solution)/shard_map/ppermute | solution.py:69
  41.4 12.2 %collective-permute-start.5 = (bf16[128,1152]{1,0:T(8,128)(2,1)S(1)}, bf16[128,1152]{1,0:T(8,128)(2,1)S(1)}, u32[]{:S(2)}, u32[]{:S(2)}) collective-permute-start(bf16[128,1152]{1,0:T(8,128)(2,1)S(1)} %get-tuple-element.70), channel_id=1, source_target_pairs={{0,1},{1,0},{4,8},{8,4},{5,9},{9,5},{12,13},{13,12},{2,3},{3,2},{6... | collective-permute-start | bytes 884744 | tf_op jit(solution)/shard_map/ppermute | solution.py:73
  41.5 12.1 %collective-permute-start.4 = (bf16[128,1024]{1,0:T(8,128)(2,1)S(1)}, bf16[128,1024]{1,0:T(8,128)(2,1)S(1)}, u32[]{:S(2)}, u32[]{:S(2)}) collective-permute-start(bf16[128,1024]{1,0:T(8,128)(2,1)S(1)} %get-tuple-element.69.rest_0_), channel_id=1, source_target_pairs={{0,4},{4,0},{8,12},{12,8},{1,5},{5,1},{9,13},{13,9},{2,6},{6,2},{1... | collective-permute-start | bytes 786440 | tf_op jit(solution)/shard_map/ppermute | solution.py:69
  48.1 9.7 %collective-permute-start.10 = (bf16[128,1024]{1,0:T(8,128)(2,1)S(1)}, bf16[128,1024]{1,0:T(8,128)(2,1)S(1)}, u32[]{:S(2)}, u32[]{:S(2)}) collective-permute-start(bf16[128,1024]{1,0:T(8,128)(2,1)S(1)} %get-tuple-element.77), channel_id=1, source_target_pairs={{0,1},{1,0},{4,8},{8,4},{5,9},{9,5},{12,13},{13,12},{2,3},{3,2},{6... | collective-permute-start | bytes 786440 | tf_op jit(solution)/shard_map/ppermute | solution.py:73
  48.2 9.9 %collective-permute-start.9 = (bf16[128,1024]{1,0:T(8,128)(2,1)S(1)}, bf16[128,1024]{1,0:T(8,128)(2,1)S(1)}, u32[]{:S(2)}, u32[]{:S(2)}) collective-permute-start(bf16[128,1024]{1,0:T(8,128)(2,1)S(1)} %get-tuple-element.72.rest_0_), channel_id=1, source_target_pairs={{0,4},{4,0},{8,12},{12,8},{1,5},{5,1},{9,13},{13,9},{2,6},{6,2},{1... | collective-permute-start | bytes 786440 | tf_op jit(solution)/shard_map/ppermute | solution.py:69
  53.7 10.7 %collective-permute-start.7 = (bf16[128,1152]{1,0:T(8,128)(2,1)S(1)}, bf16[128,1152]{1,0:T(8,128)(2,1)S(1)}, u32[]{:S(2)}, u32[]{:S(2)}) collective-permute-start(bf16[128,1152]{1,0:T(8,128)(2,1)S(1)} %get-tuple-element.75.rest_0_), channel_id=1, source_target_pairs={{0,4},{4,0},{8,12},{12,8},{1,5},{5,1},{9,13},{13,9},{2,6},{6,2},{1... | collective-permute-start | bytes 884744 | tf_op jit(solution)/shard_map/ppermute | solution.py:69
  54.8 9.3 %collective-permute-start.8 = (bf16[128,1024]{1,0:T(8,128)(2,1)S(1)}, bf16[128,1024]{1,0:T(8,128)(2,1)S(1)}, u32[]{:S(2)}, u32[]{:S(2)}) collective-permute-start(bf16[128,1024]{1,0:T(8,128)(2,1)S(1)} %get-tuple-element.76), channel_id=1, source_target_pairs={{0,1},{1,0},{4,8},{8,4},{5,9},{9,5},{12,13},{13,12},{2,3},{3,2},{6... | collective-permute-start | bytes 786440 | tf_op jit(solution)/shard_map/ppermute | solution.py:73
  58.1 11.9 %collective-permute-start.13 = (bf16[128,1024]{1,0:T(8,128)(2,1)S(1)}, bf16[128,1024]{1,0:T(8,128)(2,1)S(1)}, u32[]{:S(2)}, u32[]{:S(2)}) collective-permute-start(bf16[128,1024]{1,0:T(8,128)(2,1)S(1)} %get-tuple-element.80.rest_0_), channel_id=1, source_target_pairs={{0,4},{4,0},{8,12},{12,8},{1,5},{5,1},{9,13},{13,9},{2,6},{6,2},{1... | collective-permute-start | bytes 786440 | tf_op jit(solution)/shard_map/ppermute | solution.py:69
  61.0 9.0 %collective-permute-start.14 = (bf16[128,1024]{1,0:T(8,128)(2,1)S(1)}, bf16[128,1024]{1,0:T(8,128)(2,1)S(1)}, u32[]{:S(2)}, u32[]{:S(2)}) collective-permute-start(bf16[128,1024]{1,0:T(8,128)(2,1)S(1)} %get-tuple-element.85), channel_id=1, source_target_pairs={{0,1},{1,0},{4,8},{8,4},{5,9},{9,5},{12,13},{13,12},{2,3},{3,2},{6... | collective-permute-start | bytes 786440 | tf_op jit(solution)/shard_map/ppermute | solution.py:73
  64.6 13.8 %collective-permute-start.11 = (bf16[128,1536]{1,0:T(8,128)(2,1)S(1)}, bf16[128,1536]{1,0:T(8,128)(2,1)S(1)}, u32[]{:S(2)}, u32[]{:S(2)}) collective-permute-start(bf16[128,1536]{1,0:T(8,128)(2,1)S(1)} %get-tuple-element.83.rest_0_.sent), channel_id=1, source_target_pairs={{0,4},{4,0},{8,12},{12,8},{1,5},{5,1},{9,13},{13,9},{2,6},{6,2},{1... | collective-permute-start | bytes 1179656 | tf_op jit(solution)/shard_map/ppermute | solution.py:69
  66.6 9.6 %collective-permute-start.12 = (bf16[128,1024]{1,0:T(8,128)(2,1)S(1)}, bf16[128,1024]{1,0:T(8,128)(2,1)S(1)}, u32[]{:S(2)}, u32[]{:S(2)}) collective-permute-start(bf16[128,1024]{1,0:T(8,128)(2,1)S(1)} %get-tuple-element.84), channel_id=1, source_target_pairs={{0,1},{1,0},{4,8},{8,4},{5,9},{9,5},{12,13},{13,12},{2,3},{3,2},{6... | collective-permute-start | bytes 786440 | tf_op jit(solution)/shard_map/ppermute | solution.py:73
  70.2 16.7 %collective-permute-start.17 = (bf16[128,1536]{1,0:T(8,128)(2,1)S(1)}, bf16[128,1536]{1,0:T(8,128)(2,1)S(1)}, u32[]{:S(2)}, u32[]{:S(2)}) collective-permute-start(bf16[128,1536]{1,0:T(8,128)(2,1)S(1)} %get-tuple-element.89.rest_0_.sent), channel_id=1, source_target_pairs={{0,4},{4,0},{8,12},{12,8},{1,5},{5,1},{9,13},{13,9},{2,6},{6,2},{1... | collective-permute-start | bytes 1179656 | tf_op jit(solution)/shard_map/ppermute | solution.py:69
  73.1 12.5 %collective-permute-start.18 = (bf16[128,1024]{1,0:T(8,128)(2,1)S(1)}, bf16[128,1024]{1,0:T(8,128)(2,1)S(1)}, u32[]{:S(2)}, u32[]{:S(2)}) collective-permute-start(bf16[128,1024]{1,0:T(8,128)(2,1)S(1)} %get-tuple-element.94), channel_id=1, source_target_pairs={{0,1},{1,0},{4,8},{8,4},{5,9},{9,5},{12,13},{13,12},{2,3},{3,2},{6... | collective-permute-start | bytes 786440 | tf_op jit(solution)/shard_map/ppermute | solution.py:73
  78.8 13.5 %collective-permute-start.15 = (bf16[128,1536]{1,0:T(8,128)(2,1)S(1)}, bf16[128,1536]{1,0:T(8,128)(2,1)S(1)}, u32[]{:S(2)}, u32[]{:S(2)}) collective-permute-start(bf16[128,1536]{1,0:T(8,128)(2,1)S(1)} %get-tuple-element.92), channel_id=1, source_target_pairs={{0,1},{1,0},{4,8},{8,4},{5,9},{9,5},{12,13},{13,12},{2,3},{3,2},{6... | collective-permute-start | bytes 1179656 | tf_op jit(solution)/shard_map/ppermute | solution.py:73
  78.9 16.4 %collective-permute-start.16 = (bf16[128,1536]{1,0:T(8,128)(2,1)S(1)}, bf16[128,1536]{1,0:T(8,128)(2,1)S(1)}, u32[]{:S(2)}, u32[]{:S(2)}) collective-permute-start(bf16[128,1536]{1,0:T(8,128)(2,1)S(1)} %get-tuple-element.93.rest_0_.sent), channel_id=1, source_target_pairs={{0,4},{4,0},{8,12},{12,8},{1,5},{5,1},{9,13},{13,9},{2,6},{6,2},{1... | collective-permute-start | bytes 1179656 | tf_op jit(solution)/shard_map/ppermute | solution.py:69
  82.4 32.0 %slice-start = ((s8[22413312]{0:T(1024)(128)(4,1)}), s8[4194304]{0:T(1024)(128)(4,1)S(1)}, s32[]{:S(2)}) async-start(s8[22413312]{0:T(1024)(128)(4,1)} %bitcast.37), calls=%async_computation | async-start | bytes 8388608
  82.4 32.0 %slice-start.1 = ((s8[22413312]{0:T(1024)(128)(4,1)}), s8[4194304]{0:T(1024)(128)(4,1)S(1)}, s32[]{:S(2)}) async-start(s8[22413312]{0:T(1024)(128)(4,1)} %bitcast.37), calls=%async_computation.1 | async-start | bytes 8388608
  82.4 32.0 %slice-start.2 = ((s8[22413312]{0:T(1024)(128)(4,1)}), s8[4194304]{0:T(1024)(128)(4,1)S(1)}, s32[]{:S(2)}) async-start(s8[22413312]{0:T(1024)(128)(4,1)} %bitcast.37), calls=%async_computation.2 | async-start | bytes 8388608
  87.0 16.7 %collective-permute-start.21 = (bf16[128,1536]{1,0:T(8,128)(2,1)S(1)}, bf16[128,1536]{1,0:T(8,128)(2,1)S(1)}, u32[]{:S(2)}, u32[]{:S(2)}) collective-permute-start(bf16[128,1536]{1,0:T(8,128)(2,1)S(1)} %get-tuple-element.97.rest_0_.sent), channel_id=1, source_target_pairs={{0,4},{4,0},{8,12},{12,8},{1,5},{5,1},{9,13},{13,9},{2,6},{6,2},{1... | collective-permute-start | bytes 1179656 | tf_op jit(solution)/shard_map/ppermute | solution.py:69
  89.1 25.4 %slice-start.4 = ((s8[22413312]{0:T(1024)(128)(4,1)}), s8[4194304]{0:T(1024)(128)(4,1)S(1)}, s32[]{:S(2)}) async-start(s8[22413312]{0:T(1024)(128)(4,1)} %bitcast.37), calls=%async_computation.4 | async-start | bytes 8388608
  89.1 25.4 %slice-start.5 = ((s8[22413312]{0:T(1024)(128)(4,1)}), s8[1441792]{0:T(1024)(128)(4,1)S(1)}, s32[]{:S(2)}) async-start(s8[22413312]{0:T(1024)(128)(4,1)} %bitcast.37), calls=%async_computation.5 | async-start | bytes 2883584
  89.1 14.7 %collective-permute-start.22 = (bf16[128,1536]{1,0:T(8,128)(2,1)S(1)}, bf16[128,1536]{1,0:T(8,128)(2,1)S(1)}, u32[]{:S(2)}, u32[]{:S(2)}) collective-permute-start(bf16[128,1536]{1,0:T(8,128)(2,1)S(1)} %get-tuple-element.103), channel_id=1, source_target_pairs={{0,1},{1,0},{4,8},{8,4},{5,9},{9,5},{12,13},{13,12},{2,3},{3,2},{6... | collective-permute-start | bytes 1179656 | tf_op jit(solution)/shard_map/ppermute | solution.py:73
  95.5 16.7 %collective-permute-start.19 = (bf16[128,1536]{1,0:T(8,128)(2,1)S(1)}, bf16[128,1536]{1,0:T(8,128)(2,1)S(1)}, u32[]{:S(2)}, u32[]{:S(2)}) collective-permute-start(bf16[128,1536]{1,0:T(8,128)(2,1)S(1)} %get-tuple-element.100.refs_7_.sent), channel_id=1, source_target_pairs={{0,4},{4,0},{8,12},{12,8},{1,5},{5,1},{9,13},{13,9},{2,6},{6,2},{1... | collective-permute-start | bytes 1179656 | tf_op jit(solution)/shard_map/ppermute | solution.py:69
  97.5 14.7 %collective-permute-start.20 = (bf16[128,1536]{1,0:T(8,128)(2,1)S(1)}, bf16[128,1536]{1,0:T(8,128)(2,1)S(1)}, u32[]{:S(2)}, u32[]{:S(2)}) collective-permute-start(bf16[128,1536]{1,0:T(8,128)(2,1)S(1)} %get-tuple-element.101), channel_id=1, source_target_pairs={{0,1},{1,0},{4,8},{8,4},{5,9},{9,5},{12,13},{13,12},{2,3},{3,2},{6... | collective-permute-start | bytes 1179656 | tf_op jit(solution)/shard_map/ppermute | solution.py:73
  103.9 16.7 %collective-permute-start.23 = (bf16[128,1536]{1,0:T(8,128)(2,1)S(1)}, bf16[128,1536]{1,0:T(8,128)(2,1)S(1)}, u32[]{:S(2)}, u32[]{:S(2)}) collective-permute-start(bf16[128,1536]{1,0:T(8,128)(2,1)S(1)} %get-tuple-element.105.refs_7_.sent), channel_id=1, source_target_pairs={{0,4},{4,0},{8,12},{12,8},{1,5},{5,1},{9,13},{13,9},{2,6},{6,2},{1... | collective-permute-start | bytes 1179656 | tf_op jit(solution)/shard_map/ppermute | solution.py:69
  105.9 14.7 %collective-permute-start.24 = (bf16[128,1536]{1,0:T(8,128)(2,1)S(1)}, bf16[128,1536]{1,0:T(8,128)(2,1)S(1)}, u32[]{:S(2)}, u32[]{:S(2)}) collective-permute-start(bf16[128,1536]{1,0:T(8,128)(2,1)S(1)} %get-tuple-element.107), channel_id=1, source_target_pairs={{0,1},{1,0},{4,8},{8,4},{5,9},{9,5},{12,13},{13,12},{2,3},{3,2},{6... | collective-permute-start | bytes 1179656 | tf_op jit(solution)/shard_map/ppermute | solution.py:73
  112.3 16.7 %collective-permute-start.25 = (bf16[128,1536]{1,0:T(8,128)(2,1)S(1)}, bf16[128,1536]{1,0:T(8,128)(2,1)S(1)}, u32[]{:S(2)}, u32[]{:S(2)}) collective-permute-start(bf16[128,1536]{1,0:T(8,128)(2,1)S(1)} %get-tuple-element.106.rest_0_.sent), channel_id=1, source_target_pairs={{0,4},{4,0},{8,12},{12,8},{1,5},{5,1},{9,13},{13,9},{2,6},{6,2},{1... | collective-permute-start | bytes 1179656 | tf_op jit(solution)/shard_map/ppermute | solution.py:69
  114.3 14.7 %collective-permute-start.26 = (bf16[128,1536]{1,0:T(8,128)(2,1)S(1)}, bf16[128,1536]{1,0:T(8,128)(2,1)S(1)}, u32[]{:S(2)}, u32[]{:S(2)}) collective-permute-start(bf16[128,1536]{1,0:T(8,128)(2,1)S(1)} %get-tuple-element.110), channel_id=1, source_target_pairs={{0,1},{1,0},{4,8},{8,4},{5,9},{9,5},{12,13},{13,12},{2,3},{3,2},{6... | collective-permute-start | bytes 1179656 | tf_op jit(solution)/shard_map/ppermute | solution.py:73
  120.7 16.7 %collective-permute-start.27 = (bf16[128,1536]{1,0:T(8,128)(2,1)S(1)}, bf16[128,1536]{1,0:T(8,128)(2,1)S(1)}, u32[]{:S(2)}, u32[]{:S(2)}) collective-permute-start(bf16[128,1536]{1,0:T(8,128)(2,1)S(1)} %get-tuple-element.109.rest_0_.sent), channel_id=1, source_target_pairs={{0,4},{4,0},{8,12},{12,8},{1,5},{5,1},{9,13},{13,9},{2,6},{6,2},{1... | collective-permute-start | bytes 1179656 | tf_op jit(solution)/shard_map/ppermute | solution.py:69
  123.5 8.5 %collective-permute-start.28 = (bf16[128,512]{1,0:T(8,128)(2,1)S(1)}, bf16[128,512]{1,0:T(8,128)(2,1)S(1)}, u32[]{:S(2)}, u32[]{:S(2)}) collective-permute-start(bf16[128,512]{1,0:T(8,128)(2,1)S(1)} %get-tuple-element.113), channel_id=1, source_target_pairs={{0,1},{1,0},{4,8},{8,4},{5,9},{9,5},{12,13},{13,12},{2,3},{3,2},{6... | collective-permute-start | bytes 393224 | tf_op jit(solution)/shard_map/ppermute | solution.py:73
  129.2 16.7 %collective-permute-start.29 = (bf16[128,1536]{1,0:T(8,128)(2,1)S(1)}, bf16[128,1536]{1,0:T(8,128)(2,1)S(1)}, u32[]{:S(2)}, u32[]{:S(2)}) collective-permute-start(bf16[128,1536]{1,0:T(8,128)(2,1)S(1)} %get-tuple-element.112.rest_0_.sent), channel_id=1, source_target_pairs={{0,4},{4,0},{8,12},{12,8},{1,5},{5,1},{9,13},{13,9},{2,6},{6,2},{1... | collective-permute-start | bytes 1179656 | tf_op jit(solution)/shard_map/ppermute | solution.py:69
  131.9 8.5 %collective-permute-start.30 = (bf16[128,512]{1,0:T(8,128)(2,1)S(1)}, bf16[128,512]{1,0:T(8,128)(2,1)S(1)}, u32[]{:S(2)}, u32[]{:S(2)}) collective-permute-start(bf16[128,512]{1,0:T(8,128)(2,1)S(1)} %get-tuple-element.115), channel_id=1, source_target_pairs={{0,1},{1,0},{4,8},{8,4},{5,9},{9,5},{12,13},{13,12},{2,3},{3,2},{6... | collective-permute-start | bytes 393224 | tf_op jit(solution)/shard_map/ppermute | solution.py:73
  137.6 11.2 %collective-permute-start.31 = (bf16[128,512]{1,0:T(8,128)(2,1)S(1)}, bf16[128,512]{1,0:T(8,128)(2,1)S(1)}, u32[]{:S(2)}, u32[]{:S(2)}) collective-permute-start(bf16[128,512]{1,0:T(8,128)(2,1)S(1)} %get-tuple-element.114.rest_0_.sent), channel_id=1, source_target_pairs={{0,4},{4,0},{8,12},{12,8},{1,5},{5,1},{9,13},{13,9},{2,6},{6,2},{1... | collective-permute-start | bytes 393224 | tf_op jit(solution)/shard_map/ppermute | solution.py:69
  140.3 8.5 %collective-permute-start.32 = (bf16[128,512]{1,0:T(8,128)(2,1)S(1)}, bf16[128,512]{1,0:T(8,128)(2,1)S(1)}, u32[]{:S(2)}, u32[]{:S(2)}) collective-permute-start(bf16[128,512]{1,0:T(8,128)(2,1)S(1)} %get-tuple-element.117), channel_id=1, source_target_pairs={{0,1},{1,0},{4,8},{8,4},{5,9},{9,5},{12,13},{13,12},{2,3},{3,2},{6... | collective-permute-start | bytes 393224 | tf_op jit(solution)/shard_map/ppermute | solution.py:73
  146.0 7.0 %collective-permute-start.33 = (bf16[128,512]{1,0:T(8,128)(2,1)S(1)}, bf16[128,512]{1,0:T(8,128)(2,1)S(1)}, u32[]{:S(2)}, u32[]{:S(2)}) collective-permute-start(bf16[128,512]{1,0:T(8,128)(2,1)S(1)} %get-tuple-element.116.rest_0_.sent), channel_id=1, source_target_pairs={{0,4},{4,0},{8,12},{12,8},{1,5},{5,1},{9,13},{13,9},{2,6},{6,2},{1... | collective-permute-start | bytes 393224 | tf_op jit(solution)/shard_map/ppermute | solution.py:69
  148.7 4.3 %collective-permute-start.34 = (bf16[128,512]{1,0:T(8,128)(2,1)S(1)}, bf16[128,512]{1,0:T(8,128)(2,1)S(1)}, u32[]{:S(2)}, u32[]{:S(2)}) collective-permute-start(bf16[128,512]{1,0:T(8,128)(2,1)S(1)} %get-tuple-element.119), channel_id=1, source_target_pairs={{0,1},{1,0},{4,8},{8,4},{5,9},{9,5},{12,13},{13,12},{2,3},{3,2},{6... | collective-permute-start | bytes 393224 | tf_op jit(solution)/shard_map/ppermute | solution.py:73
  148.8 7.7 %collective-permute-start.35 = (bf16[128,512]{1,0:T(8,128)(2,1)S(1)}, bf16[128,512]{1,0:T(8,128)(2,1)S(1)}, u32[]{:S(2)}, u32[]{:S(2)}) collective-permute-start(bf16[128,512]{1,0:T(8,128)(2,1)S(1)} %get-tuple-element.118.rest_0_), channel_id=1, source_target_pairs={{0,4},{4,0},{8,12},{12,8},{1,5},{5,1},{9,13},{13,9},{2,6},{6,2},{1... | collective-permute-start | bytes 393224 | tf_op jit(solution)/shard_map/ppermute | solution.py:69
  152.9 3.7 %collective-permute-start.36 = (bf16[128,512]{1,0:T(8,128)(2,1)S(1)}, bf16[128,512]{1,0:T(8,128)(2,1)S(1)}, u32[]{:S(2)}, u32[]{:S(2)}) collective-permute-start(bf16[128,512]{1,0:T(8,128)(2,1)S(1)} %get-tuple-element.121), channel_id=1, source_target_pairs={{0,1},{1,0},{4,8},{8,4},{5,9},{9,5},{12,13},{13,12},{2,3},{3,2},{6... | collective-permute-start | bytes 393224 | tf_op jit(solution)/shard_map/ppermute | solution.py:73
  153.0 6.9 %collective-permute-start.37 = (bf16[128,512]{1,0:T(8,128)(2,1)S(1)}, bf16[128,512]{1,0:T(8,128)(2,1)S(1)}, u32[]{:S(2)}, u32[]{:S(2)}) collective-permute-start(bf16[128,512]{1,0:T(8,128)(2,1)S(1)} %get-tuple-element.120.rest_0_), channel_id=1, source_target_pairs={{0,4},{4,0},{8,12},{12,8},{1,5},{5,1},{9,13},{13,9},{2,6},{6,2},{1... | collective-permute-start | bytes 393224 | tf_op jit(solution)/shard_map/ppermute | solution.py:69
  156.5 3.4 %collective-permute-start.38 = (bf16[128,512]{1,0:T(8,128)(2,1)S(1)}, bf16[128,512]{1,0:T(8,128)(2,1)S(1)}, u32[]{:S(2)}, u32[]{:S(2)}) collective-permute-start(bf16[128,512]{1,0:T(8,128)(2,1)S(1)} %get-tuple-element.122), channel_id=1, source_target_pairs={{0,1},{1,0},{4,8},{8,4},{5,9},{9,5},{12,13},{13,12},{2,3},{3,2},{6... | collective-permute-start | bytes 393224 | tf_op jit(solution)/shard_map/ppermute | solution.py:73
  156.6 6.9 %collective-permute-start.39 = (bf16[128,512]{1,0:T(8,128)(2,1)S(1)}, bf16[128,512]{1,0:T(8,128)(2,1)S(1)}, u32[]{:S(2)}, u32[]{:S(2)}) collective-permute-start(bf16[128,512]{1,0:T(8,128)(2,1)S(1)} %hop.36.rest_0_), channel_id=1, source_target_pairs={{0,4},{4,0},{8,12},{12,8},{1,5},{5,1},{9,13},{13,9},{2,6},{6,2},{1... | collective-permute-start | bytes 393224 | tf_op jit(solution)/shard_map/ppermute | solution.py:69
  159.9 5.4 %collective-permute-start.40 = (bf16[128,512]{1,0:T(8,128)(2,1)S(1)}, bf16[128,512]{1,0:T(8,128)(2,1)S(1)}, u32[]{:S(2)}, u32[]{:S(2)}) collective-permute-start(bf16[128,512]{1,0:T(8,128)(2,1)S(1)} %hop.37.rest_0_), channel_id=1, source_target_pairs={{0,4},{4,0},{8,12},{12,8},{1,5},{5,1},{9,13},{13,9},{2,6},{6,2},{1... | collective-permute-start | bytes 393224 | tf_op jit(solution)/shard_map/ppermute | solution.py:69
  166.1 2.0 %collective-permute-start.41 = (bf16[128,2048]{1,0:T(8,128)(2,1)S(1)}, bf16[128,2048]{1,0:T(8,128)(2,1)S(1)}, u32[]{:S(2)}, u32[]{:S(2)}) collective-permute-start(bf16[128,2048]{1,0:T(8,128)(2,1)S(1)} %broadcast_select_fusion.2), channel_id=1, source_target_pairs={{0,1},{1,0},{2,3},{3,2},{4,5},{5,4},{6,7},{7,6},{8,9},{9,8},{10,11... | collective-permute-start | bytes 1572872 | tf_op jit(solution)/shard_map/ppermute | solution.py:77
  168.3 8.4 %collective-permute-start.42 = (bf16[64,2048]{1,0:T(8,128)(2,1)S(1)}, bf16[64,2048]{1,0:T(8,128)(2,1)S(1)}, u32[]{:S(2)}, u32[]{:S(2)}) collective-permute-start(bf16[64,2048]{1,0:T(8,128)(2,1)S(1)} %slice.106), channel_id=1, source_target_pairs={{0,2},{2,0},{1,3},{3,1},{4,6},{6,4},{5,7},{7,5},{8,10},{10,8},{9,1... | collective-permute-start | bytes 786440 | tf_op jit(solution)/shard_map/ppermute | solution.py:77
  (2 other events, 26.0 us)

commit v4 on v3

--- a/solution.py
+++ b/solution.py
@@ -46,10 +46,10 @@
     return mixed.reshape(rows, heads * HD)
 
 
-WIDTH = 512
 LANES = 128
-TWO = 2 * WIDTH
-SCALE = 4
+WIDTH = 384
+PARTS = 1
+SCALE = 2
 OUTWARD = ((0, 1), (1, 0), (2, 3), (3, 2))
 ACROSS = ((0, 2), (2, 0), (1, 3), (3, 1))
 MIDDLE = ((0, 1), (1, 0), (2, 4), (4, 2), (3, 5), (5, 3), (6, 7), (7, 6))
@@ -77,8 +77,18 @@
     return lax.ppermute(a, axis, SWAP)
 
 
-def chunk_columns(k):
-    return TWO + (LANES if k == 0 else 0)
+class Chunk:
+    def __init__(self, index, first, units):
+        self.index, self.first, self.units = index, first, units
+        self.width = -(-units // LANES) * LANES
+        self.pair = 2 * self.width
+        self.columns = self.pair + (LANES if index == 0 else 0)
+
+
+def chunks_of(units):
+    count = max(units // WIDTH, 1)
+    starts = [k * WIDTH for k in range(count)] + [units]
+    return [Chunk(k, starts[k], starts[k + 1] - starts[k]) for k in range(count)]
 
 
 def in_three(total, shape):
@@ -96,16 +106,20 @@
     return total, in_three(total, a.shape)
 
 
-def attend_rows(query, new_key, new_value, key_cache, value_cache, lengths, residual, norm_gain):
-    rows, features = query.shape
+def attend_rows(part, parts, query, new_key, new_value, key_cache, value_cache, lengths, residual, norm_gain, after):
+    features = query.shape[1]
+    rows = query.shape[0] // parts
     heads = features // HD
     cache_len = key_cache.shape[1]
     block = 16
     tall, wide = heads * block, block * cache_len
+    begin = part * (rows // block)
     scale = 1.0 / HD**0.5
     held = functools.partial(pltpu.with_memory_space_constraint, memory_space=pltpu.HBM)
 
-    def kernel(length_ref, q_ref, nk_ref, nv_ref, k_ref, v_ref, res_ref, gain_ref, x_ref, scaled_ref, sparse):
+    def kernel(length_ref, q_ref, nk_ref, nv_ref, k_ref, v_ref, res_ref, gain_ref, *rest):
+        x_ref, scaled_ref, sparse = rest[-3:]
+
         @pl.when(pl.program_id(0) == 0)
         def _():
             sparse[...] = jnp.zeros_like(sparse)
@@ -125,7 +139,7 @@
         candidate = lax.broadcasted_iota(jnp.int32, (tall, 1), 0) % block
         span = jnp.zeros((tall, 1), jnp.int32)
         for c in range(block):
-            span = jnp.where(candidate == c, length_ref[pl.program_id(0) * block + c], span)
+            span = jnp.where(candidate == c, length_ref[(pl.program_id(0) + begin) * block + c], span)
         valid = (offset >= 0) & (offset < span)
         scores = jnp.where(valid, scores, -jnp.inf)
         top = jnp.maximum(jnp.max(scores, axis=1, keepdims=True), own)
@@ -144,8 +158,8 @@
             squares = squares + x * x
         scaled_ref[:, features:] = in_three(jnp.sum(squares, axis=1, keepdims=True), (block, LANES))
 
-    flat = pl.BlockSpec((block, features), lambda i: (i, 0))
-    cache = pl.BlockSpec((block, cache_len, features), lambda i: (i, 0, 0))
+    flat = pl.BlockSpec((block, features), lambda i: (begin + i, 0))
+    cache = pl.BlockSpec((block, cache_len, features), lambda i: (begin + i, 0, 0))
     return pl.pallas_call(
         kernel,
         grid=(rows // block,),
@@ -158,8 +172,9 @@
             cache,
             flat,
             pl.BlockSpec((1, features), lambda i: (0, 0)),
-        ],
-        out_specs=[flat, pl.BlockSpec((block, features + LANES), lambda i: (i, 0))],
+        ]
+        + [ANY] * len(after),
+        out_specs=[pl.BlockSpec((block, features), lambda i: (i, 0)), pl.BlockSpec((block, features + LANES), lambda i: (i, 0))],
         out_shape=[
             jax.ShapeDtypeStruct((rows, features), f32),
             jax.ShapeDtypeStruct((rows, features + LANES), bf16),
@@ -181,63 +196,112 @@
         held(value_cache),
         held(residual),
         norm_gain.reshape(1, -1),
+        *after,
     )
 
 
-def partial_products(k, rows, gate_rows, up_rows, after):
+def partial_products(chunk, rows, gate_rows, up_rows, after):
     count = rows.shape[0]
-    units = gate_rows.shape[0]
+    depth = gate_rows.shape[1]
     half = count // 2
-    valid = min(WIDTH, units - k * WIDTH)
-    step = 256
-    steps = WIDTH // step
-    depth = gate_rows.shape[1]
-    columns = chunk_columns(k)
-
-    def kernel(rows_ref, gate_ref, up_ref, *rest):
+    width, pair, columns = chunk.width, chunk.pair, chunk.columns
+    if chunk.first % WIDTH == 0 and width > WIDTH:
+        tiles = [(chunk.first + at, min(WIDTH, width - at)) for at in range(0, width, WIDTH)]
+    else:
+        tiles = [(chunk.first, width)]
+    if any(first % size for first, size in tiles):
+        tiles = [(chunk.first + at, LANES) for at in range(0, width, LANES)]
+
+    def kernel(rows_ref, *rest):
         out_ref, in_ref = rest[-2:]
-        i = pl.program_id(0)
-        if columns > TWO:
-            out_ref[:, TWO:] = rest[0][:half]
-            in_ref[:, TWO:] = rest[0][half:]
-        for weight, offset in ((gate_ref, 0), (up_ref, WIDTH)):
-            part = lax.dot_general(rows_ref[...], weight[...], (((1,), (1,)), ((), ())), preferred_element_type=f32)
-            if valid < WIDTH:
-                unit = lax.broadcasted_iota(jnp.int32, part.shape, 1) + i * step
-                part = jnp.where(unit < valid, part, 0.0)
-            part = part.astype(bf16)
-            at = pl.ds(pl.multiple_of(offset + i * step, step), step)
-            out_ref[:, at] = part[:half]
-            in_ref[:, at] = part[half:]
-
+        if columns > pair:
+            squares = rest[2 * len(tiles)]
+            out_ref[:, pair:] = squares[:half]
+            in_ref[:, pair:] = squares[half:]
+        for n, (first, size) in enumerate(tiles):
+            for weight, offset in ((rest[2 * n], 0), (rest[2 * n + 1], width)):
+                part = lax.dot_general(rows_ref[...], weight[...], (((1,), (1,)), ((), ())), preferred_element_type=f32)
+                begin = first - chunk.first
+                if begin + size > chunk.units:
+                    unit = lax.broadcasted_iota(jnp.int32, part.shape, 1) + begin
+                    part = jnp.where(unit < chunk.units, part, 0.0)
+                part = part.astype(bf16)
+                at = slice(offset + begin, offset + begin + size)
+                out_ref[:, at] = part[:half]
+                in_ref[:, at] = part[half:]
+
+    brief = 0.5 if chunk.index < 2 else 1
     shape = jax.ShapeDtypeStruct((half, columns), bf16)
-    first = k * steps
+    weights, specs = [], []
+    for first, size in tiles:
+        weights += [gate_rows, up_rows]
+        specs += [pl.BlockSpec((size, depth), functools.partial(lambda at, i: (at, 0), first // size))] * 2
     return pl.pallas_call(
         kernel,
-        grid=(steps,),
-        in_specs=[
-            pl.BlockSpec((count, depth), lambda i: (0, 0)),
-            pl.BlockSpec((step, depth), lambda i: (first + i, 0)),
-            pl.BlockSpec((step, depth), lambda i: (first + i, 0)),
-        ]
-        + ([pl.BlockSpec((count, LANES), lambda i: (0, depth // LANES))] if columns > TWO else [])
+        grid=(1,),
+        in_specs=[pl.BlockSpec((count, depth), lambda i: (0, 0))]
+        + specs
+        + ([pl.BlockSpec((count, LANES), lambda i: (0, depth // LANES))] if columns > pair else [])
         + [ANY] * len(after),
         out_specs=[pl.BlockSpec((half, columns), lambda i: (0, 0))] * 2,
         out_shape=[shape, shape],
         compiler_params=pltpu.CompilerParams(vmem_limit_bytes=24 << 20),
-        cost_estimate=cost(4 * count * depth * WIDTH, 4 * depth * WIDTH + 6 * count * WIDTH),
+        cost_estimate=cost(brief * 4 * count * depth * width, brief * (4 * depth * width + 6 * count * width)),
         name="partial_products",
-    )(rows, gate_rows, up_rows, *([rows] if columns > TWO else []), *after)
-
-
-def hop(outer, inv_in, s, t, count, got_e, got_m, part_out, part_in, after):
+    )(rows, *weights, *([rows] if columns > pair else []), *after)
+
+
+def twin_products(chunks, rows, gate_rows, up_rows, after):
+    count = rows.shape[0]
+    depth = gate_rows.shape[1]
+    half = count // 2
+    width = chunks[0].width
+
+    def kernel(rows_ref, gate_ref, up_ref, *rest):
+        outs = rest[-2 * len(chunks) :]
+        parts = []
+        for weight in (gate_ref, up_ref):
+            part = lax.dot_general(rows_ref[...], weight[...], (((1,), (1,)), ((), ())), preferred_element_type=f32)
+            parts.append(part.astype(bf16))
+        for c in range(len(chunks)):
+
+            @pl.when(pl.program_id(0) == c)
+            def _():
+                for offset, part in zip((0, width), parts):
+                    outs[2 * c][:, offset : offset + width] = part[:half]
+                    outs[2 * c + 1][:, offset : offset + width] = part[half:]
+
+    brief = 0.5 if chunks[0].index < 4 else 1
+    first = chunks[0].first // width
+    return pl.pallas_call(
+        kernel,
+        grid=(len(chunks),),
+        in_specs=[
+            pl.BlockSpec((count, depth), lambda i: (0, 0)),
+            pl.BlockSpec((width, depth), lambda i: (first + i, 0)),
+            pl.BlockSpec((width, depth), lambda i: (first + i, 0)),
+        ]
+        + [ANY] * len(after),
+        out_specs=[pl.BlockSpec((half, 2 * width), lambda i: (0, 0))] * (2 * len(chunks)),
+        out_shape=[jax.ShapeDtypeStruct((half, 2 * width), bf16)] * (2 * len(chunks)),
+        compiler_params=pltpu.CompilerParams(vmem_limit_bytes=24 << 20),
+        cost_estimate=cost(brief * 8 * count * depth * width, brief * (8 * depth * width + 12 * count * width)),
+        name="twin_products",
+    )(rows, gate_rows, up_rows, *after)
+
+
+def hop(outer, inv_in, stream, t, got_e, got_m, part_out, part_in, after):
     half = part_out[0].shape[0]
+    count = len(stream)
 
     def inside(j):
         return 0 <= j < count
 
     def columns(*js):
-        return max([chunk_columns(2 * j + s) for j in js if inside(j)], default=0)
+        return max([stream[j].columns for j in js if inside(j)], default=0)
+
+    def wide(*js):
+        return max([stream[j].width for j in js if inside(j)], default=0)
 
     def hid_e(step):
         return inside(step - 3) or inside(step - 5)
@@ -259,7 +323,7 @@
         add("out", part_out[t])
     if inside(t - 1):
         add("in1", part_in[t - 1])
-    starts_inv = inside(t - 2) and columns(t - 2) > TWO
+    starts_inv = inside(t - 2) and stream[t - 2].columns > stream[t - 2].pair
     if inside(t - 2):
         add("in2", part_in[t - 2])
         if not starts_inv:
@@ -269,10 +333,10 @@
     nxt = t + 1
     hid_at_e = columns(nxt, nxt - 2)
     hid_at_got_e = columns(t, t - 2)
-    width_e = hid_at_e + (WIDTH if hid_e(nxt) else 0)
+    width_e = hid_at_e + wide(nxt - 3, nxt - 5)
     hid_at_m = columns(t)
     hid_at_got_m = columns(t - 1)
-    width_m = hid_at_m + (WIDTH if inside(t - 3) else 0)
+    width_m = hid_at_m + wide(t - 3)
     widths = [w for w in (width_e, width_m) if w]
 
     def kernel(*refs):
@@ -282,35 +346,40 @@
         to_m = outs.pop(0) if width_m else None
 
         def both(own, received, to, j):
-            to[:, :TWO] = (own[:, :TWO].astype(f32) + received[:, :TWO].astype(f32)).astype(bf16)
-            if columns(j) > TWO:
-                to[:, TWO : columns(j)] = add_in_three(own[:, TWO:], received[:, TWO : columns(j)])[1]
+            pair, end = stream[j].pair, stream[j].columns
+            to[:, :pair] = (own[:, :pair].astype(f32) + received[:, :pair].astype(f32)).astype(bf16)
+            if end > pair:
+                to[:, pair:end] = add_in_three(own[:, pair:], received[:, pair:end])[1]
 
         @pl.when(r["outer"][0] != 0)
         def _():
             if inside(t + 1):
-                to_e[:, :TWO] = r["next_out"][:, :TWO]
+                pair = stream[t + 1].pair
+                to_e[:, :pair] = r["next_out"][:, :pair]
             if inside(t - 2):
+                w, pair = stream[t - 2].width, stream[t - 2].pair
                 if starts_inv:
-                    squares, _ = add_in_three(r["in2"][:, TWO:], r["got_e"][:, TWO : TWO + LANES])
+                    squares, _ = add_in_three(r["in2"][:, pair:], r["got_e"][:, pair : pair + LANES])
                     inv = lax.rsqrt(squares / D + eps)
                     outs[0][...] = inv
                 else:
                     inv = r["inv"][...]
-                gate = (r["in2"][:, :WIDTH].astype(f32) + r["got_e"][:, :WIDTH].astype(f32)) * inv
-                up = (r["in2"][:, WIDTH:TWO].astype(f32) + r["got_e"][:, WIDTH:TWO].astype(f32)) * inv
-                to_e[:, hid_at_e : hid_at_e + WIDTH] = (gate / (1.0 + jnp.exp(-gate)) * up).astype(bf16)
+                gate = (r["in2"][:, :w].astype(f32) + r["got_e"][:, :w].astype(f32)) * inv
+                up = (r["in2"][:, w:pair].astype(f32) + r["got_e"][:, w:pair].astype(f32)) * inv
+                to_e[:, hid_at_e : hid_at_e + w] = (gate / (1.0 + jnp.exp(-gate)) * up).astype(bf16)
 
         @pl.when(r["outer"][0] == 0)
         def _():
             if inside(t - 1):
                 both(r["in1"], r["got_m"], to_e, t - 1)
             if inside(t - 4):
-                to_e[:, hid_at_e : hid_at_e + WIDTH] = r["got_m"][:, hid_at_got_m : hid_at_got_m + WIDTH]
+                w = stream[t - 4].width
+                to_e[:, hid_at_e : hid_at_e + w] = r["got_m"][:, hid_at_got_m : hid_at_got_m + w]
             if inside(t):
                 both(r["out"], r["got_e"], to_m, t)
             if inside(t - 3):
-                to_m[:, hid_at_m : hid_at_m + WIDTH] = r["got_e"][:, hid_at_got_e : hid_at_got_e + WIDTH]
+                w = stream[t - 3].width
+                to_m[:, hid_at_m : hid_at_m + w] = r["got_e"][:, hid_at_got_e : hid_at_got_e + w]
             if starts_inv:
                 outs[0][...] = jnp.zeros(outs[0].shape, f32)
 
@@ -323,7 +392,7 @@
         out_specs=[VMEM] * len(shapes),
         out_shape=shapes,
         compiler_params=pltpu.CompilerParams(vmem_limit_bytes=24 << 20),
-        cost_estimate=cost(8 * half * TWO, 10 * half * TWO),
+        cost_estimate=cost(16 * half * WIDTH, 20 * half * WIDTH),
         name="hop",
     )(*operands)
     outs = list(outs)
@@ -332,7 +401,7 @@
     return to_e, to_m, outs[0] if outs else inv_in
 
 
-def hidden_rows(outer, buffers, after):
+def hidden_rows(outer, width, buffers, after):
     half = buffers[0][0].shape[0]
 
     def kernel(outer_ref, sent, got, from_m, late, *rest):
@@ -340,27 +409,27 @@
 
         @pl.when(outer_ref[0] != 0)
         def _():
-            hid[:half] = late[:, buffers[3][1] : buffers[3][1] + WIDTH]
-            hid[half:] = sent[:, buffers[0][1] : buffers[0][1] + WIDTH]
+            hid[:half] = late[:, buffers[3][1] : buffers[3][1] + width]
+            hid[half:] = sent[:, buffers[0][1] : buffers[0][1] + width]
 
         @pl.when(outer_ref[0] == 0)
         def _():
-            hid[:half] = from_m[:, buffers[2][1] : buffers[2][1] + WIDTH]
-            hid[half:] = got[:, buffers[1][1] : buffers[1][1] + WIDTH]
+            hid[:half] = from_m[:, buffers[2][1] : buffers[2][1] + width]
+            hid[half:] = got[:, buffers[1][1] : buffers[1][1] + width]
 
     return pl.pallas_call(
         kernel,
         in_specs=[SMEM] + [VMEM] * 4 + [ANY] * len(after),
         out_specs=VMEM,
-        out_shape=jax.ShapeDtypeStruct((2 * half, WIDTH), bf16),
+        out_shape=jax.ShapeDtypeStruct((2 * half, width), bf16),
         compiler_params=pltpu.CompilerParams(vmem_limit_bytes=24 << 20),
         name="hidden_rows",
     )(outer, *[buffer for buffer, _ in buffers], *after)
 
 
-def down_product(total, k, hidden, w_down):
-    first, last = k * WIDTH, min((k + 1) * WIDTH, w_down.shape[0])
-    term = jnp.dot(hidden[:, : last - first], w_down[first:last], preferred_element_type=f32)
+def down_product(total, chunk, hidden, w_down):
+    weight = w_down[chunk.first : chunk.first + chunk.units]
+    term = jnp.dot(hidden[:, : chunk.units], weight, preferred_element_type=f32)
     return term if total is None else total + term
 
 
@@ -369,27 +438,31 @@
     left = place < 2
     outer = ((place == 0) | (place == 3)).astype(jnp.int32).reshape(1)
 
-    across = swap(scaled, "ffn")
-    beside = swap(scaled, "pair")
-    diagonal = swap(across, "pair")
-    here = jnp.concatenate([scaled, across])
-    there = jnp.concatenate([beside, diagonal])
+    across = [swap(part, "ffn") for part in scaled]
+    beside = [swap(part, "pair") for part in scaled]
+    diagonal = [swap(part, "pair") for part in across]
+    here = jnp.concatenate(scaled + across)
+    there = jnp.concatenate(beside + diagonal)
     rows = jnp.concatenate([jnp.where(left, here, there), jnp.where(left, there, here)])
     half = here.shape[0]
 
     gate_rows = pltpu.with_memory_space_constraint(w_gate.T, pltpu.HBM)
     up_rows = pltpu.with_memory_space_constraint(w_up.T, pltpu.HBM)
-    chunks = -(-gate_rows.shape[0] // WIDTH)
-    counts = (-(-chunks // 2), chunks // 2)
+    chunks = chunks_of(gate_rows.shape[0])
+    streams = (chunks[0::2], chunks[1::2])
     part_out, part_in = ({}, {}), ({}, {})
     sent, got = {}, {}
 
     def products(k, after):
-        if k < chunks:
-            a, b = partial_products(k, rows, gate_rows, up_rows, after)
-            part_out[k % 2][k // 2], part_in[k % 2][k // 2] = a, b
-            return [a]
-        return after
+        if k >= len(chunks) or k // 2 in part_out[k % 2]:
+            return after
+        if k >= 2 and k % 2 == 0 and k + 1 < len(chunks) and chunks[k + 1].units == chunks[k].width:
+            made = twin_products(chunks[k : k + 2], rows, gate_rows, up_rows, after)
+            part_out[1][k // 2], part_in[1][k // 2] = made[2:]
+        else:
+            made = partial_products(chunks[k], rows, gate_rows, up_rows, after)
+        part_out[k % 2][k // 2], part_in[k % 2][k // 2] = made[:2]
+        return [made[0]]
 
     def send(s, t, to_e, to_m):
         sent["e", s, t], sent["m", s, t] = to_e, to_m
@@ -401,22 +474,21 @@
         return [sent["e", s, j + 3], got["e", s, j + 3], got["m", s, j + 4], got["e", s, j + 5]]
 
     after = products(0, [])
-    send(0, 0, (part_out[0][0], TWO), None)
+    send(0, 0, (part_out[0][0], 0), None)
     after = products(1, after)
-    send(1, 0, (part_out[1][0], TWO), None)
+    send(1, 0, (part_out[1][0], 0), None)
     after = products(2, after)
     total, inv_in = None, None
-    for t in range(counts[0] + 5):
+    for t in range(len(streams[0]) + 5):
         for s in (0, 1):
-            count = counts[s]
+            count = len(streams[s])
             if t < count + 4:
                 got_e, got_m = got["e", s, t], got["m", s, t]
                 to_e, to_m, inv_in = hop(
                     outer,
                     inv_in,
-                    s,
+                    streams[s],
                     t,
-                    count,
                     got_e and got_e[0],
                     got_m and got_m[0],
                     part_out[s],
@@ -425,11 +497,14 @@
                 )
                 send(s, t + 1, to_e, to_m)
                 after = [(to_e or to_m)[0]]
-            after = products(2 * t + s + 3, after)
+            k = 2 * t + s + 3
+            if k < len(chunks) and k // 2 in part_out[k % 2]:
+                k += 1
+            after = products(k, after)
             if 0 <= t - 5 < count:
                 k = 2 * (t - 5) + s
-                hidden = hidden_rows(outer, hidden_of(k), after + ([] if total is None else [total]))
-                total = down_product(total, k, hidden, w_down)
+                hidden = hidden_rows(outer, chunks[k].width, hidden_of(k), after + ([] if total is None else [total]))
+                total = down_product(total, chunks[k], hidden, w_down)
                 after = [hidden]
     total = total.astype(bf16)
     far, near = total[:half], total[half:]
@@ -470,9 +545,25 @@
     w_down,
 ):
     if on_line:
-        x, scaled = attend_rows(
-            query, new_key, new_value, key_cache, value_cache, lengths, residual, norm_gain
-        )
+        xs, scaled, after = [], [], []
+        for part in range(PARTS):
+            x, ready = attend_rows(
+                part,
+                PARTS,
+                query,
+                new_key,
+                new_value,
+                key_cache,
+                value_cache,
+                lengths,
+                residual,
+                norm_gain,
+                after,
+            )
+            xs.append(x)
+            scaled.append(ready)
+            after = [ready]
+        x = jnp.concatenate(xs)
         mlp = mlp_line(scaled, w_gate, w_up, w_down)
     else:
         x = residual.astype(f32) + attend(query, new_key, new_value, key_cache, value_cache, lengths)

time: 178 us -> 171 us (0.961)
  waiting for transfers between devices: 64.1 us -> 57.4 us
  starting transfers between devices: 52.3 us -> 45.8 us
  Pallas kernels: 49.1 us -> 51.7 us
  local copies, waits for them, and re-layouts: 1.49 us -> 3.7 us
  matrix products: 7.86 us -> 9.93 us
    ppermute x21 -> x24, waiting for transfers between devices: 47.8 us -> 41.1 us  [outward(): return lax.ppermute(a, 'mix', OUTWARD)]
    ppermute x21 -> x24, starting transfers between devices: 47 us -> 40.4 us  [outward(): return lax.ppermute(a, 'mix', OUTWARD)]
    unnamed x16, local copies, waits for them, and re-layouts: 0.72 us -> 2.92 us
    dot_general x11 -> x14, matrix products: 7.86 us -> 9.93 us  [down_product(): term = jnp.dot(hidden[:, :chunk.units], weight, preferred_element_type=f32)]
    pallas_call x11 -> x9, Pallas kernels: 34.2 us -> 36.2 us  [the longest x5 22.6 us: twin_products(): pl.pallas_call(kernel, grid=(len(chunks),), in_specs=[pl.BlockSpec((count...]
  transfers between devices with their start and end apart: 43 -> 49, of which waited for: 19 -> 19; matrix products, arithmetic and copies ran while one was open for 4% -> 5% of each run, Pallas kernels for 17% -> 21%
where the time goes in v4:
time: 171 us
  waiting for transfers between devices  57.4 us (34%)
  Pallas kernels  51.7 us (30%)
  starting transfers between devices  45.8 us (27%)
  matrix products  9.93 us (6%)
  local copies, waits for them, and re-layouts  3.7 us (2%)
    ppermute x24, waiting for transfers between devices, outward(): return lax.ppermute(a, 'mix', OUTWARD)  41.1 us
    ppermute x24, starting transfers between devices, outward(): return lax.ppermute(a, 'mix', OUTWARD)  40.4 us
    pallas_call x5, Pallas kernels, twin_products(): pl.pallas_call(kernel, grid=(len(chunks),), in_specs=[pl.BlockSpec((count...  22.6 us
    ppermute x5, waiting for transfers between devices, swap(): return lax.ppermute(a, axis, SWAP)  16.2 us
    pallas_call x4, Pallas kernels, partial_products(): pl.pallas_call(kernel, grid=(1,), in_specs=[pl.BlockSpec((count, depth),...  13.7 us
    pallas_call x1, Pallas kernels, attend_rows(): pl.pallas_call(kernel, grid=(rows // block,), in_specs=[SMEM, flat, flat,...  12.4 us
    dot_general x14, matrix products, down_product(): term = jnp.dot(hidden[:, :chunk.units], weight, preferred_element_type=f32)  9.93 us
    ppermute x5, starting transfers between devices, swap(): return lax.ppermute(a, axis, SWAP)  4.65 us
  transfers between devices with their start and end apart: 49, of which 19 were waited for; matrix products, arithmetic and copies ran while one was open for 5% of the time, Pallas kernels for 21%

profile of v4, /device:TPU:0, one launch (start us, length us, event | category | flops | bytes accessed | tf_op | source)
XLA Modules:
  0.0 171.2 jit_solution(3535703010835889857)
XLA Ops:
  1.3 12.4 %attend_rows.1 = (f32[64,2048]{1,0:T(8,128)S(1)}, bf16[64,2176]{1,0:T(8,128)(2,1)S(1)}) custom-call(s32[64]{0:T(128)S(1)} %copy-done, bf16[64,2048]{1,0:T(8,128)(2,1)} %q_ref.1, bf16[64,2048]{1,0:T(8,128)(2,1)} %nk_ref.1, bf16[64,2048]{1,0:T(8,128)(2,1)} %nv_ref.1, bf16[64,32,2048]{2,1,0:T(8,128)(2,1)} %k_ref.1, bf16[64,32,2048]{2,1,0:T(8,128)(2,1)} %v_ref.1, ...), custom_call_target="tpu_custom_call" | custom-call | flops 4294967296 | bytes 16777216 | tf_op jit(solution)/shard_map/attend_rows/pallas_call | solution.py:163
  13.8 3.0 %collective-permute-start = (bf16[64,2176]{1,0:T(8,128)(2,1)S(1)}, bf16[64,2176]{1,0:T(8,128)(2,1)S(1)}, u32[]{:S(2)}, u32[]{:S(2)}) collective-permute-start(bf16[64,2176]{1,0:T(8,128)(2,1)S(1)} %get-tuple-element.77), channel_id=1, source_target_pairs={{0,2},{2,0},{1,3},{3,1},{4,6},{6,4},{5,7},{7,5},{8,10},{10,8},{9,1... | collective-permute-start | bytes 835592 | tf_op jit(solution)/shard_map/ppermute | solution.py:77
  16.8 6.6 %collective-permute-done = bf16[64,2176]{1,0:T(8,128)(2,1)S(1)} collective-permute-done((bf16[64,2176]{1,0:T(8,128)(2,1)S(1)}, bf16[64,2176]{1,0:T(8,128)(2,1)S(1)}, u32[]{:S(2)}, u32[]{:S(2)}) %collective-permute-start) | collective-permute-done | bytes 278560 | tf_op jit(solution)/shard_map/ppermute | solution.py:77
  23.5 1.5 collective-permute-done.2
  25.2 3.2 %partial_products.4 = (bf16[128,896]{1,0:T(8,128)(2,1)S(1)}, bf16[128,896]{1,0:T(8,128)(2,1)S(1)}) custom-call(bf16[256,2176]{1,0:T(8,128)(2,1)S(1)} %pad_maximum_fusion.rows_ref.rest_2_, bf16[5472,2048]{1,0:T(8,128)(2,1)} %bitcast.18, bf16[5472,2048]{1,0:T(8,128)(2,1)} %bitcast.28, bf16[256,2176]{1,0:T(8,128)(2,1)S(1)} %pad_maximum_fusion.rows_ref.rest_2_), custom_call_target="tpu_custom_call" | custom-call | flops 805306368 | bytes 3735552 | tf_op jit(solution)/shard_map/partial_products/pallas_call | solution.py:239
  28.5 1.9 %collective-permute-start.3 = (bf16[128,896]{1,0:T(8,128)(2,1)S(1)}, bf16[128,896]{1,0:T(8,128)(2,1)S(1)}, u32[]{:S(2)}, u32[]{:S(2)}) collective-permute-start(bf16[128,896]{1,0:T(8,128)(2,1)S(1)} %get-tuple-element.78.rest_2_.refs_3_), channel_id=1, source_target_pairs={{0,4},{4,0},{8,12},{12,8},{1,5},{5,1},{9,13},{13,9},{2,6},{6,2},{1... | collective-permute-start | bytes 688136 | tf_op jit(solution)/shard_map/ppermute | solution.py:69
  30.4 3.2 %partial_products.5 = (bf16[128,768]{1,0:T(8,128)(2,1)S(1)}, bf16[128,768]{1,0:T(8,128)(2,1)S(1)}) custom-call(bf16[256,2176]{1,0:T(8,128)(2,1)S(1)} %pad_maximum_fusion.rows_ref.rest_2_, bf16[5472,2048]{1,0:T(8,128)(2,1)} %bitcast.19, bf16[5472,2048]{1,0:T(8,128)(2,1)} %bitcast.29, bf16[128,896]{1,0:T(8,128)(2,1)S(1)} %get-tuple-element.78.rest_2_.refs_3_), custom_call_target="tpu_custom_call" | custom-call | flops 805306368 | bytes 3735552 | tf_op jit(solution)/shard_map/partial_products/pallas_call | solution.py:239
  33.8 4.5 %twin_products.5 = (bf16[128,768]{1,0:T(8,128)(2,1)S(1)}, bf16[128,768]{1,0:T(8,128)(2,1)S(1)}, bf16[128,768]{1,0:T(8,128)(2,1)S(1)}, bf16[128,768]{1,0:T(8,128)(2,1)S(1)}) custom-call(bf16[256,2176]{1,0:T(8,128)(2,1)S(1)} %pad_maximum_fusion.rows_ref.rest_2_, bf16[5472,2048]{1,0:T(8,128)(2,1)} %bitcast.20, bf16[5472,2048]{1,0:T(8,128)(2,1)} %bitcast.30, ...), custom_call_target="tpu_custom_call" | custom-call | flops 1610612736 | bytes 7471104 | tf_op jit(solution)/shard_map/twin_products/pallas_call | solution.py:276
  38.5 3.5 %collective-permute-start.4 = (bf16[128,768]{1,0:T(8,128)(2,1)S(1)}, bf16[128,768]{1,0:T(8,128)(2,1)S(1)}, u32[]{:S(2)}, u32[]{:S(2)}) collective-permute-start(bf16[128,768]{1,0:T(8,128)(2,1)S(1)} %get-tuple-element.81.rest_0_), channel_id=1, source_target_pairs={{0,4},{4,0},{8,12},{12,8},{1,5},{5,1},{9,13},{13,9},{2,6},{6,2},{1... | collective-permute-start | bytes 589832 | tf_op jit(solution)/shard_map/ppermute | solution.py:69
  41.9 4.5 %twin_products.6 = (bf16[128,768]{1,0:T(8,128)(2,1)S(1)}, bf16[128,768]{1,0:T(8,128)(2,1)S(1)}, bf16[128,768]{1,0:T(8,128)(2,1)S(1)}, bf16[128,768]{1,0:T(8,128)(2,1)S(1)}) custom-call(bf16[256,2176]{1,0:T(8,128)(2,1)S(1)} %pad_maximum_fusion.rows_ref.rest_2_, bf16[5472,2048]{1,0:T(8,128)(2,1)} %bitcast.21, bf16[5472,2048]{1,0:T(8,128)(2,1)} %bitcast.31, ...), custom_call_target="tpu_custom_call" | custom-call | flops 3221225472 | bytes 14942208 | tf_op jit(solution)/shard_map/twin_products/pallas_call | solution.py:276
  46.6 1.6 collective-permute-start.9
  48.9 4.5 %twin_products.7 = (bf16[128,768]{1,0:T(8,128)(2,1)S(1)}, bf16[128,768]{1,0:T(8,128)(2,1)S(1)}, bf16[128,768]{1,0:T(8,128)(2,1)S(1)}, bf16[128,768]{1,0:T(8,128)(2,1)S(1)}) custom-call(bf16[256,2176]{1,0:T(8,128)(2,1)S(1)} %pad_maximum_fusion.rows_ref.rest_2_, bf16[5472,2048]{1,0:T(8,128)(2,1)} %bitcast.22, bf16[5472,2048]{1,0:T(8,128)(2,1)} %bitcast.32, ...), custom_call_target="tpu_custom_call" | custom-call | flops 3221225472 | bytes 14942208 | tf_op jit(solution)/shard_map/twin_products/pallas_call | solution.py:276
  54.4 1.7 %collective-permute-start.13 = (bf16[128,768]{1,0:T(8,128)(2,1)S(1)}, bf16[128,768]{1,0:T(8,128)(2,1)S(1)}, u32[]{:S(2)}, u32[]{:S(2)}) collective-permute-start(bf16[128,768]{1,0:T(8,128)(2,1)S(1)} %get-tuple-element.94.refs_7_), channel_id=1, source_target_pairs={{0,4},{4,0},{8,12},{12,8},{1,5},{5,1},{9,13},{13,9},{2,6},{6,2},{1... | collective-permute-start | bytes 589832 | tf_op jit(solution)/shard_map/ppermute | solution.py:69
  56.1 3.1 %collective-permute-done.7.refs_1_ = bf16[128,896]{1,0:T(8,128)(2,1)S(1)} collective-permute-done((bf16[128,896]{1,0:T(8,128)(2,1)S(1)}, bf16[128,896]{1,0:T(8,128)(2,1)S(1)}, u32[]{:S(2)}, u32[]{:S(2)}) %collective-permute-start.7) | collective-permute-done | bytes 229408 | tf_op jit(solution)/shard_map/ppermute | solution.py:69
  59.5 1.6 collective-permute-start.11
  61.0 4.5 %twin_products.8 = (bf16[128,768]{1,0:T(8,128)(2,1)S(1)}, bf16[128,768]{1,0:T(8,128)(2,1)S(1)}, bf16[128,768]{1,0:T(8,128)(2,1)S(1)}, bf16[128,768]{1,0:T(8,128)(2,1)S(1)}) custom-call(bf16[256,2176]{1,0:T(8,128)(2,1)S(1)} %pad_maximum_fusion.rows_ref.rest_2_, bf16[5472,2048]{1,0:T(8,128)(2,1)} %bitcast.23, bf16[5472,2048]{1,0:T(8,128)(2,1)} %bitcast.33, ...), custom_call_target="tpu_custom_call" | custom-call | flops 3221225472 | bytes 14942208 | tf_op jit(solution)/shard_map/twin_products/pallas_call | solution.py:276
  66.7 3.0 %collective-permute-done.11.refs_1_.got = bf16[128,1152]{1,0:T(8,128)(2,1)S(1)} collective-permute-done((bf16[128,1152]{1,0:T(8,128)(2,1)S(1)}, bf16[128,1152]{1,0:T(8,128)(2,1)S(1)}, u32[]{:S(2)}, u32[]{:S(2)}) %collective-permute-start.11) | collective-permute-done | bytes 294944 | tf_op jit(solution)/shard_map/ppermute | solution.py:69
  70.1 1.8 %collective-permute-start.16 = (bf16[128,1152]{1,0:T(8,128)(2,1)S(1)}, bf16[128,1152]{1,0:T(8,128)(2,1)S(1)}, u32[]{:S(2)}, u32[]{:S(2)}) collective-permute-start(bf16[128,1152]{1,0:T(8,128)(2,1)S(1)} %get-tuple-element.105.rest_0_.sent), channel_id=1, source_target_pairs={{0,4},{4,0},{8,12},{12,8},{1,5},{5,1},{9,13},{13,9},{2,6},{6,2},{1... | collective-permute-start | bytes 884744 | tf_op jit(solution)/shard_map/ppermute | solution.py:69
  71.9 4.5 %twin_products.9 = (bf16[128,768]{1,0:T(8,128)(2,1)S(1)}, bf16[128,768]{1,0:T(8,128)(2,1)S(1)}, bf16[128,768]{1,0:T(8,128)(2,1)S(1)}, bf16[128,768]{1,0:T(8,128)(2,1)S(1)}) custom-call(bf16[256,2176]{1,0:T(8,128)(2,1)S(1)} %pad_maximum_fusion.rows_ref.rest_2_, bf16[5472,2048]{1,0:T(8,128)(2,1)} %bitcast.24, bf16[5472,2048]{1,0:T(8,128)(2,1)} %bitcast.34, ...), custom_call_target="tpu_custom_call" | custom-call | flops 3221225472 | bytes 14942208 | tf_op jit(solution)/shard_map/twin_products/pallas_call | solution.py:276
  76.6 1.3 collective-permute-start.21
  77.9 4.5 %collective-permute-done.16.refs_1_.got = bf16[128,1152]{1,0:T(8,128)(2,1)S(1)} collective-permute-done((bf16[128,1152]{1,0:T(8,128)(2,1)S(1)}, bf16[128,1152]{1,0:T(8,128)(2,1)S(1)}, u32[]{:S(2)}, u32[]{:S(2)}) %collective-permute-start.16) | collective-permute-done | bytes 294944 | tf_op jit(solution)/shard_map/ppermute | solution.py:69
  82.5 1.7 collective-permute-start.19
  84.2 3.2 %partial_products.6 = (bf16[128,768]{1,0:T(8,128)(2,1)S(1)}, bf16[128,768]{1,0:T(8,128)(2,1)S(1)}) custom-call(bf16[256,2176]{1,0:T(8,128)(2,1)S(1)} %pad_maximum_fusion.rows_ref.rest_2_, bf16[5472,2048]{1,0:T(8,128)(2,1)} %bitcast.25, bf16[5472,2048]{1,0:T(8,128)(2,1)} %bitcast.35, bf16[128,1152]{1,0:T(8,128)(2,1)S(1)} %get-tuple-element.112.rest_2_.sent), custom_call_target="tpu_custom_call" | custom-call | flops 1610612736 | bytes 7471104 | tf_op jit(solution)/shard_map/partial_products/pallas_call | solution.py:239
  87.4 1.3 collective-permute-done.21.refs_1_.got
  88.8 1.7 collective-permute-start.23
  90.6 4.1 %partial_products.7 = (bf16[128,1024]{1,0:T(8,128)(2,1)S(1)}, bf16[128,1024]{1,0:T(8,128)(2,1)S(1)}) custom-call(bf16[256,2176]{1,0:T(8,128)(2,1)S(1)} %pad_maximum_fusion.rows_ref.rest_2_, bf16[5472,2048]{1,0:T(8,128)(2,1)} %bitcast.26, bf16[5472,2048]{1,0:T(8,128)(2,1)} %bitcast.36, bf16[5472,2048]{1,0:T(8,128)(2,1)} %bitcast.27, ...), custom_call_target="tpu_custom_call" | custom-call | flops 2147483648 | bytes 9961472 | tf_op jit(solution)/shard_map/partial_products/pallas_call | solution.py:239
  95.2 1.7 collective-permute-start.25
  99.8 1.5 collective-permute-done.23.refs_1_.late.got
  101.5 1.7 collective-permute-start.27
  103.9 3.7 %collective-permute-done.25.refs_1_.late.got = bf16[128,1152]{1,0:T(8,128)(2,1)S(1)} collective-permute-done((bf16[128,1152]{1,0:T(8,128)(2,1)S(1)}, bf16[128,1152]{1,0:T(8,128)(2,1)S(1)}, u32[]{:S(2)}, u32[]{:S(2)}) %collective-permute-start.25) | collective-permute-done | bytes 294944 | tf_op jit(solution)/shard_map/ppermute | solution.py:69
  107.8 1.7 collective-permute-start.29
  110.2 5.1 %collective-permute-done.27.refs_1_.late.got = bf16[128,1408]{1,0:T(8,128)(2,1)S(1)} collective-permute-done((bf16[128,1408]{1,0:T(8,128)(2,1)S(1)}, bf16[128,1408]{1,0:T(8,128)(2,1)S(1)}, u32[]{:S(2)}, u32[]{:S(2)}) %collective-permute-start.27) | collective-permute-done | bytes 360480 | tf_op jit(solution)/shard_map/ppermute | solution.py:69
  115.6 2.1 %collective-permute-start.31 = (bf16[128,1152]{1,0:T(8,128)(2,1)S(1)}, bf16[128,1152]{1,0:T(8,128)(2,1)S(1)}, u32[]{:S(2)}, u32[]{:S(2)}) collective-permute-start(bf16[128,1152]{1,0:T(8,128)(2,1)S(1)} %get-tuple-element.130.rest_0_.sent), channel_id=1, source_target_pairs={{0,4},{4,0},{8,12},{12,8},{1,5},{5,1},{9,13},{13,9},{2,6},{6,2},{1... | collective-permute-start | bytes 884744 | tf_op jit(solution)/shard_map/ppermute | solution.py:69
  118.5 3.2 %collective-permute-done.29.refs_1_.late.got = bf16[128,1152]{1,0:T(8,128)(2,1)S(1)} collective-permute-done((bf16[128,1152]{1,0:T(8,128)(2,1)S(1)}, bf16[128,1152]{1,0:T(8,128)(2,1)S(1)}, u32[]{:S(2)}, u32[]{:S(2)}) %collective-permute-start.29) | collective-permute-done | bytes 294944 | tf_op jit(solution)/shard_map/ppermute | solution.py:69
  121.8 1.6 collective-permute-start.33
  124.2 3.8 %collective-permute-done.31.refs_1_.late.got = bf16[128,1152]{1,0:T(8,128)(2,1)S(1)} collective-permute-done((bf16[128,1152]{1,0:T(8,128)(2,1)S(1)}, bf16[128,1152]{1,0:T(8,128)(2,1)S(1)}, u32[]{:S(2)}, u32[]{:S(2)}) %collective-permute-start.31) | collective-permute-done | bytes 294944 | tf_op jit(solution)/shard_map/ppermute | solution.py:69
  128.2 1.7 collective-permute-start.35
  130.7 3.7 %collective-permute-done.33.refs_1_.late.got = bf16[128,1152]{1,0:T(8,128)(2,1)S(1)} collective-permute-done((bf16[128,1152]{1,0:T(8,128)(2,1)S(1)}, bf16[128,1152]{1,0:T(8,128)(2,1)S(1)}, u32[]{:S(2)}, u32[]{:S(2)}) %collective-permute-start.33) | collective-permute-done | bytes 294944 | tf_op jit(solution)/shard_map/ppermute | solution.py:69
  134.5 1.6 collective-permute-start.37
  136.9 5.1 %collective-permute-done.35.refs_1_.late.got = bf16[128,1408]{1,0:T(8,128)(2,1)S(1)} collective-permute-done((bf16[128,1408]{1,0:T(8,128)(2,1)S(1)}, bf16[128,1408]{1,0:T(8,128)(2,1)S(1)}, u32[]{:S(2)}, u32[]{:S(2)}) %collective-permute-start.35) | collective-permute-done | bytes 360480 | tf_op jit(solution)/shard_map/ppermute | solution.py:69
  142.2 1.6 collective-permute-start.39
  147.3 2.8 %collective-permute-start.43 = (bf16[128,384]{1,0:T(8,128)(2,1)S(1)}, bf16[128,384]{1,0:T(8,128)(2,1)S(1)}, u32[]{:S(2)}, u32[]{:S(2)}) collective-permute-start(bf16[128,384]{1,0:T(8,128)(2,1)S(1)} %get-tuple-element.144.rest_0_), channel_id=1, source_target_pairs={{0,4},{4,0},{8,12},{12,8},{1,5},{5,1},{9,13},{13,9},{2,6},{6,2},{1... | collective-permute-start | bytes 294920 | tf_op jit(solution)/shard_map/ppermute | solution.py:69
  150.9 2.0 %collective-permute-start.45 = (bf16[128,384]{1,0:T(8,128)(2,1)S(1)}, bf16[128,384]{1,0:T(8,128)(2,1)S(1)}, u32[]{:S(2)}, u32[]{:S(2)}) collective-permute-start(bf16[128,384]{1,0:T(8,128)(2,1)S(1)} %hop.42.rest_0_), channel_id=1, source_target_pairs={{0,4},{4,0},{8,12},{12,8},{1,5},{5,1},{9,13},{13,9},{2,6},{6,2},{1... | collective-permute-start | bytes 294920 | tf_op jit(solution)/shard_map/ppermute | solution.py:69
  153.7 2.2 %collective-permute-start.46 = (bf16[128,512]{1,0:T(8,128)(2,1)S(1)}, bf16[128,512]{1,0:T(8,128)(2,1)S(1)}, u32[]{:S(2)}, u32[]{:S(2)}) collective-permute-start(bf16[128,512]{1,0:T(8,128)(2,1)S(1)} %hop.43.rest_0_), channel_id=1, source_target_pairs={{0,4},{4,0},{8,12},{12,8},{1,5},{5,1},{9,13},{13,9},{2,6},{6,2},{1... | collective-permute-start | bytes 393224 | tf_op jit(solution)/shard_map/ppermute | solution.py:69
  157.4 1.5 collective-permute-done.46.late
  159.8 1.9 %collective-permute-done.47 = bf16[128,2048]{1,0:T(8,128)(2,1)S(1)} collective-permute-done((bf16[128,2048]{1,0:T(8,128)(2,1)S(1)}, bf16[128,2048]{1,0:T(8,128)(2,1)S(1)}, u32[]{:S(2)}, u32[]{:S(2)}) %collective-permute-start.47) | collective-permute-done | bytes 524320 | tf_op jit(solution)/shard_map/ppermute | solution.py:77
  162.0 1.6 collective-permute-start.48
  164.2 6.2 %collective-permute-done.48 = bf16[64,2048]{1,0:T(8,128)(2,1)S(1)} collective-permute-done((bf16[64,2048]{1,0:T(8,128)(2,1)S(1)}, bf16[64,2048]{1,0:T(8,128)(2,1)S(1)}, u32[]{:S(2)}, u32[]{:S(2)}) %collective-permute-start.48) | collective-permute-done | bytes 262176 | tf_op jit(solution)/shard_map/ppermute | solution.py:77
  (137 shorter events, 23.5 us)
Async XLA Ops:
  13.8 9.7 %collective-permute-start = (bf16[64,2176]{1,0:T(8,128)(2,1)S(1)}, bf16[64,2176]{1,0:T(8,128)(2,1)S(1)}, u32[]{:S(2)}, u32[]{:S(2)}) collective-permute-start(bf16[64,2176]{1,0:T(8,128)(2,1)S(1)} %get-tuple-element.77), channel_id=1, source_target_pairs={{0,2},{2,0},{1,3},{3,1},{4,6},{6,4},{5,7},{7,5},{8,10},{10,8},{9,1... | collective-permute-start | bytes 835592 | tf_op jit(solution)/shard_map/ppermute | solution.py:77
  16.8 6.7 %collective-permute-start.1 = (bf16[64,2176]{1,0:T(8,128)(2,1)S(1)}, bf16[64,2176]{1,0:T(8,128)(2,1)S(1)}, u32[]{:S(2)}, u32[]{:S(2)}) collective-permute-start(bf16[64,2176]{1,0:T(8,128)(2,1)S(1)} %get-tuple-element.77), channel_id=1, source_target_pairs={{0,1},{1,0},{2,3},{3,2},{4,5},{5,4},{6,7},{7,6},{8,9},{9,8},{10,11... | collective-permute-start | bytes 835592 | tf_op jit(solution)/shard_map/ppermute | solution.py:77
  28.5 9.9 %collective-permute-start.3 = (bf16[128,896]{1,0:T(8,128)(2,1)S(1)}, bf16[128,896]{1,0:T(8,128)(2,1)S(1)}, u32[]{:S(2)}, u32[]{:S(2)}) collective-permute-start(bf16[128,896]{1,0:T(8,128)(2,1)S(1)} %get-tuple-element.78.rest_2_.refs_3_), channel_id=1, source_target_pairs={{0,4},{4,0},{8,12},{12,8},{1,5},{5,1},{9,13},{13,9},{2,6},{6,2},{1... | collective-permute-start | bytes 688136 | tf_op jit(solution)/shard_map/ppermute | solution.py:69
  33.6 12.9 %collective-permute-start.6 = (bf16[128,768]{1,0:T(8,128)(2,1)S(1)}, bf16[128,768]{1,0:T(8,128)(2,1)S(1)}, u32[]{:S(2)}, u32[]{:S(2)}) collective-permute-start(bf16[128,768]{1,0:T(8,128)(2,1)S(1)} %get-tuple-element.79.rest_0_.refs_3_), channel_id=1, source_target_pairs={{0,4},{4,0},{8,12},{12,8},{1,5},{5,1},{9,13},{13,9},{2,6},{6,2},{1... | collective-permute-start | bytes 589832 | tf_op jit(solution)/shard_map/ppermute | solution.py:69
  38.4 9.8 %collective-permute-start.5 = (bf16[128,896]{1,0:T(8,128)(2,1)S(1)}, bf16[128,896]{1,0:T(8,128)(2,1)S(1)}, u32[]{:S(2)}, u32[]{:S(2)}) collective-permute-start(bf16[128,896]{1,0:T(8,128)(2,1)S(1)} %get-tuple-element.82), channel_id=1, source_target_pairs={{0,1},{1,0},{4,8},{8,4},{5,9},{9,5},{12,13},{13,12},{2,3},{3,2},{6... | collective-permute-start | bytes 688136 | tf_op jit(solution)/shard_map/ppermute | solution.py:73
  38.5 9.7 %collective-permute-start.4 = (bf16[128,768]{1,0:T(8,128)(2,1)S(1)}, bf16[128,768]{1,0:T(8,128)(2,1)S(1)}, u32[]{:S(2)}, u32[]{:S(2)}) collective-permute-start(bf16[128,768]{1,0:T(8,128)(2,1)S(1)} %get-tuple-element.81.rest_0_), channel_id=1, source_target_pairs={{0,4},{4,0},{8,12},{12,8},{1,5},{5,1},{9,13},{13,9},{2,6},{6,2},{1... | collective-permute-start | bytes 589832 | tf_op jit(solution)/shard_map/ppermute | solution.py:69
  46.5 6.9 %collective-permute-start.10 = (bf16[128,768]{1,0:T(8,128)(2,1)S(1)}, bf16[128,768]{1,0:T(8,128)(2,1)S(1)}, u32[]{:S(2)}, u32[]{:S(2)}) collective-permute-start(bf16[128,768]{1,0:T(8,128)(2,1)S(1)} %get-tuple-element.91), channel_id=1, source_target_pairs={{0,1},{1,0},{4,8},{8,4},{5,9},{9,5},{12,13},{13,12},{2,3},{3,2},{6... | collective-permute-start | bytes 589832 | tf_op jit(solution)/shard_map/ppermute | solution.py:73
  46.6 7.8 %collective-permute-start.9 = (bf16[128,768]{1,0:T(8,128)(2,1)S(1)}, bf16[128,768]{1,0:T(8,128)(2,1)S(1)}, u32[]{:S(2)}, u32[]{:S(2)}) collective-permute-start(bf16[128,768]{1,0:T(8,128)(2,1)S(1)} %get-tuple-element.86.refs_6_), channel_id=1, source_target_pairs={{0,4},{4,0},{8,12},{12,8},{1,5},{5,1},{9,13},{13,9},{2,6},{6,2},{1... | collective-permute-start | bytes 589832 | tf_op jit(solution)/shard_map/ppermute | solution.py:69
  48.2 11.1 %collective-permute-start.7 = (bf16[128,896]{1,0:T(8,128)(2,1)S(1)}, bf16[128,896]{1,0:T(8,128)(2,1)S(1)}, u32[]{:S(2)}, u32[]{:S(2)}) collective-permute-start(bf16[128,896]{1,0:T(8,128)(2,1)S(1)} %get-tuple-element.87.rest_0_), channel_id=1, source_target_pairs={{0,4},{4,0},{8,12},{12,8},{1,5},{5,1},{9,13},{13,9},{2,6},{6,2},{1... | collective-permute-start | bytes 688136 | tf_op jit(solution)/shard_map/ppermute | solution.py:69
  48.9 7.2 %collective-permute-start.8 = (bf16[128,768]{1,0:T(8,128)(2,1)S(1)}, bf16[128,768]{1,0:T(8,128)(2,1)S(1)}, u32[]{:S(2)}, u32[]{:S(2)}) collective-permute-start(bf16[128,768]{1,0:T(8,128)(2,1)S(1)} %get-tuple-element.88), channel_id=1, source_target_pairs={{0,1},{1,0},{4,8},{8,4},{5,9},{9,5},{12,13},{13,12},{2,3},{3,2},{6... | collective-permute-start | bytes 589832 | tf_op jit(solution)/shard_map/ppermute | solution.py:73
  54.4 11.2 %collective-permute-start.13 = (bf16[128,768]{1,0:T(8,128)(2,1)S(1)}, bf16[128,768]{1,0:T(8,128)(2,1)S(1)}, u32[]{:S(2)}, u32[]{:S(2)}) collective-permute-start(bf16[128,768]{1,0:T(8,128)(2,1)S(1)} %get-tuple-element.94.refs_7_), channel_id=1, source_target_pairs={{0,4},{4,0},{8,12},{12,8},{1,5},{5,1},{9,13},{13,9},{2,6},{6,2},{1... | collective-permute-start | bytes 589832 | tf_op jit(solution)/shard_map/ppermute | solution.py:69
  56.1 9.5 %collective-permute-start.14 = (bf16[128,768]{1,0:T(8,128)(2,1)S(1)}, bf16[128,768]{1,0:T(8,128)(2,1)S(1)}, u32[]{:S(2)}, u32[]{:S(2)}) collective-permute-start(bf16[128,768]{1,0:T(8,128)(2,1)S(1)} %get-tuple-element.100), channel_id=1, source_target_pairs={{0,1},{1,0},{4,8},{8,4},{5,9},{9,5},{12,13},{13,12},{2,3},{3,2},{6... | collective-permute-start | bytes 589832 | tf_op jit(solution)/shard_map/ppermute | solution.py:73
  59.5 10.3 %collective-permute-start.11 = (bf16[128,1152]{1,0:T(8,128)(2,1)S(1)}, bf16[128,1152]{1,0:T(8,128)(2,1)S(1)}, u32[]{:S(2)}, u32[]{:S(2)}) collective-permute-start(bf16[128,1152]{1,0:T(8,128)(2,1)S(1)} %get-tuple-element.95.rest_0_.sent), channel_id=1, source_target_pairs={{0,4},{4,0},{8,12},{12,8},{1,5},{5,1},{9,13},{13,9},{2,6},{6,2},{1... | collective-permute-start | bytes 884744 | tf_op jit(solution)/shard_map/ppermute | solution.py:69
  61.0 5.7 %collective-permute-start.12 = (bf16[128,768]{1,0:T(8,128)(2,1)S(1)}, bf16[128,768]{1,0:T(8,128)(2,1)S(1)}, u32[]{:S(2)}, u32[]{:S(2)}) collective-permute-start(bf16[128,768]{1,0:T(8,128)(2,1)S(1)} %get-tuple-element.96), channel_id=1, source_target_pairs={{0,1},{1,0},{4,8},{8,4},{5,9},{9,5},{12,13},{13,12},{2,3},{3,2},{6... | collective-permute-start | bytes 589832 | tf_op jit(solution)/shard_map/ppermute | solution.py:73
  65.8 10.7 %collective-permute-start.17 = (bf16[128,1152]{1,0:T(8,128)(2,1)S(1)}, bf16[128,1152]{1,0:T(8,128)(2,1)S(1)}, u32[]{:S(2)}, u32[]{:S(2)}) collective-permute-start(bf16[128,1152]{1,0:T(8,128)(2,1)S(1)} %get-tuple-element.103.refs_8_.sent), channel_id=1, source_target_pairs={{0,4},{4,0},{8,12},{12,8},{1,5},{5,1},{9,13},{13,9},{2,6},{6,2},{1... | collective-permute-start | bytes 884744 | tf_op jit(solution)/shard_map/ppermute | solution.py:69
  66.7 9.7 %collective-permute-start.18 = (bf16[128,768]{1,0:T(8,128)(2,1)S(1)}, bf16[128,768]{1,0:T(8,128)(2,1)S(1)}, u32[]{:S(2)}, u32[]{:S(2)}) collective-permute-start(bf16[128,768]{1,0:T(8,128)(2,1)S(1)} %get-tuple-element.108), channel_id=1, source_target_pairs={{0,1},{1,0},{4,8},{8,4},{5,9},{9,5},{12,13},{13,12},{2,3},{3,2},{6... | collective-permute-start | bytes 589832 | tf_op jit(solution)/shard_map/ppermute | solution.py:73
  70.1 7.8 %collective-permute-start.15 = (bf16[128,1152]{1,0:T(8,128)(2,1)S(1)}, bf16[128,1152]{1,0:T(8,128)(2,1)S(1)}, u32[]{:S(2)}, u32[]{:S(2)}) collective-permute-start(bf16[128,1152]{1,0:T(8,128)(2,1)S(1)} %get-tuple-element.104), channel_id=1, source_target_pairs={{0,1},{1,0},{4,8},{8,4},{5,9},{9,5},{12,13},{13,12},{2,3},{3,2},{6... | collective-permute-start | bytes 884744 | tf_op jit(solution)/shard_map/ppermute | solution.py:73
  70.1 12.2 %collective-permute-start.16 = (bf16[128,1152]{1,0:T(8,128)(2,1)S(1)}, bf16[128,1152]{1,0:T(8,128)(2,1)S(1)}, u32[]{:S(2)}, u32[]{:S(2)}) collective-permute-start(bf16[128,1152]{1,0:T(8,128)(2,1)S(1)} %get-tuple-element.105.rest_0_.sent), channel_id=1, source_target_pairs={{0,4},{4,0},{8,12},{12,8},{1,5},{5,1},{9,13},{13,9},{2,6},{6,2},{1... | collective-permute-start | bytes 884744 | tf_op jit(solution)/shard_map/ppermute | solution.py:69
  76.6 12.0 %collective-permute-start.21 = (bf16[128,1152]{1,0:T(8,128)(2,1)S(1)}, bf16[128,1152]{1,0:T(8,128)(2,1)S(1)}, u32[]{:S(2)}, u32[]{:S(2)}) collective-permute-start(bf16[128,1152]{1,0:T(8,128)(2,1)S(1)} %get-tuple-element.111.refs_8_.sent), channel_id=1, source_target_pairs={{0,4},{4,0},{8,12},{12,8},{1,5},{5,1},{9,13},{13,9},{2,6},{6,2},{1... | collective-permute-start | bytes 884744 | tf_op jit(solution)/shard_map/ppermute | solution.py:69
  77.9 10.8 %collective-permute-start.22 = (bf16[128,1152]{1,0:T(8,128)(2,1)S(1)}, bf16[128,1152]{1,0:T(8,128)(2,1)S(1)}, u32[]{:S(2)}, u32[]{:S(2)}) collective-permute-start(bf16[128,1152]{1,0:T(8,128)(2,1)S(1)} %get-tuple-element.116), channel_id=1, source_target_pairs={{0,1},{1,0},{4,8},{8,4},{5,9},{9,5},{12,13},{13,12},{2,3},{3,2},{6... | collective-permute-start | bytes 884744 | tf_op jit(solution)/shard_map/ppermute | solution.py:73
  82.5 12.5 %collective-permute-start.19 = (bf16[128,1152]{1,0:T(8,128)(2,1)S(1)}, bf16[128,1152]{1,0:T(8,128)(2,1)S(1)}, u32[]{:S(2)}, u32[]{:S(2)}) collective-permute-start(bf16[128,1152]{1,0:T(8,128)(2,1)S(1)} %get-tuple-element.112.rest_2_.sent), channel_id=1, source_target_pairs={{0,4},{4,0},{8,12},{12,8},{1,5},{5,1},{9,13},{13,9},{2,6},{6,2},{1... | collective-permute-start | bytes 884744 | tf_op jit(solution)/shard_map/ppermute | solution.py:69
  84.2 10.8 %collective-permute-start.20 = (bf16[128,1152]{1,0:T(8,128)(2,1)S(1)}, bf16[128,1152]{1,0:T(8,128)(2,1)S(1)}, u32[]{:S(2)}, u32[]{:S(2)}) collective-permute-start(bf16[128,1152]{1,0:T(8,128)(2,1)S(1)} %get-tuple-element.113), channel_id=1, source_target_pairs={{0,1},{1,0},{4,8},{8,4},{5,9},{9,5},{12,13},{13,12},{2,3},{3,2},{6... | collective-permute-start | bytes 884744 | tf_op jit(solution)/shard_map/ppermute | solution.py:73
  88.8 12.5 %collective-permute-start.23 = (bf16[128,1152]{1,0:T(8,128)(2,1)S(1)}, bf16[128,1152]{1,0:T(8,128)(2,1)S(1)}, u32[]{:S(2)}, u32[]{:S(2)}) collective-permute-start(bf16[128,1152]{1,0:T(8,128)(2,1)S(1)} %get-tuple-element.119.rest_4_.sent), channel_id=1, source_target_pairs={{0,4},{4,0},{8,12},{12,8},{1,5},{5,1},{9,13},{13,9},{2,6},{6,2},{1... | collective-permute-start | bytes 884744 | tf_op jit(solution)/shard_map/ppermute | solution.py:69
  90.6 10.8 %collective-permute-start.24 = (bf16[128,1152]{1,0:T(8,128)(2,1)S(1)}, bf16[128,1152]{1,0:T(8,128)(2,1)S(1)}, u32[]{:S(2)}, u32[]{:S(2)}) collective-permute-start(bf16[128,1152]{1,0:T(8,128)(2,1)S(1)} %get-tuple-element.122), channel_id=1, source_target_pairs={{0,1},{1,0},{4,8},{8,4},{5,9},{9,5},{12,13},{13,12},{2,3},{3,2},{6... | collective-permute-start | bytes 884744 | tf_op jit(solution)/shard_map/ppermute | solution.py:73
  95.2 12.5 %collective-permute-start.25 = (bf16[128,1152]{1,0:T(8,128)(2,1)S(1)}, bf16[128,1152]{1,0:T(8,128)(2,1)S(1)}, u32[]{:S(2)}, u32[]{:S(2)}) collective-permute-start(bf16[128,1152]{1,0:T(8,128)(2,1)S(1)} %get-tuple-element.121.rest_0_.sent), channel_id=1, source_target_pairs={{0,4},{4,0},{8,12},{12,8},{1,5},{5,1},{9,13},{13,9},{2,6},{6,2},{1... | collective-permute-start | bytes 884744 | tf_op jit(solution)/shard_map/ppermute | solution.py:69
  96.8 10.8 %collective-permute-start.26 = (bf16[128,1152]{1,0:T(8,128)(2,1)S(1)}, bf16[128,1152]{1,0:T(8,128)(2,1)S(1)}, u32[]{:S(2)}, u32[]{:S(2)}) collective-permute-start(bf16[128,1152]{1,0:T(8,128)(2,1)S(1)} %get-tuple-element.125), channel_id=1, source_target_pairs={{0,1},{1,0},{4,8},{8,4},{5,9},{9,5},{12,13},{13,12},{2,3},{3,2},{6... | collective-permute-start | bytes 884744 | tf_op jit(solution)/shard_map/ppermute | solution.py:73
  101.5 13.9 %collective-permute-start.27 = (bf16[128,1408]{1,0:T(8,128)(2,1)S(1)}, bf16[128,1408]{1,0:T(8,128)(2,1)S(1)}, u32[]{:S(2)}, u32[]{:S(2)}) collective-permute-start(bf16[128,1408]{1,0:T(8,128)(2,1)S(1)} %get-tuple-element.124.rest_0_.sent), channel_id=1, source_target_pairs={{0,4},{4,0},{8,12},{12,8},{1,5},{5,1},{9,13},{13,9},{2,6},{6,2},{1... | collective-permute-start | bytes 1081352 | tf_op jit(solution)/shard_map/ppermute | solution.py:69
  103.2 7.1 %collective-permute-start.28 = (bf16[128,1152]{1,0:T(8,128)(2,1)S(1)}, bf16[128,1152]{1,0:T(8,128)(2,1)S(1)}, u32[]{:S(2)}, u32[]{:S(2)}) collective-permute-start(bf16[128,1152]{1,0:T(8,128)(2,1)S(1)} %get-tuple-element.128), channel_id=1, source_target_pairs={{0,1},{1,0},{4,8},{8,4},{5,9},{9,5},{12,13},{13,12},{2,3},{3,2},{6... | collective-permute-start | bytes 884744 | tf_op jit(solution)/shard_map/ppermute | solution.py:73
  107.8 13.9 %collective-permute-start.29 = (bf16[128,1152]{1,0:T(8,128)(2,1)S(1)}, bf16[128,1152]{1,0:T(8,128)(2,1)S(1)}, u32[]{:S(2)}, u32[]{:S(2)}) collective-permute-start(bf16[128,1152]{1,0:T(8,128)(2,1)S(1)} %get-tuple-element.127.rest_0_.sent), channel_id=1, source_target_pairs={{0,4},{4,0},{8,12},{12,8},{1,5},{5,1},{9,13},{13,9},{2,6},{6,2},{1... | collective-permute-start | bytes 884744 | tf_op jit(solution)/shard_map/ppermute | solution.py:69
  109.5 12.2 %collective-permute-start.30 = (bf16[128,1152]{1,0:T(8,128)(2,1)S(1)}, bf16[128,1152]{1,0:T(8,128)(2,1)S(1)}, u32[]{:S(2)}, u32[]{:S(2)}) collective-permute-start(bf16[128,1152]{1,0:T(8,128)(2,1)S(1)} %get-tuple-element.131), channel_id=1, source_target_pairs={{0,1},{1,0},{4,8},{8,4},{5,9},{9,5},{12,13},{13,12},{2,3},{3,2},{6... | collective-permute-start | bytes 884744 | tf_op jit(solution)/shard_map/ppermute | solution.py:73
  115.5 12.5 %collective-permute-start.32 = (bf16[128,1408]{1,0:T(8,128)(2,1)S(1)}, bf16[128,1408]{1,0:T(8,128)(2,1)S(1)}, u32[]{:S(2)}, u32[]{:S(2)}) collective-permute-start(bf16[128,1408]{1,0:T(8,128)(2,1)S(1)} %get-tuple-element.134), channel_id=1, source_target_pairs={{0,1},{1,0},{4,8},{8,4},{5,9},{9,5},{12,13},{13,12},{2,3},{3,2},{6... | collective-permute-start | bytes 1081352 | tf_op jit(solution)/shard_map/ppermute | solution.py:73
  115.6 12.4 %collective-permute-start.31 = (bf16[128,1152]{1,0:T(8,128)(2,1)S(1)}, bf16[128,1152]{1,0:T(8,128)(2,1)S(1)}, u32[]{:S(2)}, u32[]{:S(2)}) collective-permute-start(bf16[128,1152]{1,0:T(8,128)(2,1)S(1)} %get-tuple-element.130.rest_0_.sent), channel_id=1, source_target_pairs={{0,4},{4,0},{8,12},{12,8},{1,5},{5,1},{9,13},{13,9},{2,6},{6,2},{1... | collective-permute-start | bytes 884744 | tf_op jit(solution)/shard_map/ppermute | solution.py:69
  121.8 12.5 %collective-permute-start.33 = (bf16[128,1152]{1,0:T(8,128)(2,1)S(1)}, bf16[128,1152]{1,0:T(8,128)(2,1)S(1)}, u32[]{:S(2)}, u32[]{:S(2)}) collective-permute-start(bf16[128,1152]{1,0:T(8,128)(2,1)S(1)} %get-tuple-element.133.rest_0_.sent), channel_id=1, source_target_pairs={{0,4},{4,0},{8,12},{12,8},{1,5},{5,1},{9,13},{13,9},{2,6},{6,2},{1... | collective-permute-start | bytes 884744 | tf_op jit(solution)/shard_map/ppermute | solution.py:69
  123.5 7.2 %collective-permute-start.34 = (bf16[128,384]{1,0:T(8,128)(2,1)S(1)}, bf16[128,384]{1,0:T(8,128)(2,1)S(1)}, u32[]{:S(2)}, u32[]{:S(2)}) collective-permute-start(bf16[128,384]{1,0:T(8,128)(2,1)S(1)} %get-tuple-element.137), channel_id=1, source_target_pairs={{0,1},{1,0},{4,8},{8,4},{5,9},{9,5},{12,13},{13,12},{2,3},{3,2},{6... | collective-permute-start | bytes 294920 | tf_op jit(solution)/shard_map/ppermute | solution.py:73
  128.2 13.9 %collective-permute-start.35 = (bf16[128,1408]{1,0:T(8,128)(2,1)S(1)}, bf16[128,1408]{1,0:T(8,128)(2,1)S(1)}, u32[]{:S(2)}, u32[]{:S(2)}) collective-permute-start(bf16[128,1408]{1,0:T(8,128)(2,1)S(1)} %get-tuple-element.136.rest_0_.sent), channel_id=1, source_target_pairs={{0,4},{4,0},{8,12},{12,8},{1,5},{5,1},{9,13},{13,9},{2,6},{6,2},{1... | collective-permute-start | bytes 1081352 | tf_op jit(solution)/shard_map/ppermute | solution.py:69
  130.6 6.3 %collective-permute-start.36 = (bf16[128,384]{1,0:T(8,128)(2,1)S(1)}, bf16[128,384]{1,0:T(8,128)(2,1)S(1)}, u32[]{:S(2)}, u32[]{:S(2)}) collective-permute-start(bf16[128,384]{1,0:T(8,128)(2,1)S(1)} %get-tuple-element.139), channel_id=1, source_target_pairs={{0,1},{1,0},{4,8},{8,4},{5,9},{9,5},{12,13},{13,12},{2,3},{3,2},{6... | collective-permute-start | bytes 294920 | tf_op jit(solution)/shard_map/ppermute | solution.py:73
  134.5 10.3 %collective-permute-start.37 = (bf16[128,384]{1,0:T(8,128)(2,1)S(1)}, bf16[128,384]{1,0:T(8,128)(2,1)S(1)}, u32[]{:S(2)}, u32[]{:S(2)}) collective-permute-start(bf16[128,384]{1,0:T(8,128)(2,1)S(1)} %get-tuple-element.138.rest_0_.sent), channel_id=1, source_target_pairs={{0,4},{4,0},{8,12},{12,8},{1,5},{5,1},{9,13},{13,9},{2,6},{6,2},{1... | collective-permute-start | bytes 294920 | tf_op jit(solution)/shard_map/ppermute | solution.py:69
  136.8 8.0 %collective-permute-start.38 = (bf16[128,384]{1,0:T(8,128)(2,1)S(1)}, bf16[128,384]{1,0:T(8,128)(2,1)S(1)}, u32[]{:S(2)}, u32[]{:S(2)}) collective-permute-start(bf16[128,384]{1,0:T(8,128)(2,1)S(1)} %get-tuple-element.141), channel_id=1, source_target_pairs={{0,1},{1,0},{4,8},{8,4},{5,9},{9,5},{12,13},{13,12},{2,3},{3,2},{6... | collective-permute-start | bytes 294920 | tf_op jit(solution)/shard_map/ppermute | solution.py:73
  142.2 5.0 %collective-permute-start.39 = (bf16[128,512]{1,0:T(8,128)(2,1)S(1)}, bf16[128,512]{1,0:T(8,128)(2,1)S(1)}, u32[]{:S(2)}, u32[]{:S(2)}) collective-permute-start(bf16[128,512]{1,0:T(8,128)(2,1)S(1)} %get-tuple-element.140.rest_0_.sent), channel_id=1, source_target_pairs={{0,4},{4,0},{8,12},{12,8},{1,5},{5,1},{9,13},{13,9},{2,6},{6,2},{1... | collective-permute-start | bytes 393224 | tf_op jit(solution)/shard_map/ppermute | solution.py:69
  144.7 2.0 %collective-permute-start.40 = (bf16[128,384]{1,0:T(8,128)(2,1)S(1)}, bf16[128,384]{1,0:T(8,128)(2,1)S(1)}, u32[]{:S(2)}, u32[]{:S(2)}) collective-permute-start(bf16[128,384]{1,0:T(8,128)(2,1)S(1)} %get-tuple-element.143), channel_id=1, source_target_pairs={{0,1},{1,0},{4,8},{8,4},{5,9},{9,5},{12,13},{13,12},{2,3},{3,2},{6... | collective-permute-start | bytes 294920 | tf_op jit(solution)/shard_map/ppermute | solution.py:73
  144.9 6.0 %collective-permute-start.41 = (bf16[128,384]{1,0:T(8,128)(2,1)S(1)}, bf16[128,384]{1,0:T(8,128)(2,1)S(1)}, u32[]{:S(2)}, u32[]{:S(2)}) collective-permute-start(bf16[128,384]{1,0:T(8,128)(2,1)S(1)} %get-tuple-element.142.rest_0_), channel_id=1, source_target_pairs={{0,4},{4,0},{8,12},{12,8},{1,5},{5,1},{9,13},{13,9},{2,6},{6,2},{1... | collective-permute-start | bytes 294920 | tf_op jit(solution)/shard_map/ppermute | solution.py:69
  146.6 4.2 %collective-permute-start.42 = (bf16[128,384]{1,0:T(8,128)(2,1)S(1)}, bf16[128,384]{1,0:T(8,128)(2,1)S(1)}, u32[]{:S(2)}, u32[]{:S(2)}) collective-permute-start(bf16[128,384]{1,0:T(8,128)(2,1)S(1)} %get-tuple-element.145), channel_id=1, source_target_pairs={{0,1},{1,0},{4,8},{8,4},{5,9},{9,5},{12,13},{13,12},{2,3},{3,2},{6... | collective-permute-start | bytes 294920 | tf_op jit(solution)/shard_map/ppermute | solution.py:73
  147.3 6.4 %collective-permute-start.43 = (bf16[128,384]{1,0:T(8,128)(2,1)S(1)}, bf16[128,384]{1,0:T(8,128)(2,1)S(1)}, u32[]{:S(2)}, u32[]{:S(2)}) collective-permute-start(bf16[128,384]{1,0:T(8,128)(2,1)S(1)} %get-tuple-element.144.rest_0_), channel_id=1, source_target_pairs={{0,4},{4,0},{8,12},{12,8},{1,5},{5,1},{9,13},{13,9},{2,6},{6,2},{1... | collective-permute-start | bytes 294920 | tf_op jit(solution)/shard_map/ppermute | solution.py:69
  150.8 2.9 %collective-permute-start.44 = (bf16[128,512]{1,0:T(8,128)(2,1)S(1)}, bf16[128,512]{1,0:T(8,128)(2,1)S(1)}, u32[]{:S(2)}, u32[]{:S(2)}) collective-permute-start(bf16[128,512]{1,0:T(8,128)(2,1)S(1)} %get-tuple-element.146), channel_id=1, source_target_pairs={{0,1},{1,0},{4,8},{8,4},{5,9},{9,5},{12,13},{13,12},{2,3},{3,2},{6... | collective-permute-start | bytes 393224 | tf_op jit(solution)/shard_map/ppermute | solution.py:73
  150.9 5.8 %collective-permute-start.45 = (bf16[128,384]{1,0:T(8,128)(2,1)S(1)}, bf16[128,384]{1,0:T(8,128)(2,1)S(1)}, u32[]{:S(2)}, u32[]{:S(2)}) collective-permute-start(bf16[128,384]{1,0:T(8,128)(2,1)S(1)} %hop.42.rest_0_), channel_id=1, source_target_pairs={{0,4},{4,0},{8,12},{12,8},{1,5},{5,1},{9,13},{13,9},{2,6},{6,2},{1... | collective-permute-start | bytes 294920 | tf_op jit(solution)/shard_map/ppermute | solution.py:69
  153.7 5.2 %collective-permute-start.46 = (bf16[128,512]{1,0:T(8,128)(2,1)S(1)}, bf16[128,512]{1,0:T(8,128)(2,1)S(1)}, u32[]{:S(2)}, u32[]{:S(2)}) collective-permute-start(bf16[128,512]{1,0:T(8,128)(2,1)S(1)} %hop.43.rest_0_), channel_id=1, source_target_pairs={{0,4},{4,0},{8,12},{12,8},{1,5},{5,1},{9,13},{13,9},{2,6},{6,2},{1... | collective-permute-start | bytes 393224 | tf_op jit(solution)/shard_map/ppermute | solution.py:69
  159.7 2.0 %collective-permute-start.47 = (bf16[128,2048]{1,0:T(8,128)(2,1)S(1)}, bf16[128,2048]{1,0:T(8,128)(2,1)S(1)}, u32[]{:S(2)}, u32[]{:S(2)}) collective-permute-start(bf16[128,2048]{1,0:T(8,128)(2,1)S(1)} %broadcast_select_fusion.2), channel_id=1, source_target_pairs={{0,1},{1,0},{2,3},{3,2},{4,5},{5,4},{6,7},{7,6},{8,9},{9,8},{10,11... | collective-permute-start | bytes 1572872 | tf_op jit(solution)/shard_map/ppermute | solution.py:77
  162.0 8.4 %collective-permute-start.48 = (bf16[64,2048]{1,0:T(8,128)(2,1)S(1)}, bf16[64,2048]{1,0:T(8,128)(2,1)S(1)}, u32[]{:S(2)}, u32[]{:S(2)}) collective-permute-start(bf16[64,2048]{1,0:T(8,128)(2,1)S(1)} %slice.124), channel_id=1, source_target_pairs={{0,2},{2,0},{1,3},{3,1},{4,6},{6,4},{5,7},{7,5},{8,10},{10,8},{9,1... | collective-permute-start | bytes 786440 | tf_op jit(solution)/shard_map/ppermute | solution.py:77
  (8 other events, 45.1 us)

commit v5 on v4

--- a/solution.py
+++ b/solution.py
@@ -112,7 +112,8 @@
     heads = features // HD
     cache_len = key_cache.shape[1]
     block = 16
-    tall, wide = heads * block, block * cache_len
+    few = block // 2
+    tall, wide = heads * few, few * cache_len
     begin = part * (rows // block)
     scale = 1.0 / HD**0.5
     held = functools.partial(pltpu.with_memory_space_constraint, memory_space=pltpu.HBM)
@@ -124,37 +125,50 @@
         def _():
             sparse[...] = jnp.zeros_like(sparse)
 
-        for h in range(heads):
-            sparse[h * block : (h + 1) * block, h * HD : (h + 1) * HD] = q_ref[:, h * HD : (h + 1) * HD]
-        q_rows = sparse[...]
         over = (((1,), (1,)), ((), ()))
-        keys = k_ref[...].reshape(wide, features)
-        scores = lax.dot_general(q_rows, keys, over, preferred_element_type=f32) * scale
-        own = lax.dot_general(q_rows, nk_ref[...], over, preferred_element_type=f32) * scale
-        mine = lax.broadcasted_iota(jnp.int32, own.shape, 0) % block == lax.broadcasted_iota(jnp.int32, own.shape, 1)
-        own = jnp.sum(jnp.where(mine, own, 0.0), axis=1, keepdims=True)
-        column = lax.broadcasted_iota(jnp.int32, scores.shape, 1)
-        owner = lax.broadcasted_iota(jnp.int32, scores.shape, 0) % block
-        offset = column - owner * cache_len
-        candidate = lax.broadcasted_iota(jnp.int32, (tall, 1), 0) % block
-        span = jnp.zeros((tall, 1), jnp.int32)
-        for c in range(block):
-            span = jnp.where(candidate == c, length_ref[(pl.program_id(0) + begin) * block + c], span)
-        valid = (offset >= 0) & (offset < span)
-        scores = jnp.where(valid, scores, -jnp.inf)
-        top = jnp.maximum(jnp.max(scores, axis=1, keepdims=True), own)
-        weights = jnp.exp(scores - top)
-        own_w = jnp.exp(own - top)
-        total = jnp.sum(weights, axis=1, keepdims=True) + own_w
-        probs = (weights / total).astype(bf16)
-        own_p = (own_w / total).astype(bf16).astype(f32)
-        mixed = jnp.dot(probs, v_ref[...].reshape(wide, features), preferred_element_type=f32)
+        shares = []
+        for sub in range(2):
+            mine_at = slice(sub * few, (sub + 1) * few)
+            for h in range(0, heads, 2):
+                for odd in range(2):
+                    at = slice((h + odd) * HD, (h + odd + 1) * HD)
+                    part = q_ref[:, at].astype(f32)[mine_at]
+                    none = jnp.zeros_like(part)
+                    both = jnp.concatenate([none, part] if odd else [part, none])
+                    sparse[sub, h * few : (h + 2) * few, at] = both.astype(bf16)
+            q_rows = sparse[sub]
+            keys = k_ref[mine_at].reshape(wide, features)
+            scores = lax.dot_general(q_rows, keys, over, preferred_element_type=f32) * scale
+            own = lax.dot_general(q_rows, nk_ref[...], over, preferred_element_type=f32) * scale
+            row = lax.broadcasted_iota(jnp.int32, own.shape, 0) % few
+            mine = row + sub * few == lax.broadcasted_iota(jnp.int32, own.shape, 1)
+            own = jnp.sum(jnp.where(mine, own, 0.0), axis=1, keepdims=True)
+            column = lax.broadcasted_iota(jnp.int32, scores.shape, 1)
+            owner = lax.broadcasted_iota(jnp.int32, scores.shape, 0) % few
+            offset = column - owner * cache_len
+            candidate = lax.broadcasted_iota(jnp.int32, (tall, 1), 0) % few
+            span = jnp.zeros((tall, 1), jnp.int32)
+            for c in range(few):
+                length = length_ref[(pl.program_id(0) + begin) * block + sub * few + c]
+                span = jnp.where(candidate == c, length, span)
+            valid = (offset >= 0) & (offset < span)
+            scores = jnp.where(valid, scores, -jnp.inf)
+            top = jnp.maximum(jnp.max(scores, axis=1, keepdims=True), own)
+            weights = jnp.exp(scores - top)
+            own_w = jnp.exp(own - top)
+            total = jnp.sum(weights, axis=1, keepdims=True) + own_w
+            probs = (weights / total).astype(bf16)
+            own_p = (own_w / total).astype(bf16).astype(f32)
+            mixed = jnp.dot(probs, v_ref[mine_at].reshape(wide, features), preferred_element_type=f32)
+            shares.append((mixed, own_p))
         squares = jnp.zeros((block, HD), f32)
         for h in range(heads):
-            at, rows_at = slice(h * HD, (h + 1) * HD), slice(h * block, (h + 1) * block)
-            x = res_ref[:, at].astype(f32) + mixed[rows_at, at] + own_p[rows_at] * nv_ref[:, at].astype(f32)
+            at, rows_at = slice(h * HD, (h + 1) * HD), slice(h * few, (h + 1) * few)
+            mixed = jnp.concatenate([share[0][rows_at, at] for share in shares])
+            own_p = jnp.concatenate([share[1][rows_at] for share in shares])
+            x = res_ref[:, at].astype(f32) + mixed + own_p * nv_ref[:, at].astype(f32)
             x_ref[:, at] = x
-            scaled_ref[:, at] = (x * gain_ref[:, at].astype(f32)).astype(bf16)
+            scaled_ref[:, at] = (x * gain_ref[at].astype(f32)[None, :]).astype(bf16)
             squares = squares + x * x
         scaled_ref[:, features:] = in_three(jnp.sum(squares, axis=1, keepdims=True), (block, LANES))
 
@@ -171,7 +185,7 @@
             cache,
             cache,
             flat,
-            pl.BlockSpec((1, features), lambda i: (0, 0)),
+            pl.BlockSpec((features,), lambda i: (0,)),
         ]
         + [ANY] * len(after),
         out_specs=[pl.BlockSpec((block, features), lambda i: (i, 0)), pl.BlockSpec((block, features + LANES), lambda i: (i, 0))],
@@ -179,12 +193,12 @@
             jax.ShapeDtypeStruct((rows, features), f32),
             jax.ShapeDtypeStruct((rows, features + LANES), bf16),
         ],
-        scratch_shapes=[pltpu.VMEM((tall, features), bf16)],
+        scratch_shapes=[pltpu.VMEM((2, tall, features), bf16)],
         compiler_params=pltpu.CompilerParams(vmem_limit_bytes=40 << 20),
         cost_estimate=pl.CostEstimate(
-            flops=4 * rows // block * tall * wide * features,
+            flops=8 * rows // block * tall * wide * features,
             bytes_accessed=4 * rows * cache_len * features,
-            transcendentals=rows // block * tall * wide,
+            transcendentals=2 * rows // block * tall * wide,
         ),
         name="attend_rows",
     )(
@@ -195,7 +209,7 @@
         held(key_cache),
         held(value_cache),
         held(residual),
-        norm_gain.reshape(1, -1),
+        norm_gain,
         *after,
     )
 
@@ -478,7 +492,7 @@
     after = products(1, after)
     send(1, 0, (part_out[1][0], 0), None)
     after = products(2, after)
-    total, inv_in = None, None
+    total, inv_in, totals = None, None, []
     for t in range(len(streams[0]) + 5):
         for s in (0, 1):
             count = len(streams[s])
@@ -503,8 +517,10 @@
             after = products(k, after)
             if 0 <= t - 5 < count:
                 k = 2 * (t - 5) + s
-                hidden = hidden_rows(outer, chunks[k].width, hidden_of(k), after + ([] if total is None else [total]))
+                earlier = totals[-2:-1] if t > len(streams[0]) else totals[-1:]
+                hidden = hidden_rows(outer, chunks[k].width, hidden_of(k), after + earlier)
                 total = down_product(total, chunks[k], hidden, w_down)
+                totals.append(total)
                 after = [hidden]
     total = total.astype(bf16)
     far, near = total[:half], total[half:]

time: 171 us -> 171 us (level)
    unnamed x16 -> x18, local copies, waits for them, and re-layouts: 2.92 us -> 3.61 us
  transfers between devices with their start and end apart: 49 -> 49, of which waited for: 19 -> 20; matrix products, arithmetic and copies ran while one was open for 5% -> 5% of each run, Pallas kernels for 21% -> 21%
where the time goes in v5:
time: 171 us
  waiting for transfers between devices  58.7 us (34%)
  Pallas kernels  51.5 us (30%)
  starting transfers between devices  44.6 us (26%)
  matrix products  9.95 us (6%)
  local copies, waits for them, and re-layouts  3.69 us (2%)
    ppermute x24, waiting for transfers between devices, outward(): return lax.ppermute(a, 'mix', OUTWARD)  42.5 us
    ppermute x24, starting transfers between devices, outward(): return lax.ppermute(a, 'mix', OUTWARD)  39.6 us
    pallas_call x5, Pallas kernels, twin_products(): pl.pallas_call(kernel, grid=(len(chunks),), in_specs=[pl.BlockSpec((count...  22.6 us
    ppermute x5, waiting for transfers between devices, swap(): return lax.ppermute(a, axis, SWAP)  16.2 us
    pallas_call x4, Pallas kernels, partial_products(): pl.pallas_call(kernel, grid=(1,), in_specs=[pl.BlockSpec((count, depth),...  13.7 us
    pallas_call x1, Pallas kernels, attend_rows(): pl.pallas_call(kernel, grid=(rows // block,), in_specs=[SMEM, flat, flat,...  12.3 us
    dot_general x14, matrix products, down_product(): term = jnp.dot(hidden[:, :chunk.units], weight, preferred_element_type=f32)  9.95 us
    ppermute x5, starting transfers between devices, swap(): return lax.ppermute(a, axis, SWAP)  4.63 us
  transfers between devices with their start and end apart: 49, of which 20 were waited for; matrix products, arithmetic and copies ran while one was open for 5% of the time, Pallas kernels for 21%

profile of v5, /device:TPU:0, one launch (start us, length us, event | category | flops | bytes accessed | tf_op | source)
XLA Modules:
  0.0 171.2 jit_solution(7545436519404672582)
XLA Ops:
  1.3 12.3 %attend_rows.1 = (f32[64,2048]{1,0:T(8,128)S(1)}, bf16[64,2176]{1,0:T(8,128)(2,1)S(1)}) custom-call(s32[64]{0:T(128)S(1)} %copy-done.1, bf16[64,2048]{1,0:T(8,128)(2,1)} %q_ref.1, bf16[64,2048]{1,0:T(8,128)(2,1)} %nk_ref.1, bf16[64,2048]{1,0:T(8,128)(2,1)} %nv_ref.1, bf16[64,32,2048]{2,1,0:T(8,128)(2,1)} %k_ref.1, bf16[64,32,2048]{2,1,0:T(8,128)(2,1)} %v_ref.1, ...), custom_call_target="tpu_custom_call" | custom-call | flops 2147483648 | bytes 16777216 | tf_op jit(solution)/shard_map/attend_rows/pallas_call | solution.py:177
  13.6 3.0 %collective-permute-start = (bf16[64,2176]{1,0:T(8,128)(2,1)S(1)}, bf16[64,2176]{1,0:T(8,128)(2,1)S(1)}, u32[]{:S(2)}, u32[]{:S(2)}) collective-permute-start(bf16[64,2176]{1,0:T(8,128)(2,1)S(1)} %get-tuple-element.77), channel_id=1, source_target_pairs={{0,2},{2,0},{1,3},{3,1},{4,6},{6,4},{5,7},{7,5},{8,10},{10,8},{9,1... | collective-permute-start | bytes 835592 | tf_op jit(solution)/shard_map/ppermute | solution.py:77
  16.7 6.6 %collective-permute-done = bf16[64,2176]{1,0:T(8,128)(2,1)S(1)} collective-permute-done((bf16[64,2176]{1,0:T(8,128)(2,1)S(1)}, bf16[64,2176]{1,0:T(8,128)(2,1)S(1)}, u32[]{:S(2)}, u32[]{:S(2)}) %collective-permute-start) | collective-permute-done | bytes 278560 | tf_op jit(solution)/shard_map/ppermute | solution.py:77
  23.4 1.5 collective-permute-done.2
  25.1 3.2 %partial_products.4 = (bf16[128,896]{1,0:T(8,128)(2,1)S(1)}, bf16[128,896]{1,0:T(8,128)(2,1)S(1)}) custom-call(bf16[256,2176]{1,0:T(8,128)(2,1)S(1)} %pad_maximum_fusion.rows_ref.rest_2_, bf16[5472,2048]{1,0:T(8,128)(2,1)} %bitcast.18, bf16[5472,2048]{1,0:T(8,128)(2,1)} %bitcast.28, bf16[256,2176]{1,0:T(8,128)(2,1)S(1)} %pad_maximum_fusion.rows_ref.rest_2_), custom_call_target="tpu_custom_call" | custom-call | flops 805306368 | bytes 3735552 | tf_op jit(solution)/shard_map/partial_products/pallas_call | solution.py:253
  28.3 1.9 %collective-permute-start.3 = (bf16[128,896]{1,0:T(8,128)(2,1)S(1)}, bf16[128,896]{1,0:T(8,128)(2,1)S(1)}, u32[]{:S(2)}, u32[]{:S(2)}) collective-permute-start(bf16[128,896]{1,0:T(8,128)(2,1)S(1)} %get-tuple-element.78.rest_2_.refs_3_), channel_id=1, source_target_pairs={{0,4},{4,0},{8,12},{12,8},{1,5},{5,1},{9,13},{13,9},{2,6},{6,2},{1... | collective-permute-start | bytes 688136 | tf_op jit(solution)/shard_map/ppermute | solution.py:69
  30.2 3.2 %partial_products.5 = (bf16[128,768]{1,0:T(8,128)(2,1)S(1)}, bf16[128,768]{1,0:T(8,128)(2,1)S(1)}) custom-call(bf16[256,2176]{1,0:T(8,128)(2,1)S(1)} %pad_maximum_fusion.rows_ref.rest_2_, bf16[5472,2048]{1,0:T(8,128)(2,1)} %bitcast.19, bf16[5472,2048]{1,0:T(8,128)(2,1)} %bitcast.29, bf16[128,896]{1,0:T(8,128)(2,1)S(1)} %get-tuple-element.78.rest_2_.refs_3_), custom_call_target="tpu_custom_call" | custom-call | flops 805306368 | bytes 3735552 | tf_op jit(solution)/shard_map/partial_products/pallas_call | solution.py:253
  33.7 4.5 %twin_products.5 = (bf16[128,768]{1,0:T(8,128)(2,1)S(1)}, bf16[128,768]{1,0:T(8,128)(2,1)S(1)}, bf16[128,768]{1,0:T(8,128)(2,1)S(1)}, bf16[128,768]{1,0:T(8,128)(2,1)S(1)}) custom-call(bf16[256,2176]{1,0:T(8,128)(2,1)S(1)} %pad_maximum_fusion.rows_ref.rest_2_, bf16[5472,2048]{1,0:T(8,128)(2,1)} %bitcast.20, bf16[5472,2048]{1,0:T(8,128)(2,1)} %bitcast.30, ...), custom_call_target="tpu_custom_call" | custom-call | flops 1610612736 | bytes 7471104 | tf_op jit(solution)/shard_map/twin_products/pallas_call | solution.py:290
  38.3 3.5 %collective-permute-start.4 = (bf16[128,768]{1,0:T(8,128)(2,1)S(1)}, bf16[128,768]{1,0:T(8,128)(2,1)S(1)}, u32[]{:S(2)}, u32[]{:S(2)}) collective-permute-start(bf16[128,768]{1,0:T(8,128)(2,1)S(1)} %get-tuple-element.81.rest_0_), channel_id=1, source_target_pairs={{0,4},{4,0},{8,12},{12,8},{1,5},{5,1},{9,13},{13,9},{2,6},{6,2},{1... | collective-permute-start | bytes 589832 | tf_op jit(solution)/shard_map/ppermute | solution.py:69
  41.8 4.5 %twin_products.6 = (bf16[128,768]{1,0:T(8,128)(2,1)S(1)}, bf16[128,768]{1,0:T(8,128)(2,1)S(1)}, bf16[128,768]{1,0:T(8,128)(2,1)S(1)}, bf16[128,768]{1,0:T(8,128)(2,1)S(1)}) custom-call(bf16[256,2176]{1,0:T(8,128)(2,1)S(1)} %pad_maximum_fusion.rows_ref.rest_2_, bf16[5472,2048]{1,0:T(8,128)(2,1)} %bitcast.21, bf16[5472,2048]{1,0:T(8,128)(2,1)} %bitcast.31, ...), custom_call_target="tpu_custom_call" | custom-call | flops 3221225472 | bytes 14942208 | tf_op jit(solution)/shard_map/twin_products/pallas_call | solution.py:290
  46.4 1.6 collective-permute-start.9
  48.8 4.5 %twin_products.7 = (bf16[128,768]{1,0:T(8,128)(2,1)S(1)}, bf16[128,768]{1,0:T(8,128)(2,1)S(1)}, bf16[128,768]{1,0:T(8,128)(2,1)S(1)}, bf16[128,768]{1,0:T(8,128)(2,1)S(1)}) custom-call(bf16[256,2176]{1,0:T(8,128)(2,1)S(1)} %pad_maximum_fusion.rows_ref.rest_2_, bf16[5472,2048]{1,0:T(8,128)(2,1)} %bitcast.22, bf16[5472,2048]{1,0:T(8,128)(2,1)} %bitcast.32, ...), custom_call_target="tpu_custom_call" | custom-call | flops 3221225472 | bytes 14942208 | tf_op jit(solution)/shard_map/twin_products/pallas_call | solution.py:290
  54.2 1.7 %collective-permute-start.13 = (bf16[128,768]{1,0:T(8,128)(2,1)S(1)}, bf16[128,768]{1,0:T(8,128)(2,1)S(1)}, u32[]{:S(2)}, u32[]{:S(2)}) collective-permute-start(bf16[128,768]{1,0:T(8,128)(2,1)S(1)} %get-tuple-element.94.refs_7_), channel_id=1, source_target_pairs={{0,4},{4,0},{8,12},{12,8},{1,5},{5,1},{9,13},{13,9},{2,6},{6,2},{1... | collective-permute-start | bytes 589832 | tf_op jit(solution)/shard_map/ppermute | solution.py:69
  56.0 3.1 %collective-permute-done.7.refs_1_ = bf16[128,896]{1,0:T(8,128)(2,1)S(1)} collective-permute-done((bf16[128,896]{1,0:T(8,128)(2,1)S(1)}, bf16[128,896]{1,0:T(8,128)(2,1)S(1)}, u32[]{:S(2)}, u32[]{:S(2)}) %collective-permute-start.7) | collective-permute-done | bytes 229408 | tf_op jit(solution)/shard_map/ppermute | solution.py:69
  59.3 1.6 collective-permute-start.11
  60.9 4.5 %twin_products.8 = (bf16[128,768]{1,0:T(8,128)(2,1)S(1)}, bf16[128,768]{1,0:T(8,128)(2,1)S(1)}, bf16[128,768]{1,0:T(8,128)(2,1)S(1)}, bf16[128,768]{1,0:T(8,128)(2,1)S(1)}) custom-call(bf16[256,2176]{1,0:T(8,128)(2,1)S(1)} %pad_maximum_fusion.rows_ref.rest_2_, bf16[5472,2048]{1,0:T(8,128)(2,1)} %bitcast.23, bf16[5472,2048]{1,0:T(8,128)(2,1)} %bitcast.33, ...), custom_call_target="tpu_custom_call" | custom-call | flops 3221225472 | bytes 14942208 | tf_op jit(solution)/shard_map/twin_products/pallas_call | solution.py:290
  66.6 3.0 %collective-permute-done.11.refs_1_.got = bf16[128,1152]{1,0:T(8,128)(2,1)S(1)} collective-permute-done((bf16[128,1152]{1,0:T(8,128)(2,1)S(1)}, bf16[128,1152]{1,0:T(8,128)(2,1)S(1)}, u32[]{:S(2)}, u32[]{:S(2)}) %collective-permute-start.11) | collective-permute-done | bytes 294944 | tf_op jit(solution)/shard_map/ppermute | solution.py:69
  70.0 1.8 %collective-permute-start.16 = (bf16[128,1152]{1,0:T(8,128)(2,1)S(1)}, bf16[128,1152]{1,0:T(8,128)(2,1)S(1)}, u32[]{:S(2)}, u32[]{:S(2)}) collective-permute-start(bf16[128,1152]{1,0:T(8,128)(2,1)S(1)} %get-tuple-element.105.rest_0_.sent), channel_id=1, source_target_pairs={{0,4},{4,0},{8,12},{12,8},{1,5},{5,1},{9,13},{13,9},{2,6},{6,2},{1... | collective-permute-start | bytes 884744 | tf_op jit(solution)/shard_map/ppermute | solution.py:69
  71.8 4.5 %twin_products.9 = (bf16[128,768]{1,0:T(8,128)(2,1)S(1)}, bf16[128,768]{1,0:T(8,128)(2,1)S(1)}, bf16[128,768]{1,0:T(8,128)(2,1)S(1)}, bf16[128,768]{1,0:T(8,128)(2,1)S(1)}) custom-call(bf16[256,2176]{1,0:T(8,128)(2,1)S(1)} %pad_maximum_fusion.rows_ref.rest_2_, bf16[5472,2048]{1,0:T(8,128)(2,1)} %bitcast.24, bf16[5472,2048]{1,0:T(8,128)(2,1)} %bitcast.34, ...), custom_call_target="tpu_custom_call" | custom-call | flops 3221225472 | bytes 14942208 | tf_op jit(solution)/shard_map/twin_products/pallas_call | solution.py:290
  76.5 1.2 collective-permute-start.21
  77.7 4.5 %collective-permute-done.16.refs_1_.got = bf16[128,1152]{1,0:T(8,128)(2,1)S(1)} collective-permute-done((bf16[128,1152]{1,0:T(8,128)(2,1)S(1)}, bf16[128,1152]{1,0:T(8,128)(2,1)S(1)}, u32[]{:S(2)}, u32[]{:S(2)}) %collective-permute-start.16) | collective-permute-done | bytes 294944 | tf_op jit(solution)/shard_map/ppermute | solution.py:69
  82.4 1.7 collective-permute-start.19
  84.0 3.2 %partial_products.6 = (bf16[128,768]{1,0:T(8,128)(2,1)S(1)}, bf16[128,768]{1,0:T(8,128)(2,1)S(1)}) custom-call(bf16[256,2176]{1,0:T(8,128)(2,1)S(1)} %pad_maximum_fusion.rows_ref.rest_2_, bf16[5472,2048]{1,0:T(8,128)(2,1)} %bitcast.25, bf16[5472,2048]{1,0:T(8,128)(2,1)} %bitcast.35, bf16[128,1152]{1,0:T(8,128)(2,1)S(1)} %get-tuple-element.112.rest_2_.sent), custom_call_target="tpu_custom_call" | custom-call | flops 1610612736 | bytes 7471104 | tf_op jit(solution)/shard_map/partial_products/pallas_call | solution.py:253
  87.2 1.3 collective-permute-done.21.refs_1_.got
  88.7 1.7 collective-permute-start.23
  90.5 4.1 %partial_products.7 = (bf16[128,1024]{1,0:T(8,128)(2,1)S(1)}, bf16[128,1024]{1,0:T(8,128)(2,1)S(1)}) custom-call(bf16[256,2176]{1,0:T(8,128)(2,1)S(1)} %pad_maximum_fusion.rows_ref.rest_2_, bf16[5472,2048]{1,0:T(8,128)(2,1)} %bitcast.26, bf16[5472,2048]{1,0:T(8,128)(2,1)} %bitcast.36, bf16[5472,2048]{1,0:T(8,128)(2,1)} %bitcast.27, ...), custom_call_target="tpu_custom_call" | custom-call | flops 2147483648 | bytes 9961472 | tf_op jit(solution)/shard_map/partial_products/pallas_call | solution.py:253
  95.0 1.7 collective-permute-start.25
  99.7 1.5 collective-permute-done.23.refs_1_.late.got
  101.3 1.7 collective-permute-start.27
  103.8 3.7 %collective-permute-done.25.refs_1_.late.got = bf16[128,1152]{1,0:T(8,128)(2,1)S(1)} collective-permute-done((bf16[128,1152]{1,0:T(8,128)(2,1)S(1)}, bf16[128,1152]{1,0:T(8,128)(2,1)S(1)}, u32[]{:S(2)}, u32[]{:S(2)}) %collective-permute-start.25) | collective-permute-done | bytes 294944 | tf_op jit(solution)/shard_map/ppermute | solution.py:69
  107.6 1.7 collective-permute-start.29
  110.1 5.1 %collective-permute-done.27.refs_1_.late.got = bf16[128,1408]{1,0:T(8,128)(2,1)S(1)} collective-permute-done((bf16[128,1408]{1,0:T(8,128)(2,1)S(1)}, bf16[128,1408]{1,0:T(8,128)(2,1)S(1)}, u32[]{:S(2)}, u32[]{:S(2)}) %collective-permute-start.27) | collective-permute-done | bytes 360480 | tf_op jit(solution)/shard_map/ppermute | solution.py:69
  115.4 2.1 %collective-permute-start.31 = (bf16[128,1152]{1,0:T(8,128)(2,1)S(1)}, bf16[128,1152]{1,0:T(8,128)(2,1)S(1)}, u32[]{:S(2)}, u32[]{:S(2)}) collective-permute-start(bf16[128,1152]{1,0:T(8,128)(2,1)S(1)} %get-tuple-element.130.rest_0_.sent), channel_id=1, source_target_pairs={{0,4},{4,0},{8,12},{12,8},{1,5},{5,1},{9,13},{13,9},{2,6},{6,2},{1... | collective-permute-start | bytes 884744 | tf_op jit(solution)/shard_map/ppermute | solution.py:69
  118.3 3.2 %collective-permute-done.29.refs_1_.late.got = bf16[128,1152]{1,0:T(8,128)(2,1)S(1)} collective-permute-done((bf16[128,1152]{1,0:T(8,128)(2,1)S(1)}, bf16[128,1152]{1,0:T(8,128)(2,1)S(1)}, u32[]{:S(2)}, u32[]{:S(2)}) %collective-permute-start.29) | collective-permute-done | bytes 294944 | tf_op jit(solution)/shard_map/ppermute | solution.py:69
  121.7 1.6 collective-permute-start.33
  124.1 3.8 %collective-permute-done.31.refs_1_.late.got = bf16[128,1152]{1,0:T(8,128)(2,1)S(1)} collective-permute-done((bf16[128,1152]{1,0:T(8,128)(2,1)S(1)}, bf16[128,1152]{1,0:T(8,128)(2,1)S(1)}, u32[]{:S(2)}, u32[]{:S(2)}) %collective-permute-start.31) | collective-permute-done | bytes 294944 | tf_op jit(solution)/shard_map/ppermute | solution.py:69
  128.0 1.7 collective-permute-start.35
  130.5 3.7 %collective-permute-done.33.refs_1_.late.got = bf16[128,1152]{1,0:T(8,128)(2,1)S(1)} collective-permute-done((bf16[128,1152]{1,0:T(8,128)(2,1)S(1)}, bf16[128,1152]{1,0:T(8,128)(2,1)S(1)}, u32[]{:S(2)}, u32[]{:S(2)}) %collective-permute-start.33) | collective-permute-done | bytes 294944 | tf_op jit(solution)/shard_map/ppermute | solution.py:69
  134.3 1.6 collective-permute-start.37
  136.7 5.2 %collective-permute-done.35.refs_1_.late.got = bf16[128,1408]{1,0:T(8,128)(2,1)S(1)} collective-permute-done((bf16[128,1408]{1,0:T(8,128)(2,1)S(1)}, bf16[128,1408]{1,0:T(8,128)(2,1)S(1)}, u32[]{:S(2)}, u32[]{:S(2)}) %collective-permute-start.35) | collective-permute-done | bytes 360480 | tf_op jit(solution)/shard_map/ppermute | solution.py:69
  142.1 1.6 collective-permute-start.39
  147.1 2.5 %collective-permute-start.43 = (bf16[128,384]{1,0:T(8,128)(2,1)S(1)}, bf16[128,384]{1,0:T(8,128)(2,1)S(1)}, u32[]{:S(2)}, u32[]{:S(2)}) collective-permute-start(bf16[128,384]{1,0:T(8,128)(2,1)S(1)} %get-tuple-element.144.rest_0_), channel_id=1, source_target_pairs={{0,4},{4,0},{8,12},{12,8},{1,5},{5,1},{9,13},{13,9},{2,6},{6,2},{1... | collective-permute-start | bytes 294920 | tf_op jit(solution)/shard_map/ppermute | solution.py:69
  150.4 2.0 %collective-permute-start.45 = (bf16[128,384]{1,0:T(8,128)(2,1)S(1)}, bf16[128,384]{1,0:T(8,128)(2,1)S(1)}, u32[]{:S(2)}, u32[]{:S(2)}) collective-permute-start(bf16[128,384]{1,0:T(8,128)(2,1)S(1)} %hop.42.rest_0_), channel_id=1, source_target_pairs={{0,4},{4,0},{8,12},{12,8},{1,5},{5,1},{9,13},{13,9},{2,6},{6,2},{1... | collective-permute-start | bytes 294920 | tf_op jit(solution)/shard_map/ppermute | solution.py:69
  153.2 1.6 collective-permute-start.46
  155.8 2.4 %collective-permute-done.46.late = bf16[128,512]{1,0:T(8,128)(2,1)S(1)} collective-permute-done((bf16[128,512]{1,0:T(8,128)(2,1)S(1)}, bf16[128,512]{1,0:T(8,128)(2,1)S(1)}, u32[]{:S(2)}, u32[]{:S(2)}) %collective-permute-start.46) | collective-permute-done | bytes 131104 | tf_op jit(solution)/shard_map/ppermute | solution.py:69
  159.9 1.9 %collective-permute-done.47 = bf16[128,2048]{1,0:T(8,128)(2,1)S(1)} collective-permute-done((bf16[128,2048]{1,0:T(8,128)(2,1)S(1)}, bf16[128,2048]{1,0:T(8,128)(2,1)S(1)}, u32[]{:S(2)}, u32[]{:S(2)}) %collective-permute-start.47) | collective-permute-done | bytes 524320 | tf_op jit(solution)/shard_map/ppermute | solution.py:77
  162.0 1.6 collective-permute-start.48
  164.2 6.2 %collective-permute-done.48 = bf16[64,2048]{1,0:T(8,128)(2,1)S(1)} collective-permute-done((bf16[64,2048]{1,0:T(8,128)(2,1)S(1)}, bf16[64,2048]{1,0:T(8,128)(2,1)S(1)}, u32[]{:S(2)}, u32[]{:S(2)}) %collective-permute-start.48) | collective-permute-done | bytes 262176 | tf_op jit(solution)/shard_map/ppermute | solution.py:77
  (138 shorter events, 23.5 us)
Async XLA Ops:
  13.6 9.7 %collective-permute-start = (bf16[64,2176]{1,0:T(8,128)(2,1)S(1)}, bf16[64,2176]{1,0:T(8,128)(2,1)S(1)}, u32[]{:S(2)}, u32[]{:S(2)}) collective-permute-start(bf16[64,2176]{1,0:T(8,128)(2,1)S(1)} %get-tuple-element.77), channel_id=1, source_target_pairs={{0,2},{2,0},{1,3},{3,1},{4,6},{6,4},{5,7},{7,5},{8,10},{10,8},{9,1... | collective-permute-start | bytes 835592 | tf_op jit(solution)/shard_map/ppermute | solution.py:77
  16.6 6.7 %collective-permute-start.1 = (bf16[64,2176]{1,0:T(8,128)(2,1)S(1)}, bf16[64,2176]{1,0:T(8,128)(2,1)S(1)}, u32[]{:S(2)}, u32[]{:S(2)}) collective-permute-start(bf16[64,2176]{1,0:T(8,128)(2,1)S(1)} %get-tuple-element.77), channel_id=1, source_target_pairs={{0,1},{1,0},{2,3},{3,2},{4,5},{5,4},{6,7},{7,6},{8,9},{9,8},{10,11... | collective-permute-start | bytes 835592 | tf_op jit(solution)/shard_map/ppermute | solution.py:77
  28.3 9.9 %collective-permute-start.3 = (bf16[128,896]{1,0:T(8,128)(2,1)S(1)}, bf16[128,896]{1,0:T(8,128)(2,1)S(1)}, u32[]{:S(2)}, u32[]{:S(2)}) collective-permute-start(bf16[128,896]{1,0:T(8,128)(2,1)S(1)} %get-tuple-element.78.rest_2_.refs_3_), channel_id=1, source_target_pairs={{0,4},{4,0},{8,12},{12,8},{1,5},{5,1},{9,13},{13,9},{2,6},{6,2},{1... | collective-permute-start | bytes 688136 | tf_op jit(solution)/shard_map/ppermute | solution.py:69
  33.4 12.9 %collective-permute-start.6 = (bf16[128,768]{1,0:T(8,128)(2,1)S(1)}, bf16[128,768]{1,0:T(8,128)(2,1)S(1)}, u32[]{:S(2)}, u32[]{:S(2)}) collective-permute-start(bf16[128,768]{1,0:T(8,128)(2,1)S(1)} %get-tuple-element.79.rest_0_.refs_3_), channel_id=1, source_target_pairs={{0,4},{4,0},{8,12},{12,8},{1,5},{5,1},{9,13},{13,9},{2,6},{6,2},{1... | collective-permute-start | bytes 589832 | tf_op jit(solution)/shard_map/ppermute | solution.py:69
  38.2 9.8 %collective-permute-start.5 = (bf16[128,896]{1,0:T(8,128)(2,1)S(1)}, bf16[128,896]{1,0:T(8,128)(2,1)S(1)}, u32[]{:S(2)}, u32[]{:S(2)}) collective-permute-start(bf16[128,896]{1,0:T(8,128)(2,1)S(1)} %get-tuple-element.82), channel_id=1, source_target_pairs={{0,1},{1,0},{4,8},{8,4},{5,9},{9,5},{12,13},{13,12},{2,3},{3,2},{6... | collective-permute-start | bytes 688136 | tf_op jit(solution)/shard_map/ppermute | solution.py:73
  38.3 9.7 %collective-permute-start.4 = (bf16[128,768]{1,0:T(8,128)(2,1)S(1)}, bf16[128,768]{1,0:T(8,128)(2,1)S(1)}, u32[]{:S(2)}, u32[]{:S(2)}) collective-permute-start(bf16[128,768]{1,0:T(8,128)(2,1)S(1)} %get-tuple-element.81.rest_0_), channel_id=1, source_target_pairs={{0,4},{4,0},{8,12},{12,8},{1,5},{5,1},{9,13},{13,9},{2,6},{6,2},{1... | collective-permute-start | bytes 589832 | tf_op jit(solution)/shard_map/ppermute | solution.py:69
  46.3 6.9 %collective-permute-start.10 = (bf16[128,768]{1,0:T(8,128)(2,1)S(1)}, bf16[128,768]{1,0:T(8,128)(2,1)S(1)}, u32[]{:S(2)}, u32[]{:S(2)}) collective-permute-start(bf16[128,768]{1,0:T(8,128)(2,1)S(1)} %get-tuple-element.91), channel_id=1, source_target_pairs={{0,1},{1,0},{4,8},{8,4},{5,9},{9,5},{12,13},{13,12},{2,3},{3,2},{6... | collective-permute-start | bytes 589832 | tf_op jit(solution)/shard_map/ppermute | solution.py:73
  46.4 7.8 %collective-permute-start.9 = (bf16[128,768]{1,0:T(8,128)(2,1)S(1)}, bf16[128,768]{1,0:T(8,128)(2,1)S(1)}, u32[]{:S(2)}, u32[]{:S(2)}) collective-permute-start(bf16[128,768]{1,0:T(8,128)(2,1)S(1)} %get-tuple-element.86.refs_6_), channel_id=1, source_target_pairs={{0,4},{4,0},{8,12},{12,8},{1,5},{5,1},{9,13},{13,9},{2,6},{6,2},{1... | collective-permute-start | bytes 589832 | tf_op jit(solution)/shard_map/ppermute | solution.py:69
  48.0 11.1 %collective-permute-start.7 = (bf16[128,896]{1,0:T(8,128)(2,1)S(1)}, bf16[128,896]{1,0:T(8,128)(2,1)S(1)}, u32[]{:S(2)}, u32[]{:S(2)}) collective-permute-start(bf16[128,896]{1,0:T(8,128)(2,1)S(1)} %get-tuple-element.87.rest_0_), channel_id=1, source_target_pairs={{0,4},{4,0},{8,12},{12,8},{1,5},{5,1},{9,13},{13,9},{2,6},{6,2},{1... | collective-permute-start | bytes 688136 | tf_op jit(solution)/shard_map/ppermute | solution.py:69
  48.8 7.2 %collective-permute-start.8 = (bf16[128,768]{1,0:T(8,128)(2,1)S(1)}, bf16[128,768]{1,0:T(8,128)(2,1)S(1)}, u32[]{:S(2)}, u32[]{:S(2)}) collective-permute-start(bf16[128,768]{1,0:T(8,128)(2,1)S(1)} %get-tuple-element.88), channel_id=1, source_target_pairs={{0,1},{1,0},{4,8},{8,4},{5,9},{9,5},{12,13},{13,12},{2,3},{3,2},{6... | collective-permute-start | bytes 589832 | tf_op jit(solution)/shard_map/ppermute | solution.py:73
  54.2 11.2 %collective-permute-start.13 = (bf16[128,768]{1,0:T(8,128)(2,1)S(1)}, bf16[128,768]{1,0:T(8,128)(2,1)S(1)}, u32[]{:S(2)}, u32[]{:S(2)}) collective-permute-start(bf16[128,768]{1,0:T(8,128)(2,1)S(1)} %get-tuple-element.94.refs_7_), channel_id=1, source_target_pairs={{0,4},{4,0},{8,12},{12,8},{1,5},{5,1},{9,13},{13,9},{2,6},{6,2},{1... | collective-permute-start | bytes 589832 | tf_op jit(solution)/shard_map/ppermute | solution.py:69
  56.0 9.5 %collective-permute-start.14 = (bf16[128,768]{1,0:T(8,128)(2,1)S(1)}, bf16[128,768]{1,0:T(8,128)(2,1)S(1)}, u32[]{:S(2)}, u32[]{:S(2)}) collective-permute-start(bf16[128,768]{1,0:T(8,128)(2,1)S(1)} %get-tuple-element.100), channel_id=1, source_target_pairs={{0,1},{1,0},{4,8},{8,4},{5,9},{9,5},{12,13},{13,12},{2,3},{3,2},{6... | collective-permute-start | bytes 589832 | tf_op jit(solution)/shard_map/ppermute | solution.py:73
  59.3 10.3 %collective-permute-start.11 = (bf16[128,1152]{1,0:T(8,128)(2,1)S(1)}, bf16[128,1152]{1,0:T(8,128)(2,1)S(1)}, u32[]{:S(2)}, u32[]{:S(2)}) collective-permute-start(bf16[128,1152]{1,0:T(8,128)(2,1)S(1)} %get-tuple-element.95.rest_0_.sent), channel_id=1, source_target_pairs={{0,4},{4,0},{8,12},{12,8},{1,5},{5,1},{9,13},{13,9},{2,6},{6,2},{1... | collective-permute-start | bytes 884744 | tf_op jit(solution)/shard_map/ppermute | solution.py:69
  60.9 5.7 %collective-permute-start.12 = (bf16[128,768]{1,0:T(8,128)(2,1)S(1)}, bf16[128,768]{1,0:T(8,128)(2,1)S(1)}, u32[]{:S(2)}, u32[]{:S(2)}) collective-permute-start(bf16[128,768]{1,0:T(8,128)(2,1)S(1)} %get-tuple-element.96), channel_id=1, source_target_pairs={{0,1},{1,0},{4,8},{8,4},{5,9},{9,5},{12,13},{13,12},{2,3},{3,2},{6... | collective-permute-start | bytes 589832 | tf_op jit(solution)/shard_map/ppermute | solution.py:73
  65.6 10.7 %collective-permute-start.17 = (bf16[128,1152]{1,0:T(8,128)(2,1)S(1)}, bf16[128,1152]{1,0:T(8,128)(2,1)S(1)}, u32[]{:S(2)}, u32[]{:S(2)}) collective-permute-start(bf16[128,1152]{1,0:T(8,128)(2,1)S(1)} %get-tuple-element.103.refs_8_.sent), channel_id=1, source_target_pairs={{0,4},{4,0},{8,12},{12,8},{1,5},{5,1},{9,13},{13,9},{2,6},{6,2},{1... | collective-permute-start | bytes 884744 | tf_op jit(solution)/shard_map/ppermute | solution.py:69
  66.6 9.7 %collective-permute-start.18 = (bf16[128,768]{1,0:T(8,128)(2,1)S(1)}, bf16[128,768]{1,0:T(8,128)(2,1)S(1)}, u32[]{:S(2)}, u32[]{:S(2)}) collective-permute-start(bf16[128,768]{1,0:T(8,128)(2,1)S(1)} %get-tuple-element.108), channel_id=1, source_target_pairs={{0,1},{1,0},{4,8},{8,4},{5,9},{9,5},{12,13},{13,12},{2,3},{3,2},{6... | collective-permute-start | bytes 589832 | tf_op jit(solution)/shard_map/ppermute | solution.py:73
  69.9 7.8 %collective-permute-start.15 = (bf16[128,1152]{1,0:T(8,128)(2,1)S(1)}, bf16[128,1152]{1,0:T(8,128)(2,1)S(1)}, u32[]{:S(2)}, u32[]{:S(2)}) collective-permute-start(bf16[128,1152]{1,0:T(8,128)(2,1)S(1)} %get-tuple-element.104), channel_id=1, source_target_pairs={{0,1},{1,0},{4,8},{8,4},{5,9},{9,5},{12,13},{13,12},{2,3},{3,2},{6... | collective-permute-start | bytes 884744 | tf_op jit(solution)/shard_map/ppermute | solution.py:73
  70.0 12.2 %collective-permute-start.16 = (bf16[128,1152]{1,0:T(8,128)(2,1)S(1)}, bf16[128,1152]{1,0:T(8,128)(2,1)S(1)}, u32[]{:S(2)}, u32[]{:S(2)}) collective-permute-start(bf16[128,1152]{1,0:T(8,128)(2,1)S(1)} %get-tuple-element.105.rest_0_.sent), channel_id=1, source_target_pairs={{0,4},{4,0},{8,12},{12,8},{1,5},{5,1},{9,13},{13,9},{2,6},{6,2},{1... | collective-permute-start | bytes 884744 | tf_op jit(solution)/shard_map/ppermute | solution.py:69
  76.5 12.0 %collective-permute-start.21 = (bf16[128,1152]{1,0:T(8,128)(2,1)S(1)}, bf16[128,1152]{1,0:T(8,128)(2,1)S(1)}, u32[]{:S(2)}, u32[]{:S(2)}) collective-permute-start(bf16[128,1152]{1,0:T(8,128)(2,1)S(1)} %get-tuple-element.111.refs_8_.sent), channel_id=1, source_target_pairs={{0,4},{4,0},{8,12},{12,8},{1,5},{5,1},{9,13},{13,9},{2,6},{6,2},{1... | collective-permute-start | bytes 884744 | tf_op jit(solution)/shard_map/ppermute | solution.py:69
  77.7 10.8 %collective-permute-start.22 = (bf16[128,1152]{1,0:T(8,128)(2,1)S(1)}, bf16[128,1152]{1,0:T(8,128)(2,1)S(1)}, u32[]{:S(2)}, u32[]{:S(2)}) collective-permute-start(bf16[128,1152]{1,0:T(8,128)(2,1)S(1)} %get-tuple-element.116), channel_id=1, source_target_pairs={{0,1},{1,0},{4,8},{8,4},{5,9},{9,5},{12,13},{13,12},{2,3},{3,2},{6... | collective-permute-start | bytes 884744 | tf_op jit(solution)/shard_map/ppermute | solution.py:73
  82.4 12.5 %collective-permute-start.19 = (bf16[128,1152]{1,0:T(8,128)(2,1)S(1)}, bf16[128,1152]{1,0:T(8,128)(2,1)S(1)}, u32[]{:S(2)}, u32[]{:S(2)}) collective-permute-start(bf16[128,1152]{1,0:T(8,128)(2,1)S(1)} %get-tuple-element.112.rest_2_.sent), channel_id=1, source_target_pairs={{0,4},{4,0},{8,12},{12,8},{1,5},{5,1},{9,13},{13,9},{2,6},{6,2},{1... | collective-permute-start | bytes 884744 | tf_op jit(solution)/shard_map/ppermute | solution.py:69
  84.0 10.8 %collective-permute-start.20 = (bf16[128,1152]{1,0:T(8,128)(2,1)S(1)}, bf16[128,1152]{1,0:T(8,128)(2,1)S(1)}, u32[]{:S(2)}, u32[]{:S(2)}) collective-permute-start(bf16[128,1152]{1,0:T(8,128)(2,1)S(1)} %get-tuple-element.113), channel_id=1, source_target_pairs={{0,1},{1,0},{4,8},{8,4},{5,9},{9,5},{12,13},{13,12},{2,3},{3,2},{6... | collective-permute-start | bytes 884744 | tf_op jit(solution)/shard_map/ppermute | solution.py:73
  88.7 12.5 %collective-permute-start.23 = (bf16[128,1152]{1,0:T(8,128)(2,1)S(1)}, bf16[128,1152]{1,0:T(8,128)(2,1)S(1)}, u32[]{:S(2)}, u32[]{:S(2)}) collective-permute-start(bf16[128,1152]{1,0:T(8,128)(2,1)S(1)} %get-tuple-element.119.rest_4_.sent), channel_id=1, source_target_pairs={{0,4},{4,0},{8,12},{12,8},{1,5},{5,1},{9,13},{13,9},{2,6},{6,2},{1... | collective-permute-start | bytes 884744 | tf_op jit(solution)/shard_map/ppermute | solution.py:69
  90.4 10.8 %collective-permute-start.24 = (bf16[128,1152]{1,0:T(8,128)(2,1)S(1)}, bf16[128,1152]{1,0:T(8,128)(2,1)S(1)}, u32[]{:S(2)}, u32[]{:S(2)}) collective-permute-start(bf16[128,1152]{1,0:T(8,128)(2,1)S(1)} %get-tuple-element.122), channel_id=1, source_target_pairs={{0,1},{1,0},{4,8},{8,4},{5,9},{9,5},{12,13},{13,12},{2,3},{3,2},{6... | collective-permute-start | bytes 884744 | tf_op jit(solution)/shard_map/ppermute | solution.py:73
  95.0 12.5 %collective-permute-start.25 = (bf16[128,1152]{1,0:T(8,128)(2,1)S(1)}, bf16[128,1152]{1,0:T(8,128)(2,1)S(1)}, u32[]{:S(2)}, u32[]{:S(2)}) collective-permute-start(bf16[128,1152]{1,0:T(8,128)(2,1)S(1)} %get-tuple-element.121.rest_0_.sent), channel_id=1, source_target_pairs={{0,4},{4,0},{8,12},{12,8},{1,5},{5,1},{9,13},{13,9},{2,6},{6,2},{1... | collective-permute-start | bytes 884744 | tf_op jit(solution)/shard_map/ppermute | solution.py:69
  96.7 10.8 %collective-permute-start.26 = (bf16[128,1152]{1,0:T(8,128)(2,1)S(1)}, bf16[128,1152]{1,0:T(8,128)(2,1)S(1)}, u32[]{:S(2)}, u32[]{:S(2)}) collective-permute-start(bf16[128,1152]{1,0:T(8,128)(2,1)S(1)} %get-tuple-element.125), channel_id=1, source_target_pairs={{0,1},{1,0},{4,8},{8,4},{5,9},{9,5},{12,13},{13,12},{2,3},{3,2},{6... | collective-permute-start | bytes 884744 | tf_op jit(solution)/shard_map/ppermute | solution.py:73
  101.3 13.9 %collective-permute-start.27 = (bf16[128,1408]{1,0:T(8,128)(2,1)S(1)}, bf16[128,1408]{1,0:T(8,128)(2,1)S(1)}, u32[]{:S(2)}, u32[]{:S(2)}) collective-permute-start(bf16[128,1408]{1,0:T(8,128)(2,1)S(1)} %get-tuple-element.124.rest_0_.sent), channel_id=1, source_target_pairs={{0,4},{4,0},{8,12},{12,8},{1,5},{5,1},{9,13},{13,9},{2,6},{6,2},{1... | collective-permute-start | bytes 1081352 | tf_op jit(solution)/shard_map/ppermute | solution.py:69
  103.0 7.1 %collective-permute-start.28 = (bf16[128,1152]{1,0:T(8,128)(2,1)S(1)}, bf16[128,1152]{1,0:T(8,128)(2,1)S(1)}, u32[]{:S(2)}, u32[]{:S(2)}) collective-permute-start(bf16[128,1152]{1,0:T(8,128)(2,1)S(1)} %get-tuple-element.128), channel_id=1, source_target_pairs={{0,1},{1,0},{4,8},{8,4},{5,9},{9,5},{12,13},{13,12},{2,3},{3,2},{6... | collective-permute-start | bytes 884744 | tf_op jit(solution)/shard_map/ppermute | solution.py:73
  107.6 13.9 %collective-permute-start.29 = (bf16[128,1152]{1,0:T(8,128)(2,1)S(1)}, bf16[128,1152]{1,0:T(8,128)(2,1)S(1)}, u32[]{:S(2)}, u32[]{:S(2)}) collective-permute-start(bf16[128,1152]{1,0:T(8,128)(2,1)S(1)} %get-tuple-element.127.rest_0_.sent), channel_id=1, source_target_pairs={{0,4},{4,0},{8,12},{12,8},{1,5},{5,1},{9,13},{13,9},{2,6},{6,2},{1... | collective-permute-start | bytes 884744 | tf_op jit(solution)/shard_map/ppermute | solution.py:69
  109.3 12.2 %collective-permute-start.30 = (bf16[128,1152]{1,0:T(8,128)(2,1)S(1)}, bf16[128,1152]{1,0:T(8,128)(2,1)S(1)}, u32[]{:S(2)}, u32[]{:S(2)}) collective-permute-start(bf16[128,1152]{1,0:T(8,128)(2,1)S(1)} %get-tuple-element.131), channel_id=1, source_target_pairs={{0,1},{1,0},{4,8},{8,4},{5,9},{9,5},{12,13},{13,12},{2,3},{3,2},{6... | collective-permute-start | bytes 884744 | tf_op jit(solution)/shard_map/ppermute | solution.py:73
  115.4 12.5 %collective-permute-start.32 = (bf16[128,1408]{1,0:T(8,128)(2,1)S(1)}, bf16[128,1408]{1,0:T(8,128)(2,1)S(1)}, u32[]{:S(2)}, u32[]{:S(2)}) collective-permute-start(bf16[128,1408]{1,0:T(8,128)(2,1)S(1)} %get-tuple-element.134), channel_id=1, source_target_pairs={{0,1},{1,0},{4,8},{8,4},{5,9},{9,5},{12,13},{13,12},{2,3},{3,2},{6... | collective-permute-start | bytes 1081352 | tf_op jit(solution)/shard_map/ppermute | solution.py:73
  115.4 12.4 %collective-permute-start.31 = (bf16[128,1152]{1,0:T(8,128)(2,1)S(1)}, bf16[128,1152]{1,0:T(8,128)(2,1)S(1)}, u32[]{:S(2)}, u32[]{:S(2)}) collective-permute-start(bf16[128,1152]{1,0:T(8,128)(2,1)S(1)} %get-tuple-element.130.rest_0_.sent), channel_id=1, source_target_pairs={{0,4},{4,0},{8,12},{12,8},{1,5},{5,1},{9,13},{13,9},{2,6},{6,2},{1... | collective-permute-start | bytes 884744 | tf_op jit(solution)/shard_map/ppermute | solution.py:69
  121.7 12.5 %collective-permute-start.33 = (bf16[128,1152]{1,0:T(8,128)(2,1)S(1)}, bf16[128,1152]{1,0:T(8,128)(2,1)S(1)}, u32[]{:S(2)}, u32[]{:S(2)}) collective-permute-start(bf16[128,1152]{1,0:T(8,128)(2,1)S(1)} %get-tuple-element.133.rest_0_.sent), channel_id=1, source_target_pairs={{0,4},{4,0},{8,12},{12,8},{1,5},{5,1},{9,13},{13,9},{2,6},{6,2},{1... | collective-permute-start | bytes 884744 | tf_op jit(solution)/shard_map/ppermute | solution.py:69
  123.3 7.2 %collective-permute-start.34 = (bf16[128,384]{1,0:T(8,128)(2,1)S(1)}, bf16[128,384]{1,0:T(8,128)(2,1)S(1)}, u32[]{:S(2)}, u32[]{:S(2)}) collective-permute-start(bf16[128,384]{1,0:T(8,128)(2,1)S(1)} %get-tuple-element.137), channel_id=1, source_target_pairs={{0,1},{1,0},{4,8},{8,4},{5,9},{9,5},{12,13},{13,12},{2,3},{3,2},{6... | collective-permute-start | bytes 294920 | tf_op jit(solution)/shard_map/ppermute | solution.py:73
  128.0 13.9 %collective-permute-start.35 = (bf16[128,1408]{1,0:T(8,128)(2,1)S(1)}, bf16[128,1408]{1,0:T(8,128)(2,1)S(1)}, u32[]{:S(2)}, u32[]{:S(2)}) collective-permute-start(bf16[128,1408]{1,0:T(8,128)(2,1)S(1)} %get-tuple-element.136.rest_0_.sent), channel_id=1, source_target_pairs={{0,4},{4,0},{8,12},{12,8},{1,5},{5,1},{9,13},{13,9},{2,6},{6,2},{1... | collective-permute-start | bytes 1081352 | tf_op jit(solution)/shard_map/ppermute | solution.py:69
  130.4 6.3 %collective-permute-start.36 = (bf16[128,384]{1,0:T(8,128)(2,1)S(1)}, bf16[128,384]{1,0:T(8,128)(2,1)S(1)}, u32[]{:S(2)}, u32[]{:S(2)}) collective-permute-start(bf16[128,384]{1,0:T(8,128)(2,1)S(1)} %get-tuple-element.139), channel_id=1, source_target_pairs={{0,1},{1,0},{4,8},{8,4},{5,9},{9,5},{12,13},{13,12},{2,3},{3,2},{6... | collective-permute-start | bytes 294920 | tf_op jit(solution)/shard_map/ppermute | solution.py:73
  134.3 10.3 %collective-permute-start.37 = (bf16[128,384]{1,0:T(8,128)(2,1)S(1)}, bf16[128,384]{1,0:T(8,128)(2,1)S(1)}, u32[]{:S(2)}, u32[]{:S(2)}) collective-permute-start(bf16[128,384]{1,0:T(8,128)(2,1)S(1)} %get-tuple-element.138.rest_0_.sent), channel_id=1, source_target_pairs={{0,4},{4,0},{8,12},{12,8},{1,5},{5,1},{9,13},{13,9},{2,6},{6,2},{1... | collective-permute-start | bytes 294920 | tf_op jit(solution)/shard_map/ppermute | solution.py:69
  135.9 8.7 %collective-permute-start.38 = (bf16[128,384]{1,0:T(8,128)(2,1)S(1)}, bf16[128,384]{1,0:T(8,128)(2,1)S(1)}, u32[]{:S(2)}, u32[]{:S(2)}) collective-permute-start(bf16[128,384]{1,0:T(8,128)(2,1)S(1)} %get-tuple-element.141), channel_id=1, source_target_pairs={{0,1},{1,0},{4,8},{8,4},{5,9},{9,5},{12,13},{13,12},{2,3},{3,2},{6... | collective-permute-start | bytes 294920 | tf_op jit(solution)/shard_map/ppermute | solution.py:73
  142.1 5.0 %collective-permute-start.39 = (bf16[128,512]{1,0:T(8,128)(2,1)S(1)}, bf16[128,512]{1,0:T(8,128)(2,1)S(1)}, u32[]{:S(2)}, u32[]{:S(2)}) collective-permute-start(bf16[128,512]{1,0:T(8,128)(2,1)S(1)} %get-tuple-element.140.rest_0_.sent), channel_id=1, source_target_pairs={{0,4},{4,0},{8,12},{12,8},{1,5},{5,1},{9,13},{13,9},{2,6},{6,2},{1... | collective-permute-start | bytes 393224 | tf_op jit(solution)/shard_map/ppermute | solution.py:69
  143.6 2.8 %collective-permute-start.40 = (bf16[128,384]{1,0:T(8,128)(2,1)S(1)}, bf16[128,384]{1,0:T(8,128)(2,1)S(1)}, u32[]{:S(2)}, u32[]{:S(2)}) collective-permute-start(bf16[128,384]{1,0:T(8,128)(2,1)S(1)} %get-tuple-element.143), channel_id=1, source_target_pairs={{0,1},{1,0},{4,8},{8,4},{5,9},{9,5},{12,13},{13,12},{2,3},{3,2},{6... | collective-permute-start | bytes 294920 | tf_op jit(solution)/shard_map/ppermute | solution.py:73
  144.6 5.7 %collective-permute-start.41 = (bf16[128,384]{1,0:T(8,128)(2,1)S(1)}, bf16[128,384]{1,0:T(8,128)(2,1)S(1)}, u32[]{:S(2)}, u32[]{:S(2)}) collective-permute-start(bf16[128,384]{1,0:T(8,128)(2,1)S(1)} %get-tuple-element.142.rest_0_), channel_id=1, source_target_pairs={{0,4},{4,0},{8,12},{12,8},{1,5},{5,1},{9,13},{13,9},{2,6},{6,2},{1... | collective-permute-start | bytes 294920 | tf_op jit(solution)/shard_map/ppermute | solution.py:69
  145.7 4.7 %collective-permute-start.42 = (bf16[128,384]{1,0:T(8,128)(2,1)S(1)}, bf16[128,384]{1,0:T(8,128)(2,1)S(1)}, u32[]{:S(2)}, u32[]{:S(2)}) collective-permute-start(bf16[128,384]{1,0:T(8,128)(2,1)S(1)} %get-tuple-element.145), channel_id=1, source_target_pairs={{0,1},{1,0},{4,8},{8,4},{5,9},{9,5},{12,13},{13,12},{2,3},{3,2},{6... | collective-permute-start | bytes 294920 | tf_op jit(solution)/shard_map/ppermute | solution.py:73
  147.1 6.1 %collective-permute-start.44 = (bf16[128,512]{1,0:T(8,128)(2,1)S(1)}, bf16[128,512]{1,0:T(8,128)(2,1)S(1)}, u32[]{:S(2)}, u32[]{:S(2)}) collective-permute-start(bf16[128,512]{1,0:T(8,128)(2,1)S(1)} %get-tuple-element.146), channel_id=1, source_target_pairs={{0,1},{1,0},{4,8},{8,4},{5,9},{9,5},{12,13},{13,12},{2,3},{3,2},{6... | collective-permute-start | bytes 393224 | tf_op jit(solution)/shard_map/ppermute | solution.py:73
  147.1 6.1 %collective-permute-start.43 = (bf16[128,384]{1,0:T(8,128)(2,1)S(1)}, bf16[128,384]{1,0:T(8,128)(2,1)S(1)}, u32[]{:S(2)}, u32[]{:S(2)}) collective-permute-start(bf16[128,384]{1,0:T(8,128)(2,1)S(1)} %get-tuple-element.144.rest_0_), channel_id=1, source_target_pairs={{0,4},{4,0},{8,12},{12,8},{1,5},{5,1},{9,13},{13,9},{2,6},{6,2},{1... | collective-permute-start | bytes 294920 | tf_op jit(solution)/shard_map/ppermute | solution.py:69
  150.4 5.4 %collective-permute-start.45 = (bf16[128,384]{1,0:T(8,128)(2,1)S(1)}, bf16[128,384]{1,0:T(8,128)(2,1)S(1)}, u32[]{:S(2)}, u32[]{:S(2)}) collective-permute-start(bf16[128,384]{1,0:T(8,128)(2,1)S(1)} %hop.42.rest_0_), channel_id=1, source_target_pairs={{0,4},{4,0},{8,12},{12,8},{1,5},{5,1},{9,13},{13,9},{2,6},{6,2},{1... | collective-permute-start | bytes 294920 | tf_op jit(solution)/shard_map/ppermute | solution.py:69
  153.2 5.0 %collective-permute-start.46 = (bf16[128,512]{1,0:T(8,128)(2,1)S(1)}, bf16[128,512]{1,0:T(8,128)(2,1)S(1)}, u32[]{:S(2)}, u32[]{:S(2)}) collective-permute-start(bf16[128,512]{1,0:T(8,128)(2,1)S(1)} %hop.43.rest_0_), channel_id=1, source_target_pairs={{0,4},{4,0},{8,12},{12,8},{1,5},{5,1},{9,13},{13,9},{2,6},{6,2},{1... | collective-permute-start | bytes 393224 | tf_op jit(solution)/shard_map/ppermute | solution.py:69
  159.8 2.0 %collective-permute-start.47 = (bf16[128,2048]{1,0:T(8,128)(2,1)S(1)}, bf16[128,2048]{1,0:T(8,128)(2,1)S(1)}, u32[]{:S(2)}, u32[]{:S(2)}) collective-permute-start(bf16[128,2048]{1,0:T(8,128)(2,1)S(1)} %broadcast_select_fusion.2), channel_id=1, source_target_pairs={{0,1},{1,0},{2,3},{3,2},{4,5},{5,4},{6,7},{7,6},{8,9},{9,8},{10,11... | collective-permute-start | bytes 1572872 | tf_op jit(solution)/shard_map/ppermute | solution.py:77
  162.0 8.4 %collective-permute-start.48 = (bf16[64,2048]{1,0:T(8,128)(2,1)S(1)}, bf16[64,2048]{1,0:T(8,128)(2,1)S(1)}, u32[]{:S(2)}, u32[]{:S(2)}) collective-permute-start(bf16[64,2048]{1,0:T(8,128)(2,1)S(1)} %slice.124), channel_id=1, source_target_pairs={{0,2},{2,0},{1,3},{3,1},{4,6},{6,4},{5,7},{7,5},{8,10},{10,8},{9,1... | collective-permute-start | bytes 786440 | tf_op jit(solution)/shard_map/ppermute | solution.py:77
  (9 other events, 45.8 us)
